TPU v7x, 32 devices: a whole 2x2x4 slice. The times are simulated.
32 devices in a mesh: row: 4 (over y, x), col: 8 (over z, core).
Axes of the slice: x: 2, y: 2, z: 4, core: 2. Of those that a mesh axis runs over, the one named last changes fastest.
Arguments:
- residual_in: float32 [8, 4, 32, 256], P(None, 'row', None, 'col'), may hold values from -6 to 6
- diag_inverse: bfloat16 [8, 4, 256, 256], P(None, 'row'), may hold values from -0.04 to 1.04, as said below
- lower_blocks: bfloat16 [7, 4, 3, 256, 256], P(None, 'row'), may hold values from -0.15625 to 0.15625
- column_lists: int32 [7, 4, 3], replicated, may hold values from 0 to 27, as said below
Outputs:
- precond: float32 [8, 4, 32, 256], P(None, 'row', None, 'col')
Inputs may be any that keep to these rules, and one draw needn't show every extreme that they name: `column_lists`: for a block row of level s, every entry names a block row of a level below s; its first entry names a block row of level s - 1, and every block row of level s - 1 is named so by exactly one block row of level s. `diag_inverse`: each block is the identity plus small entries.
All inputs are finite; a program needn't handle non-finite values.
Results may differ from a plain program's by a relative error of at most 0.0003.
Values sent between devices are 32-bit elements; how exact they have to be, the bound alone decides.
No kernel may reach another device: no remote copies, remote signals or barrier semaphores. Data moves between devices by JAX's collectives and lax.ppermute only.
A program may use at most 64 MiB of HBM per device.

v0:
```python
import jax
import jax.numpy as jnp
from jax import lax
from jax.sharding import PartitionSpec as P


def pick_index(array, index, axis_number):
    return lax.dynamic_index_in_dim(array, index, axis_number, keepdims=False)


def shards(residual_in, diag_inverse, lower_blocks, column_lists):
    highest = lax.Precision.HIGHEST
    sweep_input = lax.all_to_all(residual_in, "col", split_axis=2, concat_axis=3, tiled=True)[:, 0]
    slot_count, probe_count, block_size = sweep_input.shape
    owners = lax.axis_size("row")
    self_row = lax.axis_index("row")
    inverses = diag_inverse[:, 0]
    lowers = lower_blocks[:, 0]
    slot_numbers = jnp.arange(slot_count, dtype=jnp.int32)

    def solve_forward(current, source):
        inverse_block = pick_index(inverses, current, 0).astype(jnp.float32)
        return jnp.einsum("pc,dc->pd", source, inverse_block, precision=highest)

    def solve_backward(current, source):
        inverse_block = pick_index(inverses, current, 0).astype(jnp.float32)
        return jnp.einsum("pc,cd->pd", source, inverse_block, precision=highest)

    def contributions_of(current, solved):
        factor_blocks = pick_index(lowers, current - 1, 0).astype(jnp.float32)
        return jnp.einsum("pd,kdc->kpc", solved, factor_blocks, precision=highest)

    finished = jnp.zeros((slot_count, owners, probe_count, block_size), jnp.float32)
    forward = jnp.zeros((slot_count, probe_count, block_size), jnp.float32)
    forward = forward.at[0].set(solve_forward(0, sweep_input[0]))

    def forward_step(current, loop_state):
        finished, forward = loop_state
        previous = lax.dynamic_index_in_dim(forward, current - 1, 0, keepdims=True)
        arrived = lax.all_gather(previous, "row", axis=0, tiled=True)
        finished = lax.dynamic_update_index_in_dim(finished, arrived, current - 1, 0)
        targets = pick_index(pick_index(column_lists, current - 1, 0), self_row, 0)
        pulled = finished.reshape(slot_count * owners, probe_count, block_size)[targets]
        factor_blocks = pick_index(lowers, current - 1, 0).astype(jnp.float32)
        source = pick_index(sweep_input, current, 0) - jnp.einsum(
            "kpc,kdc->pd", pulled, factor_blocks, precision=highest
        )
        forward = lax.dynamic_update_index_in_dim(
            forward, solve_forward(current, source), current, 0
        )
        return (finished, forward)

    finished, forward = lax.fori_loop(1, slot_count, forward_step, (finished, forward))
    final_level = slot_count - 1
    backward = jnp.zeros((slot_count, probe_count, block_size), jnp.float32)
    backward = backward.at[final_level].set(solve_backward(final_level, forward[final_level]))

    def backward_step(counter, loop_state):
        accumulated, backward = loop_state
        current = final_level - counter
        contributions = contributions_of(current, pick_index(backward, current, 0))
        arrived = lax.all_gather(contributions[None], "row", axis=0, tiled=True)
        targets = pick_index(column_lists, current - 1, 0)
        owner_match = (targets % owners == self_row)[:, :, None]
        slot_match = (targets // owners)[:, :, None] == slot_numbers[None, None, :]
        routing = (owner_match & slot_match).astype(jnp.float32)
        accumulated = accumulated + jnp.einsum("nks,nkpc->spc", routing, arrived, precision=highest)
        source = pick_index(forward, current - 1, 0) - pick_index(accumulated, current - 1, 0)
        backward = lax.dynamic_update_index_in_dim(
            backward, solve_backward(current - 1, source), current - 1, 0
        )
        return (accumulated, backward)

    accumulated = jnp.zeros((slot_count, probe_count, block_size), jnp.float32)
    accumulated, backward = lax.fori_loop(0, final_level, backward_step, (accumulated, backward))
    return lax.all_to_all(backward[:, None], "col", split_axis=3, concat_axis=2, tiled=True)


def solution(mesh):
    placed = (
        P(None, "row", None, "col"),
        P(None, "row", None, None),
        P(None, "row", None, None, None),
        P(),
    )
    return jax.shard_map(
        shards, mesh=mesh, in_specs=placed, out_specs=P(None, "row", None, "col"), check_vma=False
    )
```

profile of v0, /device:TPU:0, one launch (start us, length us, event | category | flops | bytes accessed | tf_op | source)
XLA Modules:
  0.0 180.9 jit_solution(12505656492565178275)
XLA Ops:
  1.7 6.3 %all-to-all-start = ((f32[8,1,1024]{2,1,0:T(1,128)}), f32[8,1,1024]{2,1,0:T(1,128)S(1)}, u32[]{:S(2)}, u32[]{:S(2)}) async-start(f32[8,1,1024]{2,1,0:T(1,128)} %reshape.229), calls=%async_computation | async-start | bytes 65536 | tf_op jit(solution)/shard_map/all_to_all | solution.py:13
  8.8 4.9 %all-to-all-done = f32[8,1,1024]{2,1,0:T(1,128)S(1)} async-done(((f32[8,1,1024]{2,1,0:T(1,128)}), f32[8,1,1024]{2,1,0:T(1,128)S(1)}, u32[]{:S(2)}, u32[]{:S(2)}) %all-to-all-start) | async-done | bytes 32800 | tf_op jit(solution)/shard_map/all_to_all | solution.py:13
  16.6 76.8 %while.44 = (s32[]{:T(128)}, f32[8,4,4,256]{3,2,1,0:T(4,128)S(1)}, f32[8,4,256]{2,1,0:T(4,128)S(1)}, f32[8,4,256]{2,1,0:T(4,128)S(1)}, s32[7,4,3]{2,1,0:T(4,128)...) while((s32[]{:T(128)}, f32[8,4,4,256]{3,2,1,0:T(4,128)S(1)}, ...), condition=%wide.region_1.2_spmd, body=%wide.region_0.1_spmd.sunk | while | flops 12584975 | bytes 644343 | solution.py:53
  16.7 8.2 %all_gather.31 = f32[4,4,256]{2,1,0:T(4,128)S(1)} all-gather(f32[1,4,256]{2,1,0:T(4,128)S(1)} %constant_dynamic-slice_fusion.6), channel_id=1, replica_groups=mesh['row'=4,'col'=8] {'row'}, dimensions={0}, use_global_device_ids=true | all-gather | bytes 20480 | tf_op jit(solution)/shard_map/while/body/eval_jaxpr/all_gather | solution.py:40
  25.4 1.4 fusion.63
  28.1 8.1 %all_gather.31 = f32[4,4,256]{2,1,0:T(4,128)S(1)} all-gather(f32[1,4,256]{2,1,0:T(4,128)S(1)} %constant_dynamic-slice_fusion.6), channel_id=1, replica_groups=mesh['row'=4,'col'=8] {'row'}, dimensions={0}, use_global_device_ids=true | all-gather | bytes 20480 | tf_op jit(solution)/shard_map/while/body/eval_jaxpr/all_gather | solution.py:40
  36.8 1.4 fusion.63
  39.4 7.2 %all_gather.31 = f32[4,4,256]{2,1,0:T(4,128)S(1)} all-gather(f32[1,4,256]{2,1,0:T(4,128)S(1)} %constant_dynamic-slice_fusion.6), channel_id=1, replica_groups=mesh['row'=4,'col'=8] {'row'}, dimensions={0}, use_global_device_ids=true | all-gather | bytes 20480 | tf_op jit(solution)/shard_map/while/body/eval_jaxpr/all_gather | solution.py:40
  47.2 1.4 fusion.63
  49.9 8.1 %all_gather.31 = f32[4,4,256]{2,1,0:T(4,128)S(1)} all-gather(f32[1,4,256]{2,1,0:T(4,128)S(1)} %constant_dynamic-slice_fusion.6), channel_id=1, replica_groups=mesh['row'=4,'col'=8] {'row'}, dimensions={0}, use_global_device_ids=true | all-gather | bytes 20480 | tf_op jit(solution)/shard_map/while/body/eval_jaxpr/all_gather | solution.py:40
  58.6 1.4 fusion.63
  61.2 7.2 %all_gather.31 = f32[4,4,256]{2,1,0:T(4,128)S(1)} all-gather(f32[1,4,256]{2,1,0:T(4,128)S(1)} %constant_dynamic-slice_fusion.6), channel_id=1, replica_groups=mesh['row'=4,'col'=8] {'row'}, dimensions={0}, use_global_device_ids=true | all-gather | bytes 20480 | tf_op jit(solution)/shard_map/while/body/eval_jaxpr/all_gather | solution.py:40
  69.0 1.4 fusion.63
  71.6 8.1 %all_gather.31 = f32[4,4,256]{2,1,0:T(4,128)S(1)} all-gather(f32[1,4,256]{2,1,0:T(4,128)S(1)} %constant_dynamic-slice_fusion.6), channel_id=1, replica_groups=mesh['row'=4,'col'=8] {'row'}, dimensions={0}, use_global_device_ids=true | all-gather | bytes 20480 | tf_op jit(solution)/shard_map/while/body/eval_jaxpr/all_gather | solution.py:40
  83.0 7.2 %all_gather.31 = f32[4,4,256]{2,1,0:T(4,128)S(1)} all-gather(f32[1,4,256]{2,1,0:T(4,128)S(1)} %constant_dynamic-slice_fusion.6), channel_id=1, replica_groups=mesh['row'=4,'col'=8] {'row'}, dimensions={0}, use_global_device_ids=true | all-gather | bytes 20480 | tf_op jit(solution)/shard_map/while/body/eval_jaxpr/all_gather | solution.py:40
  94.5 75.1 %while.45 = (s32[]{:T(128)}, f32[8,4,256]{2,0,1:T(8,128)S(1)}, f32[8,4,256]{2,1,0:T(4,128)S(1)}, s32[7,4,3]{2,1,0:T(4,128)S(1)}, s32[]{:T(128)}, /*index=5*/bf16...) while((s32[]{:T(128)}, f32[8,4,256]{2,0,1:T(8,128)S(1)}, ...), condition=%wide.region_3.4_spmd.clone, body=%wide.region_2.3_spmd.clone.sunk | while | flops 13780497 | bytes 747136 | solution.py:75
  96.1 8.2 %all-gather.3 = f32[12,4,256]{2,1,0:T(4,128)S(1)} all-gather(f32[3,4,256]{2,1,0:T(4,128)S(1)} %convolution_bitcast_fusion.8), channel_id=2, replica_groups=mesh['row'=4,'col'=8] {'row'}, dimensions={0}, use_global_device_ids=true | all-gather | bytes 61440 | tf_op jit(solution)/shard_map/while/body/eval_jaxpr/all_gather | solution.py:62
  107.2 7.3 %all-gather.3 = f32[12,4,256]{2,1,0:T(4,128)S(1)} all-gather(f32[3,4,256]{2,1,0:T(4,128)S(1)} %convolution_bitcast_fusion.8), channel_id=2, replica_groups=mesh['row'=4,'col'=8] {'row'}, dimensions={0}, use_global_device_ids=true | all-gather | bytes 61440 | tf_op jit(solution)/shard_map/while/body/eval_jaxpr/all_gather | solution.py:62
  117.4 8.2 %all-gather.3 = f32[12,4,256]{2,1,0:T(4,128)S(1)} all-gather(f32[3,4,256]{2,1,0:T(4,128)S(1)} %convolution_bitcast_fusion.8), channel_id=2, replica_groups=mesh['row'=4,'col'=8] {'row'}, dimensions={0}, use_global_device_ids=true | all-gather | bytes 61440 | tf_op jit(solution)/shard_map/while/body/eval_jaxpr/all_gather | solution.py:62
  128.5 7.3 %all-gather.3 = f32[12,4,256]{2,1,0:T(4,128)S(1)} all-gather(f32[3,4,256]{2,1,0:T(4,128)S(1)} %convolution_bitcast_fusion.8), channel_id=2, replica_groups=mesh['row'=4,'col'=8] {'row'}, dimensions={0}, use_global_device_ids=true | all-gather | bytes 61440 | tf_op jit(solution)/shard_map/while/body/eval_jaxpr/all_gather | solution.py:62
  138.7 8.2 %all-gather.3 = f32[12,4,256]{2,1,0:T(4,128)S(1)} all-gather(f32[3,4,256]{2,1,0:T(4,128)S(1)} %convolution_bitcast_fusion.8), channel_id=2, replica_groups=mesh['row'=4,'col'=8] {'row'}, dimensions={0}, use_global_device_ids=true | all-gather | bytes 61440 | tf_op jit(solution)/shard_map/while/body/eval_jaxpr/all_gather | solution.py:62
  149.9 7.3 %all-gather.3 = f32[12,4,256]{2,1,0:T(4,128)S(1)} all-gather(f32[3,4,256]{2,1,0:T(4,128)S(1)} %convolution_bitcast_fusion.8), channel_id=2, replica_groups=mesh['row'=4,'col'=8] {'row'}, dimensions={0}, use_global_device_ids=true | all-gather | bytes 61440 | tf_op jit(solution)/shard_map/while/body/eval_jaxpr/all_gather | solution.py:62
  160.1 8.2 %all-gather.3 = f32[12,4,256]{2,1,0:T(4,128)S(1)} all-gather(f32[3,4,256]{2,1,0:T(4,128)S(1)} %convolution_bitcast_fusion.8), channel_id=2, replica_groups=mesh['row'=4,'col'=8] {'row'}, dimensions={0}, use_global_device_ids=true | all-gather | bytes 61440 | tf_op jit(solution)/shard_map/while/body/eval_jaxpr/all_gather | solution.py:62
  170.5 8.1 %all_to_all.33 = f32[8,1,1024]{2,1,0:T(1,128)S(1)} all-to-all(f32[8,1,1024]{2,1,0:T(1,128)S(1)} %reshape.231), channel_id=1, replica_groups=mesh['row'=4,'col'=8] {'col'}, dimensions={0} | all-to-all | bytes 65536 | tf_op jit(solution)/shard_map/all_to_all | solution.py:76
  (129 shorter events, 45.3 us)
Async XLA Ops:
  1.7 12.1 %all-to-all-start = ((f32[8,1,1024]{2,1,0:T(1,128)}), f32[8,1,1024]{2,1,0:T(1,128)S(1)}, u32[]{:S(2)}, u32[]{:S(2)}) async-start(f32[8,1,1024]{2,1,0:T(1,128)} %reshape.229), calls=%async_computation | async-start | bytes 65536 | tf_op jit(solution)/shard_map/all_to_all | solution.py:13
where the time goes:
time: 182 us; the launch traced here: 181 us
  blocking collectives  117 us (64%)
  matrix products  38.3 us (21%)
  local copies, waits for them, and re-layouts  11.5 us (6%)
  starting transfers between devices  6.33 us (3%)
  waiting for transfers between devices  4.95 us (3%)
  other arithmetic  2.43 us (1%)
    all_gather x7, blocking collectives, backward_step(): arrived = lax.all_gather(contributions[None], 'row', axis=0, tiled=True)  54.6 us
    all_gather x7, blocking collectives, forward_step(): arrived = lax.all_gather(previous, 'row', axis=0, tiled=True)  54.2 us
    dot_general x7, matrix products, forward_step(): jnp.einsum('kpc,kdc->pd', pulled, factor_blocks, precision=highest)  9.65 us
    dot_general x8, matrix products, solve_forward(): return jnp.einsum('pc,dc->pd', source, inverse_block, precision=highest)  9.19 us
    dot_general x7, matrix products, contributions_of(): return jnp.einsum('pd,kdc->kpc', solved, factor_blocks, precision=highest)  8.88 us
    dot_general x8, matrix products, solve_backward(): return jnp.einsum('pc,cd->pd', source, inverse_block, precision=highest)  8.46 us
    all_to_all x1, blocking collectives, shards(): lax.all_to_all(backward[:, None], 'col', split_axis=3, concat_axis=2, til...  8.12 us
    all_to_all x1, starting transfers between devices, shards(): lax.all_to_all(residual_in, 'col', split_axis=2, concat_axis=3, tiled=True)  6.33 us
  transfers between devices with their start and end apart: 1, of which 1 were waited for; matrix products, arithmetic and copies ran while one was open for 0% of the time, Pallas kernels for 0%

commit v1 on v0

v1 whole, which is shorter than its diff:
```python
import functools

import jax
import jax.numpy as jnp
from jax import lax
from jax.experimental import pallas as pl
from jax.experimental.pallas import tpu as pltpu
from jax.sharding import PartitionSpec as P

VMEM = pltpu.VMEM
SMEM = pltpu.SMEM


def two_parts(rows):
    high = rows.astype(jnp.bfloat16).astype(jnp.float32)
    return jnp.concatenate([high, rows - high], axis=0).astype(jnp.bfloat16)


def times(rows, block, transposed):
    contract = 1 if transposed else 0
    product = lax.dot_general(
        two_parts(rows), block, (((1,), (contract,)), ((), ())),
        preferred_element_type=jnp.float32,
    )
    count = rows.shape[0]
    return product[:count] + product[count:]


def first_kernel(owners, lists, me, source, inverses, finished, solved):
    answer = times(source[0], inverses[0], True)
    finished[me[0]] = answer
    solved[...] = answer


def forward_kernel(level, owners, blocks, lists, me, source, inverses, lowers, finished_in, *rest):
    arrived, (finished, solved) = rest[: owners - 1], rest[owners - 1 :]
    own = me[0]
    for mask in range(1, owners):
        finished[(level - 1) * owners + (own ^ mask)] = arrived[mask - 1][...]
    total = source[level]
    for k in range(blocks):
        pulled = finished[lists[((level - 1) * owners + own) * blocks + k]]
        total = total - times(pulled, lowers[level - 1, k], True)
    answer = times(total, inverses[level], True)
    finished[level * owners + own] = answer
    solved[...] = answer


def backward_kernel(level, levels, owners, blocks, lists, me, inverses, lowers, finished, *rest):
    own = me[0]
    top = level == levels - 1
    rest = list(rest)
    if top:
        (accumulated, answers, sent) = rest
        accumulated[...] = jnp.zeros_like(accumulated)
        answers[...] = jnp.zeros_like(answers)
    else:
        arrived, rest = rest[: owners - 1], rest[owners - 1 :]
        (_, _, accumulated, answers, *sent) = rest
        for mask in range(1, owners):
            for k in range(blocks):
                column = lists[(level * owners + (own ^ mask)) * blocks + k]
                mine = (lax.rem(column, owners) == own).astype(jnp.float32)
                slot = lax.div(column, owners)
                accumulated[slot] += mine * arrived[mask - 1][k]
        sent = sent[0] if sent else None
    source = finished[level * owners + own] - accumulated[level]
    answer = times(source, inverses[level], False)
    answers[level] = answer
    if level > 0:
        for k in range(blocks):
            product = times(answer, lowers[level - 1, k], False)
            sent[k] = product
            column = lists[((level - 1) * owners + own) * blocks + k]
            mine = (lax.rem(column, owners) == own).astype(jnp.float32)
            slot = lax.div(column, owners)
            accumulated[slot] += mine * product


def in_vmem(array):
    return pltpu.with_memory_space_constraint(array, VMEM)


def shards(residual_in, diag_inverse, lower_blocks, column_lists):
    sweep_input = lax.all_to_all(residual_in, "col", split_axis=2, concat_axis=3, tiled=True)[:, 0]
    levels, probes, size = sweep_input.shape
    owners = lax.axis_size("row")
    blocks = column_lists.shape[2]
    me = lax.axis_index("row").astype(jnp.int32).reshape(1)
    lists = column_lists.reshape(-1)
    inverses = in_vmem(diag_inverse[:, 0])
    lowers = in_vmem(lower_blocks[:, 0])
    sweep_input = in_vmem(sweep_input)
    vmem = pl.BlockSpec(memory_space=VMEM)
    smem = pl.BlockSpec(memory_space=SMEM)
    params = pltpu.CompilerParams(vmem_limit_bytes=16 * 2**20)
    rows = VMEM((probes, size), jnp.float32)
    all_rows = VMEM((levels * owners, probes, size), jnp.float32)
    own_rows = VMEM((levels, probes, size), jnp.float32)
    products = VMEM((blocks, probes, size), jnp.float32)

    def exchange(array):
        return [
            in_vmem(lax.ppermute(array, "row", [(i, i ^ mask) for i in range(owners)]))
            for mask in range(1, owners)
        ]

    finished, solved = pl.pallas_call(
        functools.partial(first_kernel, owners),
        in_specs=[smem, smem, vmem, vmem],
        out_specs=[vmem, vmem],
        out_shape=[all_rows, rows],
        compiler_params=params,
        name="forward_first",
    )(lists, me, sweep_input, inverses)
    for level in range(1, levels):
        arrived = exchange(solved)
        finished, solved = pl.pallas_call(
            functools.partial(forward_kernel, level, owners, blocks),
            in_specs=[smem, smem] + [vmem] * (4 + owners - 1),
            out_specs=[vmem, vmem],
            out_shape=[all_rows, rows],
            input_output_aliases={5: 0},
            compiler_params=params,
            name="forward_level",
        )(lists, me, sweep_input, inverses, lowers, in_vmem(finished), *arrived)

    finished = in_vmem(finished)
    accumulated, answers, sent = pl.pallas_call(
        functools.partial(backward_kernel, levels - 1, levels, owners, blocks),
        in_specs=[smem, smem, vmem, vmem, vmem],
        out_specs=[vmem] * 3,
        out_shape=[own_rows, own_rows, products],
        compiler_params=params,
        name="backward_first",
    )(lists, me, inverses, lowers, finished)
    for level in reversed(range(levels - 1)):
        arrived = exchange(sent)
        base = 5 + owners - 1
        out = pl.pallas_call(
            functools.partial(backward_kernel, level, levels, owners, blocks),
            in_specs=[smem, smem] + [vmem] * (3 + owners - 1 + 2),
            out_specs=[vmem] * (3 if level else 2),
            out_shape=[own_rows, own_rows] + ([products] if level else []),
            input_output_aliases={base: 0, base + 1: 1},
            compiler_params=params,
            name="backward_level",
        )(lists, me, inverses, lowers, finished, *arrived, in_vmem(accumulated), in_vmem(answers))
        accumulated, answers = out[:2]
        sent = out[2] if level else None
    return lax.all_to_all(answers[:, None], "col", split_axis=3, concat_axis=2, tiled=True)


def solution(mesh):
    placed = (
        P(None, "row", None, "col"),
        P(None, "row", None, None),
        P(None, "row", None, None, None),
        P(),
    )
    return jax.shard_map(
        shards, mesh=mesh, in_specs=placed, out_specs=P(None, "row", None, "col"), check_vma=False
    )
```

time: 182 us -> 131 us (0.72)
  blocking collectives: 117 us -> 8.12 us
  starting transfers between devices: 6.33 us -> 55.7 us
  matrix products: 38.3 us -> 0 us
  waiting for transfers between devices: 4.95 us -> 41.9 us
  Pallas kernels: 0 us -> 14.4 us
  local copies, waits for them, and re-layouts: 11.5 us -> 8.76 us
    all_gather x14 -> x0, blocking collectives: 109 us -> none  [the longest x7 54.6 us: backward_step(): arrived = lax.all_gather(contributions[None], 'row', axis=0, tiled=True)]
    ppermute x0 -> x42, starting transfers between devices: none -> 49.4 us  [exchange(): lax.ppermute(array, 'row', [(i, i ^ mask) for i in range(owners)])]
    dot_general x37 -> x0, matrix products: 38.3 us -> none  [the longest x7 9.65 us: forward_step(): jnp.einsum('kpc,kdc->pd', pulled, factor_blocks, precision=highest)]
    ppermute x0 -> x42, waiting for transfers between devices: none -> 37.1 us  [exchange(): lax.ppermute(array, 'row', [(i, i ^ mask) for i in range(owners)])]
    pallas_call x0 -> x16, Pallas kernels: none -> 14.4 us  [the longest x7 6.94 us: shards(): pl.pallas_call(functools.partial(forward_kernel, level, owners, blocks),...]
    gather x7 -> x0, local copies, waits for them, and re-layouts: 3.99 us -> none  [forward_step(): finished.reshape(slot_count * owners, probe_count, block_size)[targets]]
    unnamed x6 -> x14, local copies, waits for them, and re-layouts: 3.03 us -> 6.79 us
  transfers between devices with their start and end apart: 1 -> 43, of which waited for: 1 -> 43; matrix products, arithmetic and copies ran while one was open for 0% -> 1% of each run, Pallas kernels for 0% -> 0%
where the time goes in v1:
time: 131 us
  starting transfers between devices  55.7 us (43%)
  waiting for transfers between devices  41.9 us (32%)
  Pallas kernels  14.4 us (11%)
  local copies, waits for them, and re-layouts  8.76 us (7%)
  blocking collectives  8.12 us (6%)
  other arithmetic  1.49 us (1%)
    ppermute x42, starting transfers between devices, exchange(): lax.ppermute(array, 'row', [(i, i ^ mask) for i in range(owners)])  49.4 us
    ppermute x42, waiting for transfers between devices, exchange(): lax.ppermute(array, 'row', [(i, i ^ mask) for i in range(owners)])  37.1 us
    all_to_all x1, blocking collectives, shards(): lax.all_to_all(answers[:, None], 'col', split_axis=3, concat_axis=2, tile...  8.12 us
    pallas_call x7, Pallas kernels, shards(): pl.pallas_call(functools.partial(forward_kernel, level, owners, blocks),...  6.94 us
    unnamed x14, local copies, waits for them, and re-layouts  6.79 us
    all_to_all x1, starting transfers between devices, shards(): lax.all_to_all(residual_in, 'col', split_axis=2, concat_axis=3, tiled=True)  6.33 us
    pallas_call x7, Pallas kernels, shards(): pl.pallas_call(functools.partial(backward_kernel, level, levels, owners,...  5.94 us
    all_to_all x1, waiting for transfers between devices, shards(): lax.all_to_all(residual_in, 'col', split_axis=2, concat_axis=3, tiled=True)  4.84 us
  transfers between devices with their start and end apart: 43, of which 43 were waited for; matrix products, arithmetic and copies ran while one was open for 1% of the time, Pallas kernels for 0%

profile of v1, /device:TPU:0, one launch (start us, length us, event | category | flops | bytes accessed | tf_op | source)
XLA Modules:
  0.0 130.5 jit_solution(17388396003359497231)
XLA Ops:
  1.7 6.3 %all-to-all-start = ((f32[8,1,1024]{2,1,0:T(1,128)}), f32[8,1,1024]{2,1,0:T(1,128)S(1)}, u32[]{:S(2)}, u32[]{:S(2)}) async-start(f32[8,1,1024]{2,1,0:T(1,128)} %reshape.9), calls=%async_computation | async-start | bytes 65536 | tf_op jit(solution)/shard_map/all_to_all | solution.py:85
  8.9 4.8 %all-to-all-done = f32[8,1,1024]{2,1,0:T(1,128)S(1)} async-done(((f32[8,1,1024]{2,1,0:T(1,128)}), f32[8,1,1024]{2,1,0:T(1,128)S(1)}, u32[]{:S(2)}, u32[]{:S(2)}) %all-to-all-start) | async-done | bytes 32800 | tf_op jit(solution)/shard_map/all_to_all | solution.py:85
  17.3 2.5 %collective-permute-start.2 = (f32[4,256]{1,0:T(4,128)S(1)}, f32[4,256]{1,0:T(4,128)S(1)}, u32[]{:S(2)}, u32[]{:S(2)}) collective-permute-start(f32[4,256]{1,0:T(4,128)S(1)} %get-tuple-element.43), channel_id=1, source_target_pairs={{0,24},{8,16},{16,8},{24,0},{1,25},{9,17},{17,9},{25,1},{2,26},{10... | collective-permute-start | bytes 12296 | tf_op jit(solution)/shard_map/ppermute | solution.py:104
  21.9 1.5 %collective-permute-done.1.rest_1_ = f32[4,256]{1,0:T(4,128)S(1)} collective-permute-done((f32[4,256]{1,0:T(4,128)S(1)}, f32[4,256]{1,0:T(4,128)S(1)}, u32[]{:S(2)}, u32[]{:S(2)}) %collective-permute-start.1) | collective-permute-done | bytes 4128 | tf_op jit(solution)/shard_map/ppermute | solution.py:104
  23.9 1.8 %copy-done = bf16[7,1,3,256,256]{4,3,2,1,0:T(8,128)(2,1)S(1)} copy-done((bf16[7,1,3,256,256]{4,3,2,1,0:T(8,128)(2,1)S(1)}, bf16[7,1,3,256,256]{4,3,2,1,0:T(8,128)(2,1)}, u32[]{:S(2)}) %copy-start) | copy-done | bytes 2752536
  26.6 1.5 %collective-permute-start.5 = (f32[4,256]{1,0:T(4,128)S(1)}, f32[4,256]{1,0:T(4,128)S(1)}, u32[]{:S(2)}, u32[]{:S(2)}) collective-permute-start(f32[4,256]{1,0:T(4,128)S(1)} %get-tuple-element.45), channel_id=1, source_target_pairs={{0,24},{8,16},{16,8},{24,0},{1,25},{9,17},{17,9},{25,1},{2,26},{10... | collective-permute-start | bytes 12296 | tf_op jit(solution)/shard_map/ppermute | solution.py:104
  33.1 2.5 %collective-permute-start.8 = (f32[4,256]{1,0:T(4,128)S(1)}, f32[4,256]{1,0:T(4,128)S(1)}, u32[]{:S(2)}, u32[]{:S(2)}) collective-permute-start(f32[4,256]{1,0:T(4,128)S(1)} %get-tuple-element.47), channel_id=1, source_target_pairs={{0,24},{8,16},{16,8},{24,0},{1,25},{9,17},{17,9},{25,1},{2,26},{10... | collective-permute-start | bytes 12296 | tf_op jit(solution)/shard_map/ppermute | solution.py:104
  37.6 1.5 %collective-permute-done.7.rest_1_ = f32[4,256]{1,0:T(4,128)S(1)} collective-permute-done((f32[4,256]{1,0:T(4,128)S(1)}, f32[4,256]{1,0:T(4,128)S(1)}, u32[]{:S(2)}, u32[]{:S(2)}) %collective-permute-start.7) | collective-permute-done | bytes 4128 | tf_op jit(solution)/shard_map/ppermute | solution.py:104
  40.6 1.5 %collective-permute-start.11 = (f32[4,256]{1,0:T(4,128)S(1)}, f32[4,256]{1,0:T(4,128)S(1)}, u32[]{:S(2)}, u32[]{:S(2)}) collective-permute-start(f32[4,256]{1,0:T(4,128)S(1)} %get-tuple-element.49), channel_id=1, source_target_pairs={{0,24},{8,16},{16,8},{24,0},{1,25},{9,17},{17,9},{25,1},{2,26},{10... | collective-permute-start | bytes 12296 | tf_op jit(solution)/shard_map/ppermute | solution.py:104
  47.1 2.5 %collective-permute-start.14 = (f32[4,256]{1,0:T(4,128)S(1)}, f32[4,256]{1,0:T(4,128)S(1)}, u32[]{:S(2)}, u32[]{:S(2)}) collective-permute-start(f32[4,256]{1,0:T(4,128)S(1)} %get-tuple-element.51), channel_id=1, source_target_pairs={{0,24},{8,16},{16,8},{24,0},{1,25},{9,17},{17,9},{25,1},{2,26},{10... | collective-permute-start | bytes 12296 | tf_op jit(solution)/shard_map/ppermute | solution.py:104
  51.7 1.5 %collective-permute-done.13.rest_1_ = f32[4,256]{1,0:T(4,128)S(1)} collective-permute-done((f32[4,256]{1,0:T(4,128)S(1)}, f32[4,256]{1,0:T(4,128)S(1)}, u32[]{:S(2)}, u32[]{:S(2)}) %collective-permute-start.13) | collective-permute-done | bytes 4128 | tf_op jit(solution)/shard_map/ppermute | solution.py:104
  54.6 1.5 %collective-permute-start.17 = (f32[4,256]{1,0:T(4,128)S(1)}, f32[4,256]{1,0:T(4,128)S(1)}, u32[]{:S(2)}, u32[]{:S(2)}) collective-permute-start(f32[4,256]{1,0:T(4,128)S(1)} %get-tuple-element.53), channel_id=1, source_target_pairs={{0,24},{8,16},{16,8},{24,0},{1,25},{9,17},{17,9},{25,1},{2,26},{10... | collective-permute-start | bytes 12296 | tf_op jit(solution)/shard_map/ppermute | solution.py:104
  61.2 2.5 %collective-permute-start.20 = (f32[4,256]{1,0:T(4,128)S(1)}, f32[4,256]{1,0:T(4,128)S(1)}, u32[]{:S(2)}, u32[]{:S(2)}) collective-permute-start(f32[4,256]{1,0:T(4,128)S(1)} %get-tuple-element.55), channel_id=1, source_target_pairs={{0,24},{8,16},{16,8},{24,0},{1,25},{9,17},{17,9},{25,1},{2,26},{10... | collective-permute-start | bytes 12296 | tf_op jit(solution)/shard_map/ppermute | solution.py:104
  65.7 1.5 %collective-permute-done.19.rest_1_ = f32[4,256]{1,0:T(4,128)S(1)} collective-permute-done((f32[4,256]{1,0:T(4,128)S(1)}, f32[4,256]{1,0:T(4,128)S(1)}, u32[]{:S(2)}, u32[]{:S(2)}) %collective-permute-start.19) | collective-permute-done | bytes 4128 | tf_op jit(solution)/shard_map/ppermute | solution.py:104
  67.7 1.5 %forward_level.13 = (f32[32,4,256]{2,1,0:T(4,128)S(1)}, f32[4,256]{1,0:T(4,128)}) custom-call(s32[84]{0:T(128)S(1)} %reshape.7.lists, s32[1]{0:T(128)} %bitcast.me, f32[8,4,256]{2,1,0:T(4,128)S(1)} %squeeze.11.source, bf16[8,256,256]{2,1,0:T(8,128)(2,1)S(1)} %bitcast.44, bf16[7,3,256,256]{3,2,1,0:T(8,128)(2,1)S(1)} %bitcast.28, ...), custom_call_target="tpu_custom_call", output_to_operand_aliasing={{0}: (5, {})} | custom-call | tf_op jit(solution)/shard_map/forward_level/pallas_call | solution.py:118
  70.1 1.5 %collective-permute-start.23 = (f32[3,4,256]{2,1,0:T(4,128)S(1)}, f32[3,4,256]{2,1,0:T(4,128)S(1)}, u32[]{:S(2)}, u32[]{:S(2)}) collective-permute-start(f32[3,4,256]{2,1,0:T(4,128)S(1)} %get-tuple-element.57), channel_id=1, source_target_pairs={{0,24},{8,16},{16,8},{24,0},{1,25},{9,17},{17,9},{25,1},{2,26},{10... | collective-permute-start | bytes 36872 | tf_op jit(solution)/shard_map/ppermute | solution.py:104
  76.8 2.5 %collective-permute-start.26 = (f32[3,4,256]{2,1,0:T(4,128)S(1)}, f32[3,4,256]{2,1,0:T(4,128)S(1)}, u32[]{:S(2)}, u32[]{:S(2)}) collective-permute-start(f32[3,4,256]{2,1,0:T(4,128)S(1)} %get-tuple-element.60), channel_id=1, source_target_pairs={{0,24},{8,16},{16,8},{24,0},{1,25},{9,17},{17,9},{25,1},{2,26},{10... | collective-permute-start | bytes 36872 | tf_op jit(solution)/shard_map/ppermute | solution.py:104
  81.4 1.5 %collective-permute-done.25.rest_1_ = f32[3,4,256]{2,1,0:T(4,128)S(1)} collective-permute-done((f32[3,4,256]{2,1,0:T(4,128)S(1)}, f32[3,4,256]{2,1,0:T(4,128)S(1)}, u32[]{:S(2)}, u32[]{:S(2)}) %collective-permute-start.25) | collective-permute-done | bytes 12320 | tf_op jit(solution)/shard_map/ppermute | solution.py:104
  84.3 1.5 %collective-permute-start.29 = (f32[3,4,256]{2,1,0:T(4,128)S(1)}, f32[3,4,256]{2,1,0:T(4,128)S(1)}, u32[]{:S(2)}, u32[]{:S(2)}) collective-permute-start(f32[3,4,256]{2,1,0:T(4,128)S(1)} %get-tuple-element.63), channel_id=1, source_target_pairs={{0,24},{8,16},{16,8},{24,0},{1,25},{9,17},{17,9},{25,1},{2,26},{10... | collective-permute-start | bytes 36872 | tf_op jit(solution)/shard_map/ppermute | solution.py:104
  91.1 2.3 %collective-permute-start.32 = (f32[3,4,256]{2,1,0:T(4,128)S(1)}, f32[3,4,256]{2,1,0:T(4,128)S(1)}, u32[]{:S(2)}, u32[]{:S(2)}) collective-permute-start(f32[3,4,256]{2,1,0:T(4,128)S(1)} %get-tuple-element.66), channel_id=1, source_target_pairs={{0,24},{8,16},{16,8},{24,0},{1,25},{9,17},{17,9},{25,1},{2,26},{10... | collective-permute-start | bytes 36872 | tf_op jit(solution)/shard_map/ppermute | solution.py:104
  98.5 1.5 %collective-permute-start.35 = (f32[3,4,256]{2,1,0:T(4,128)S(1)}, f32[3,4,256]{2,1,0:T(4,128)S(1)}, u32[]{:S(2)}, u32[]{:S(2)}) collective-permute-start(f32[3,4,256]{2,1,0:T(4,128)S(1)} %get-tuple-element.69), channel_id=1, source_target_pairs={{0,24},{8,16},{16,8},{24,0},{1,25},{9,17},{17,9},{25,1},{2,26},{10... | collective-permute-start | bytes 36872 | tf_op jit(solution)/shard_map/ppermute | solution.py:104
  105.3 2.3 %collective-permute-start.38 = (f32[3,4,256]{2,1,0:T(4,128)S(1)}, f32[3,4,256]{2,1,0:T(4,128)S(1)}, u32[]{:S(2)}, u32[]{:S(2)}) collective-permute-start(f32[3,4,256]{2,1,0:T(4,128)S(1)} %get-tuple-element.72), channel_id=1, source_target_pairs={{0,24},{8,16},{16,8},{24,0},{1,25},{9,17},{17,9},{25,1},{2,26},{10... | collective-permute-start | bytes 36872 | tf_op jit(solution)/shard_map/ppermute | solution.py:104
  112.7 1.5 %collective-permute-start.41 = (f32[3,4,256]{2,1,0:T(4,128)S(1)}, f32[3,4,256]{2,1,0:T(4,128)S(1)}, u32[]{:S(2)}, u32[]{:S(2)}) collective-permute-start(f32[3,4,256]{2,1,0:T(4,128)S(1)} %get-tuple-element.75), channel_id=1, source_target_pairs={{0,24},{8,16},{16,8},{24,0},{1,25},{9,17},{17,9},{25,1},{2,26},{10... | collective-permute-start | bytes 36872 | tf_op jit(solution)/shard_map/ppermute | solution.py:104
  120.1 8.1 %all_to_all.33 = f32[8,1,1024]{2,1,0:T(1,128)S(1)} all-to-all(f32[8,1,1024]{2,1,0:T(1,128)S(1)} %reshape.11), channel_id=1, replica_groups=mesh['row'=4,'col'=8] {'col'}, dimensions={0} | all-to-all | bytes 65536 | tf_op jit(solution)/shard_map/all_to_all | solution.py:151
  (101 shorter events, 72.5 us)
Async XLA Ops:
  1.7 12.1 %all-to-all-start = ((f32[8,1,1024]{2,1,0:T(1,128)}), f32[8,1,1024]{2,1,0:T(1,128)S(1)}, u32[]{:S(2)}, u32[]{:S(2)}) async-start(f32[8,1,1024]{2,1,0:T(1,128)} %reshape.9), calls=%async_computation | async-start | bytes 65536 | tf_op jit(solution)/shard_map/all_to_all | solution.py:85
  17.3 4.5 %collective-permute-start.2 = (f32[4,256]{1,0:T(4,128)S(1)}, f32[4,256]{1,0:T(4,128)S(1)}, u32[]{:S(2)}, u32[]{:S(2)}) collective-permute-start(f32[4,256]{1,0:T(4,128)S(1)} %get-tuple-element.43), channel_id=1, source_target_pairs={{0,24},{8,16},{16,8},{24,0},{1,25},{9,17},{17,9},{25,1},{2,26},{10... | collective-permute-start | bytes 12296 | tf_op jit(solution)/shard_map/ppermute | solution.py:104
  26.6 4.5 %collective-permute-start.5 = (f32[4,256]{1,0:T(4,128)S(1)}, f32[4,256]{1,0:T(4,128)S(1)}, u32[]{:S(2)}, u32[]{:S(2)}) collective-permute-start(f32[4,256]{1,0:T(4,128)S(1)} %get-tuple-element.45), channel_id=1, source_target_pairs={{0,24},{8,16},{16,8},{24,0},{1,25},{9,17},{17,9},{25,1},{2,26},{10... | collective-permute-start | bytes 12296 | tf_op jit(solution)/shard_map/ppermute | solution.py:104
  33.1 4.5 %collective-permute-start.8 = (f32[4,256]{1,0:T(4,128)S(1)}, f32[4,256]{1,0:T(4,128)S(1)}, u32[]{:S(2)}, u32[]{:S(2)}) collective-permute-start(f32[4,256]{1,0:T(4,128)S(1)} %get-tuple-element.47), channel_id=1, source_target_pairs={{0,24},{8,16},{16,8},{24,0},{1,25},{9,17},{17,9},{25,1},{2,26},{10... | collective-permute-start | bytes 12296 | tf_op jit(solution)/shard_map/ppermute | solution.py:104
  40.6 4.5 %collective-permute-start.11 = (f32[4,256]{1,0:T(4,128)S(1)}, f32[4,256]{1,0:T(4,128)S(1)}, u32[]{:S(2)}, u32[]{:S(2)}) collective-permute-start(f32[4,256]{1,0:T(4,128)S(1)} %get-tuple-element.49), channel_id=1, source_target_pairs={{0,24},{8,16},{16,8},{24,0},{1,25},{9,17},{17,9},{25,1},{2,26},{10... | collective-permute-start | bytes 12296 | tf_op jit(solution)/shard_map/ppermute | solution.py:104
  47.1 4.5 %collective-permute-start.14 = (f32[4,256]{1,0:T(4,128)S(1)}, f32[4,256]{1,0:T(4,128)S(1)}, u32[]{:S(2)}, u32[]{:S(2)}) collective-permute-start(f32[4,256]{1,0:T(4,128)S(1)} %get-tuple-element.51), channel_id=1, source_target_pairs={{0,24},{8,16},{16,8},{24,0},{1,25},{9,17},{17,9},{25,1},{2,26},{10... | collective-permute-start | bytes 12296 | tf_op jit(solution)/shard_map/ppermute | solution.py:104
  54.6 4.5 %collective-permute-start.17 = (f32[4,256]{1,0:T(4,128)S(1)}, f32[4,256]{1,0:T(4,128)S(1)}, u32[]{:S(2)}, u32[]{:S(2)}) collective-permute-start(f32[4,256]{1,0:T(4,128)S(1)} %get-tuple-element.53), channel_id=1, source_target_pairs={{0,24},{8,16},{16,8},{24,0},{1,25},{9,17},{17,9},{25,1},{2,26},{10... | collective-permute-start | bytes 12296 | tf_op jit(solution)/shard_map/ppermute | solution.py:104
  61.2 4.5 %collective-permute-start.20 = (f32[4,256]{1,0:T(4,128)S(1)}, f32[4,256]{1,0:T(4,128)S(1)}, u32[]{:S(2)}, u32[]{:S(2)}) collective-permute-start(f32[4,256]{1,0:T(4,128)S(1)} %get-tuple-element.55), channel_id=1, source_target_pairs={{0,24},{8,16},{16,8},{24,0},{1,25},{9,17},{17,9},{25,1},{2,26},{10... | collective-permute-start | bytes 12296 | tf_op jit(solution)/shard_map/ppermute | solution.py:104
  70.1 4.7 %collective-permute-start.23 = (f32[3,4,256]{2,1,0:T(4,128)S(1)}, f32[3,4,256]{2,1,0:T(4,128)S(1)}, u32[]{:S(2)}, u32[]{:S(2)}) collective-permute-start(f32[3,4,256]{2,1,0:T(4,128)S(1)} %get-tuple-element.57), channel_id=1, source_target_pairs={{0,24},{8,16},{16,8},{24,0},{1,25},{9,17},{17,9},{25,1},{2,26},{10... | collective-permute-start | bytes 36872 | tf_op jit(solution)/shard_map/ppermute | solution.py:104
  71.7 3.7 %collective-permute-start.22 = (f32[3,4,256]{2,1,0:T(4,128)S(1)}, f32[3,4,256]{2,1,0:T(4,128)S(1)}, u32[]{:S(2)}, u32[]{:S(2)}) collective-permute-start(f32[3,4,256]{2,1,0:T(4,128)S(1)} %get-tuple-element.57), channel_id=1, source_target_pairs={{0,16},{8,24},{16,0},{24,8},{1,17},{9,25},{17,1},{25,9},{2,18},{10... | collective-permute-start | bytes 36872 | tf_op jit(solution)/shard_map/ppermute | solution.py:104
  72.2 3.7 %collective-permute-start.21 = (f32[3,4,256]{2,1,0:T(4,128)S(1)}, f32[3,4,256]{2,1,0:T(4,128)S(1)}, u32[]{:S(2)}, u32[]{:S(2)}) collective-permute-start(f32[3,4,256]{2,1,0:T(4,128)S(1)} %get-tuple-element.57), channel_id=1, source_target_pairs={{0,8},{8,0},{16,24},{24,16},{1,9},{9,1},{17,25},{25,17},{2,10},{10... | collective-permute-start | bytes 36872 | tf_op jit(solution)/shard_map/ppermute | solution.py:104
  76.8 4.7 %collective-permute-start.26 = (f32[3,4,256]{2,1,0:T(4,128)S(1)}, f32[3,4,256]{2,1,0:T(4,128)S(1)}, u32[]{:S(2)}, u32[]{:S(2)}) collective-permute-start(f32[3,4,256]{2,1,0:T(4,128)S(1)} %get-tuple-element.60), channel_id=1, source_target_pairs={{0,24},{8,16},{16,8},{24,0},{1,25},{9,17},{17,9},{25,1},{2,26},{10... | collective-permute-start | bytes 36872 | tf_op jit(solution)/shard_map/ppermute | solution.py:104
  79.2 3.7 %collective-permute-start.25 = (f32[3,4,256]{2,1,0:T(4,128)S(1)}, f32[3,4,256]{2,1,0:T(4,128)S(1)}, u32[]{:S(2)}, u32[]{:S(2)}) collective-permute-start(f32[3,4,256]{2,1,0:T(4,128)S(1)} %get-tuple-element.60), channel_id=1, source_target_pairs={{0,16},{8,24},{16,0},{24,8},{1,17},{9,25},{17,1},{25,9},{2,18},{10... | collective-permute-start | bytes 36872 | tf_op jit(solution)/shard_map/ppermute | solution.py:104
  79.7 3.8 %collective-permute-start.24 = (f32[3,4,256]{2,1,0:T(4,128)S(1)}, f32[3,4,256]{2,1,0:T(4,128)S(1)}, u32[]{:S(2)}, u32[]{:S(2)}) collective-permute-start(f32[3,4,256]{2,1,0:T(4,128)S(1)} %get-tuple-element.60), channel_id=1, source_target_pairs={{0,8},{8,0},{16,24},{24,16},{1,9},{9,1},{17,25},{25,17},{2,10},{10... | collective-permute-start | bytes 36872 | tf_op jit(solution)/shard_map/ppermute | solution.py:104
  84.3 4.7 %collective-permute-start.29 = (f32[3,4,256]{2,1,0:T(4,128)S(1)}, f32[3,4,256]{2,1,0:T(4,128)S(1)}, u32[]{:S(2)}, u32[]{:S(2)}) collective-permute-start(f32[3,4,256]{2,1,0:T(4,128)S(1)} %get-tuple-element.63), channel_id=1, source_target_pairs={{0,24},{8,16},{16,8},{24,0},{1,25},{9,17},{17,9},{25,1},{2,26},{10... | collective-permute-start | bytes 36872 | tf_op jit(solution)/shard_map/ppermute | solution.py:104
  85.8 3.7 %collective-permute-start.28 = (f32[3,4,256]{2,1,0:T(4,128)S(1)}, f32[3,4,256]{2,1,0:T(4,128)S(1)}, u32[]{:S(2)}, u32[]{:S(2)}) collective-permute-start(f32[3,4,256]{2,1,0:T(4,128)S(1)} %get-tuple-element.63), channel_id=1, source_target_pairs={{0,16},{8,24},{16,0},{24,8},{1,17},{9,25},{17,1},{25,9},{2,18},{10... | collective-permute-start | bytes 36872 | tf_op jit(solution)/shard_map/ppermute | solution.py:104
  91.1 4.8 %collective-permute-start.32 = (f32[3,4,256]{2,1,0:T(4,128)S(1)}, f32[3,4,256]{2,1,0:T(4,128)S(1)}, u32[]{:S(2)}, u32[]{:S(2)}) collective-permute-start(f32[3,4,256]{2,1,0:T(4,128)S(1)} %get-tuple-element.66), channel_id=1, source_target_pairs={{0,24},{8,16},{16,8},{24,0},{1,25},{9,17},{17,9},{25,1},{2,26},{10... | collective-permute-start | bytes 36872 | tf_op jit(solution)/shard_map/ppermute | solution.py:104
  93.4 3.7 %collective-permute-start.31 = (f32[3,4,256]{2,1,0:T(4,128)S(1)}, f32[3,4,256]{2,1,0:T(4,128)S(1)}, u32[]{:S(2)}, u32[]{:S(2)}) collective-permute-start(f32[3,4,256]{2,1,0:T(4,128)S(1)} %get-tuple-element.66), channel_id=1, source_target_pairs={{0,16},{8,24},{16,0},{24,8},{1,17},{9,25},{17,1},{25,9},{2,18},{10... | collective-permute-start | bytes 36872 | tf_op jit(solution)/shard_map/ppermute | solution.py:104
  98.5 4.7 %collective-permute-start.35 = (f32[3,4,256]{2,1,0:T(4,128)S(1)}, f32[3,4,256]{2,1,0:T(4,128)S(1)}, u32[]{:S(2)}, u32[]{:S(2)}) collective-permute-start(f32[3,4,256]{2,1,0:T(4,128)S(1)} %get-tuple-element.69), channel_id=1, source_target_pairs={{0,24},{8,16},{16,8},{24,0},{1,25},{9,17},{17,9},{25,1},{2,26},{10... | collective-permute-start | bytes 36872 | tf_op jit(solution)/shard_map/ppermute | solution.py:104
  105.3 4.7 %collective-permute-start.38 = (f32[3,4,256]{2,1,0:T(4,128)S(1)}, f32[3,4,256]{2,1,0:T(4,128)S(1)}, u32[]{:S(2)}, u32[]{:S(2)}) collective-permute-start(f32[3,4,256]{2,1,0:T(4,128)S(1)} %get-tuple-element.72), channel_id=1, source_target_pairs={{0,24},{8,16},{16,8},{24,0},{1,25},{9,17},{17,9},{25,1},{2,26},{10... | collective-permute-start | bytes 36872 | tf_op jit(solution)/shard_map/ppermute | solution.py:104
  107.6 3.7 %collective-permute-start.37 = (f32[3,4,256]{2,1,0:T(4,128)S(1)}, f32[3,4,256]{2,1,0:T(4,128)S(1)}, u32[]{:S(2)}, u32[]{:S(2)}) collective-permute-start(f32[3,4,256]{2,1,0:T(4,128)S(1)} %get-tuple-element.72), channel_id=1, source_target_pairs={{0,16},{8,24},{16,0},{24,8},{1,17},{9,25},{17,1},{25,9},{2,18},{10... | collective-permute-start | bytes 36872 | tf_op jit(solution)/shard_map/ppermute | solution.py:104
  112.7 4.7 %collective-permute-start.41 = (f32[3,4,256]{2,1,0:T(4,128)S(1)}, f32[3,4,256]{2,1,0:T(4,128)S(1)}, u32[]{:S(2)}, u32[]{:S(2)}) collective-permute-start(f32[3,4,256]{2,1,0:T(4,128)S(1)} %get-tuple-element.75), channel_id=1, source_target_pairs={{0,24},{8,16},{16,8},{24,0},{1,25},{9,17},{17,9},{25,1},{2,26},{10... | collective-permute-start | bytes 36872 | tf_op jit(solution)/shard_map/ppermute | solution.py:104
  114.2 3.7 %collective-permute-start.40 = (f32[3,4,256]{2,1,0:T(4,128)S(1)}, f32[3,4,256]{2,1,0:T(4,128)S(1)}, u32[]{:S(2)}, u32[]{:S(2)}) collective-permute-start(f32[3,4,256]{2,1,0:T(4,128)S(1)} %get-tuple-element.75), channel_id=1, source_target_pairs={{0,16},{8,24},{16,0},{24,8},{1,17},{9,25},{17,1},{25,9},{2,18},{10... | collective-permute-start | bytes 36872 | tf_op jit(solution)/shard_map/ppermute | solution.py:104
  114.9 3.7 %collective-permute-start.39 = (f32[3,4,256]{2,1,0:T(4,128)S(1)}, f32[3,4,256]{2,1,0:T(4,128)S(1)}, u32[]{:S(2)}, u32[]{:S(2)}) collective-permute-start(f32[3,4,256]{2,1,0:T(4,128)S(1)} %get-tuple-element.75), channel_id=1, source_target_pairs={{0,8},{8,0},{16,24},{24,16},{1,9},{9,1},{17,25},{25,17},{2,10},{10... | collective-permute-start | bytes 36872 | tf_op jit(solution)/shard_map/ppermute | solution.py:104
  (23 other events, 88.2 us)

commit v2 on v0

v2 whole, which is shorter than its diff:
```python
import types

import jax
import jax.numpy as jnp
from jax import lax
from jax.experimental import pallas as pl
from jax.experimental.pallas import tpu as pltpu
from jax.sharding import PartitionSpec as P

VMEM = pltpu.VMEM
SMEM = pltpu.SMEM
F32 = jnp.float32
BF16 = jnp.bfloat16
GROUPS = ()
SCALARS = ("lists", "listed")
FAR = ("residual", "diag_inverse", "lower_blocks", "gathered")


def two_parts(rows):
    high = rows.astype(BF16).astype(F32)
    return jnp.concatenate([high, rows - high], axis=0).astype(BF16)


def times(rows, block, transposed):
    contract = 1 if transposed else 0
    product = lax.dot_general(
        two_parts(rows), block, (((1,), (contract,)), ((), ())), preferred_element_type=F32
    )
    count = rows.shape[0]
    return product[:count] + product[count:]


def lane_group(shape, width):
    return lax.broadcasted_iota(jnp.int32, shape, 1) // width


def regroup(pieces, width):
    rows, size = pieces[0].shape
    groups = size // width
    stacked = jnp.concatenate(pieces, axis=0)
    rolled = [stacked if d == 0 else pltpu.roll(stacked, d * width, 1) for d in range(groups)]
    group = lane_group((rows, size), width)

    def result(b):
        total = jnp.zeros((rows, size), F32)
        for a in range(len(pieces)):
            moved = rolled[(a - b) % groups][a * rows : (a + 1) * rows]
            total = jnp.where(group == a, moved, total)
        return total

    return result


def regroup_one(pieces, width, b):
    rows, size = pieces[0].shape
    groups = size // width
    group = lane_group((rows, size), width)
    total = jnp.zeros((rows, size), F32)
    for a, piece in enumerate(pieces):
        shift = (a - b) % groups
        total = jnp.where(group == a, pltpu.roll(piece, shift * width, 1) if shift else piece, total)
    return total


def placed_in(key, array):
    if key == "listed":
        return array
    space = SMEM if key in SCALARS else pltpu.HBM if key in FAR else VMEM
    return pltpu.with_memory_space_constraint(array, space)


def call(name, body, reads, updates=None, makes=None, scratch=None, cost=None):
    updates, makes, scratch = updates or {}, makes or {}, scratch or {}
    ins = {**reads, **updates}
    outs = {key: VMEM(value.shape, value.dtype) for key, value in updates.items()} | makes
    in_names, out_names, scratch_names = list(ins), list(outs), list(scratch)

    def kernel(*refs):
        space = types.SimpleNamespace()
        for key, ref in zip(in_names + out_names + scratch_names, refs, strict=True):
            setattr(space, key, ref)
        space.place = (lax.axis_index("row"), lax.axis_index("col"))
        body(space)

    def spec(key):
        if key in SCALARS:
            return pl.BlockSpec(memory_space=SMEM)
        return pl.BlockSpec(memory_space=pltpu.HBM if key in FAR else VMEM)

    results = pl.pallas_call(
        kernel,
        in_specs=[spec(key) for key in in_names],
        out_specs=[spec(key) for key in out_names],
        out_shape=[outs[key] for key in out_names],
        input_output_aliases={in_names.index(key): out_names.index(key) for key in updates},
        scratch_shapes=list(scratch.values()),
        compiler_params=pltpu.CompilerParams(vmem_limit_bytes=24 * 2**20),
        cost_estimate=cost,
        name=name,
    )(*[placed_in(key, value) for key, value in ins.items()])
    return dict(zip(out_names, results, strict=True))


def shards(residual_in, diag_inverse, lower_blocks, column_lists):
    levels, _, probes, width = residual_in.shape
    size = diag_inverse.shape[-1]
    owners, columns = lax.axis_size("row"), lax.axis_size("col")
    each = probes // columns
    blocks = column_lists.shape[2]
    pair = 2
    shared_groups = GROUPS if owners <= 4 and blocks == 3 else ()
    shared_levels = [level for group in shared_groups for level in group]
    shared_forward = [level for level in shared_levels if level == levels - 2]
    rows = VMEM((each, size), F32)
    all_rows = VMEM((levels * owners, each, size), F32)
    own_rows = VMEM((levels, each, size), F32)
    products = VMEM((blocks, each, size), F32)
    messages = VMEM((owners * columns, 2 * each, size), F32)
    ring = [position ^ (position >> 1) for position in range(owners)]

    def exchange(array):
        return {
            f"arrived_{mask}": lax.ppermute(array, "row", [(i, i ^ mask) for i in range(owners)])
            for mask in range(1, owners)
        }

    def to_all(array):
        return lax.all_to_all(array, ("row", "col"), split_axis=0, concat_axis=0, tiled=True)

    def column_of(r, level, owner, k):
        return r.lists[((level - 1) * owners + owner) * blocks + k]

    def send_body(r):
        first = pltpu.make_async_copy(r.residual, r.near, r.sems.at[0])
        second = pltpu.make_async_copy(r.diag_inverse.at[0, 0], r.inverse, r.sems.at[1])
        first.start()
        second.start()

        def widened(array, shift):
            padded = jnp.concatenate([array, jnp.zeros((probes, size - width), F32)], axis=1)
            return pltpu.roll(padded, shift, 1)

        first.wait()
        packed = widened(r.near[1, 0], 0)
        for level in range(2, levels):
            packed = packed + widened(r.near[level, 0], (level - 1) * width)
        start = widened(r.near[0, 0], r.place[1] * width)
        second.wait()
        partial = times(start, r.inverse[...], True)
        for column in range(columns):
            part = slice(column * each, (column + 1) * each)
            message = jnp.concatenate([partial[part], packed[part]], axis=0)
            for owner in range(owners):
                r.messages[owner * columns + column] = message

    def hold_body(r):
        for i in range(r.lists.shape[0]):
            r.lists[i] = r.listed[i]
        first = pltpu.make_async_copy(r.diag_inverse.at[:, 0], r.inverses, r.sems.at[0])
        second = pltpu.make_async_copy(r.lower_blocks.at[:, 0], r.lowers, r.sems.at[1])
        first.start()
        second.start()
        first.wait()
        second.wait()

    def widen_body(group):
        def body(r):
            half = lax.rem(r.place[1], pair)

            @pl.when(half == 0)
            def _():
                copies = []
                for n, level in enumerate(group):
                    copies.append(pltpu.make_async_copy(r.diag_inverse.at[level, 0], r.near.at[n, 0], r.sems.at[n, 0]))
                    copies.append(pltpu.make_async_copy(r.lower_blocks.at[level - 1, 0, 0], r.near.at[n, 1], r.sems.at[n, 1]))
                for copy in copies:
                    copy.start()
                for copy in copies:
                    copy.wait()

            @pl.when(half != 0)
            def _():
                copies = []
                for n, level in enumerate(group):
                    for k in (1, 2):
                        source = r.lower_blocks.at[level - 1, 0, k]
                        copies.append(pltpu.make_async_copy(source, r.near.at[n, k - 1], r.sems.at[n, k - 1]))
                for copy in copies:
                    copy.start()
                for copy in copies:
                    copy.wait()

            r.wide[...] = r.near[...].astype(F32)

        return body

    def narrow_body(n):
        def body(r):
            copies = [
                pltpu.make_async_copy(r.gathered.at[p, n], r.near.at[p], r.sems.at[p]) for p in range(owners * pair)
            ]
            for copy in copies:
                copy.start()
            for p, copy in enumerate(copies):
                copy.wait()
                r.shared[p] = r.near[p].astype(BF16)

        return body

    def shared_block(r, owner, k):
        return r.shared[ring.index(owner) * pair + k // 2, k % 2]

    def own_forward(r, level):
        own = r.place[0]
        total = r.source[level]
        for k in range(blocks):
            total = total - times(r.finished[column_of(r, level, own, k)], r.lowers[level - 1, k], True)
        answer = times(total, r.inverses[level], True)
        r.finished[level * owners + own] = answer
        return answer

    def all_forward(r, level):
        answers = []
        for owner in range(owners):
            pieces = [r.received[owner * columns + c, each:] for c in range(columns)]
            total = regroup_one(pieces, width, level - 1)
            for k in range(blocks):
                total = total - times(r.finished[column_of(r, level, owner, k)], shared_block(r, owner, k + 1), True)
            answers.append(times(total, shared_block(r, owner, 0), True))
        for owner in range(owners):
            r.finished[level * owners + owner] = answers[owner]

    def own_backward(r, level):
        row = level * owners + r.place[0]
        answer = times(r.finished[row] - r.accumulated[row], r.inverses[level], False)
        r.answers[level] = answer
        return answer

    def own_products(r, level, answer):
        for k in range(blocks):
            product = times(answer, r.lowers[level - 1, k], False)
            r.sent[k] = product
            r.accumulated[column_of(r, level, r.place[0], k)] += product

    def all_backward(r, level):
        answers = []
        for owner in range(owners):
            row = level * owners + owner
            answers.append(times(r.finished[row] - r.accumulated[row], shared_block(r, owner, 0), False))
        results = [
            [times(answers[owner], shared_block(r, owner, k + 1), False) for k in range(blocks)] for owner in range(owners)
        ]
        own_answer = answers[0]
        for owner in range(1, owners):
            own_answer = jnp.where(r.place[0] == owner, answers[owner], own_answer)
        r.answers[level] = own_answer
        for owner in range(owners):
            for k in range(blocks):
                r.accumulated[column_of(r, level, owner, k)] += results[owner][k]

    def take_finished(r, level):
        for mask in range(1, owners):
            r.finished[level * owners + (r.place[0] ^ mask)] = getattr(r, f"arrived_{mask}")[...]

    def take_products(r, level):
        for mask in range(1, owners):
            for k in range(blocks):
                column = column_of(r, level, r.place[0] ^ mask, k)
                r.accumulated[column] += getattr(r, f"arrived_{mask}")[k]

    def receive_body(r):
        for owner in range(owners):
            total = r.received[owner * columns, :each]
            for column in range(1, columns):
                total = total + r.received[owner * columns + column, :each]
            r.finished[owner] = total
        moved = regroup([r.received[r.place[0] * columns + c, each:] for c in range(columns)], width)
        for level in range(1, levels):
            r.source[level] = moved(level - 1)
        r.solved[...] = own_forward(r, 1)

    def last_send(r):
        answer = own_backward(r, 1)
        r.pieces[...] = jnp.zeros_like(r.pieces)
        r.pieces[r.place[0]] = r.finished[r.place[0]] - r.accumulated[r.place[0]]
        for k in range(blocks):
            r.pieces[column_of(r, 1, r.place[0], k)] -= times(answer, r.lowers[0, k], False)
        moved = regroup([r.answers[level] for level in range(1, levels)], width)
        for column in range(columns):
            packed = moved(column)
            for owner in range(owners):
                r.messages[owner * columns + column] = jnp.concatenate([r.pieces[owner], packed], axis=0)

    def last_body(r):
        sums, packed = [], []
        for column in range(columns):
            total = r.received[column, :each]
            for owner in range(1, owners):
                total = total + r.received[owner * columns + column, :each]
            sums.append(total)
            packed.append(r.received[r.place[0] * columns + column, each:])
        answer = times(jnp.concatenate(sums, axis=0), r.inverses[0], False)
        r.out[0, 0] = pltpu.roll(answer, lax.rem(size - r.place[1] * width, size), 1)[:, :width]
        packed = jnp.concatenate(packed, axis=0)
        for level in range(1, levels):
            moved = packed if level == 1 else pltpu.roll(packed, size - (level - 1) * width, 1)
            r.out[level, 0] = moved[:, :width]

    dma = pltpu.SemaphoreType.DMA
    far_blocks = {"diag_inverse": diag_inverse, "lower_blocks": lower_blocks}

    order = [
        [owner * columns + column + half for owner in ring for half in range(pair)]
        for column in range(0, columns, pair)
    ]
    gathered = {}
    for g, group in enumerate(shared_groups):
        wide = call(
            f"widen_{g}", widen_body(group), far_blocks,
            makes={"wide": jax.ShapeDtypeStruct((len(group), 2, size, size), F32)},
            scratch={"near": VMEM((len(group), 2, size, size), BF16), "sems": dma((len(group), 2))},
        )["wide"]
        arrays = lax.all_gather(wide, ("row", "col"), axis=0, axis_index_groups=order)
        for n, level in enumerate(group):
            gathered[level] = (arrays, n)

    def shared_of(level, after):
        arrays, n = gathered[level]
        shape = (owners * pair, 2, size, size)
        return call(
            f"narrow_{level}", narrow_body(n), {"gathered": arrays, "after": after},
            makes={"shared": VMEM(shape, BF16)},
            scratch={"near": VMEM(shape, F32), "sems": dma((owners * pair,))},
        )["shared"]

    sent = call(
        "send_level_0", send_body, {"residual": residual_in, "diag_inverse": diag_inverse},
        makes={"messages": messages},
        scratch={"near": VMEM(residual_in.shape, F32), "inverse": VMEM((size, size), BF16), "sems": dma((2,))},
    )["messages"]
    constants = call(
        "hold_blocks", hold_body, {"listed": column_lists.reshape(-1), **far_blocks},
        makes={
            "lists": SMEM((column_lists.size,), jnp.int32),
            "inverses": VMEM((levels, size, size), BF16),
            "lowers": VMEM((levels - 1, blocks, size, size), BF16),
        },
        scratch={"sems": dma((2,))},
        cost=pl.CostEstimate(flops=0, bytes_accessed=16 * 2**20, transcendentals=0),
    )
    received = to_all(sent)
    state = call(
        "forward_1", receive_body, {**constants, "received": received},
        makes={"source": own_rows, "finished": all_rows, "solved": rows},
    )
    source, finished, solved = state["source"], state["finished"], state["solved"]

    shared = {}
    level = 2
    accumulated = answers = products_sent = None
    while level < levels:
        arrived = exchange(solved)
        reads = {**constants, "source": source, **arrived}
        everywhere = level in shared_forward
        if everywhere:
            shared[level] = shared_of(level, solved)
            reads |= {"shared": shared[level], "received": received}
        last = level + everywhere == levels - 1

        def body(r, level=level, everywhere=everywhere, last=last):
            take_finished(r, level - 1)
            if everywhere:
                all_forward(r, level)
            answer = own_forward(r, level + everywhere)
            if last:
                r.accumulated[...] = jnp.zeros_like(r.accumulated)
                r.answers[...] = jnp.zeros_like(r.answers)
                own_products(r, levels - 1, own_backward(r, levels - 1))
            else:
                r.solved[...] = answer

        makes = {"accumulated": all_rows, "answers": own_rows, "sent": products} if last else {"solved": rows}
        state = call(f"forward_{level}", body, reads, {"finished": finished}, makes)
        finished, solved = state["finished"], state.get("solved")
        level += 1 + everywhere
    accumulated, answers, products_sent = state["accumulated"], state["answers"], state["sent"]

    level = levels - 2
    while level > 0:
        arrived = exchange(products_sent)
        reads = {**constants, "finished": finished, **arrived}
        everywhere = level in shared_levels
        if everywhere:
            if level not in shared:
                shared[level] = shared_of(level, products_sent)
            reads["shared"] = shared[level]
        last = level - everywhere == 1

        def body(r, level=level, everywhere=everywhere, last=last):
            take_products(r, level + 1)
            if everywhere:
                all_backward(r, level)
            if last:
                last_send(r)
            else:
                own = level - everywhere
                own_products(r, own, own_backward(r, own))

        state = call(
            f"backward_{level}", body, reads, {"accumulated": accumulated, "answers": answers},
            {"messages": messages} if last else {"sent": products},
            {"pieces": VMEM((owners, each, size), F32)} if last else {},
        )
        accumulated, answers, products_sent = state["accumulated"], state["answers"], state.get("sent")
        level -= 1 + everywhere
    return call(
        "backward_0", last_body,
        {"inverses": constants["inverses"], "received": to_all(state["messages"])},
        makes={"out": jax.ShapeDtypeStruct(residual_in.shape, F32)},
    )["out"]


def solution(mesh):
    placed = (
        P(None, "row", None, "col"),
        P(None, "row", None, None),
        P(None, "row", None, None, None),
        P(),
    )
    return jax.shard_map(
        shards, mesh=mesh, in_specs=placed, out_specs=P(None, "row", None, "col"), check_vma=False
    )
```

time: 182 us -> 114 us (0.63)
  blocking collectives: 117 us -> 12.6 us
  starting transfers between devices: 6.33 us -> 49.6 us
  matrix products: 38.3 us -> 0 us
  waiting for transfers between devices: 4.95 us -> 37.4 us
  Pallas kernels: 0 us -> 10.3 us
  local copies, waits for them, and re-layouts: 11.5 us -> 3.12 us
  other arithmetic: 2.43 us -> 0 us
    all_gather x14 -> x0, blocking collectives: 109 us -> none  [the longest x7 54.6 us: backward_step(): arrived = lax.all_gather(contributions[None], 'row', axis=0, tiled=True)]
    ppermute x0 -> x36, starting transfers between devices: none -> 42.3 us  [exchange(): lax.ppermute(array, 'row', [(i, i ^ mask) for i in range(owners)])]
    dot_general x37 -> x0, matrix products: 38.3 us -> none  [the longest x7 9.65 us: forward_step(): jnp.einsum('kpc,kdc->pd', pulled, factor_blocks, precision=highest)]
    ppermute x0 -> x36, waiting for transfers between devices: none -> 31.7 us  [exchange(): lax.ppermute(array, 'row', [(i, i ^ mask) for i in range(owners)])]
    pallas_call x0 -> x16, Pallas kernels: none -> 10.3 us  [call(): pl.pallas_call(kernel, in_specs=[spec(key) for key in in_names], out_spec...]
    all_to_all x1, blocking collectives: 8.12 us -> 12.6 us  [to_all(): lax.all_to_all(array, ('row', 'col'), split_axis=0, concat_axis=0, tiled=...]
    gather x7 -> x0, local copies, waits for them, and re-layouts: 3.99 us -> none  [forward_step(): finished.reshape(slot_count * owners, probe_count, block_size)[targets]]
  transfers between devices with their start and end apart: 1 -> 37, of which waited for: 1 -> 31; matrix products, arithmetic and copies ran while one was open for 0% -> 1% of each run, Pallas kernels for 0% -> 2%
where the time goes in v2:
time: 114 us; the launch traced here: 113 us
  starting transfers between devices  49.6 us (44%)
  waiting for transfers between devices  37.4 us (33%)
  blocking collectives  12.6 us (11%)
  Pallas kernels  10.3 us (9%)
  local copies, waits for them, and re-layouts  3.12 us (3%)
    ppermute x36, starting transfers between devices, exchange(): lax.ppermute(array, 'row', [(i, i ^ mask) for i in range(owners)])  42.3 us
    ppermute x36, waiting for transfers between devices, exchange(): lax.ppermute(array, 'row', [(i, i ^ mask) for i in range(owners)])  31.7 us
    all_to_all x1, blocking collectives, to_all(): lax.all_to_all(array, ('row', 'col'), split_axis=0, concat_axis=0, tiled=...  12.6 us
    pallas_call x16, Pallas kernels, call(): pl.pallas_call(kernel, in_specs=[spec(key) for key in in_names], out_spec...  10.3 us
    all_to_all x1, starting transfers between devices, to_all(): lax.all_to_all(array, ('row', 'col'), split_axis=0, concat_axis=0, tiled=...  7.3 us
    all_to_all x1, waiting for transfers between devices, to_all(): lax.all_to_all(array, ('row', 'col'), split_axis=0, concat_axis=0, tiled=...  5.74 us
    unnamed x5, local copies, waits for them, and re-layouts  3.01 us
  transfers between devices with their start and end apart: 37, of which 31 were waited for; matrix products, arithmetic and copies ran while one was open for 1% of the time, Pallas kernels for 2%

profile of v2, /device:TPU:0, one launch (start us, length us, event | category | flops | bytes accessed | tf_op | source)
XLA Modules:
  0.0 113.2 jit_solution(5345854597372825051)
XLA Ops:
  0.0 1.9 %send_level_0.1 = f32[32,8,256]{2,1,0:T(8,128)} custom-call(f32[8,1,32,32]{3,2,1,0:T(8,128)} %refs_0_.1, bf16[8,1,256,256]{3,2,1,0:T(8,128)(2,1)} %refs_1_.3), custom_call_target="tpu_custom_call" | custom-call | tf_op jit(solution)/shard_map/send_level_0/pallas_call | solution.py:90
  1.9 7.3 %all-to-all-start = ((f32[32,8,256]{2,1,0:T(8,128)}), f32[32,8,256]{2,1,0:T(8,128)S(1)}, u32[]{:S(2)}, u32[]{:S(2)}) async-start(f32[32,8,256]{2,1,0:T(8,128)} %send_level_0.1), calls=%async_computation | async-start | bytes 524288 | tf_op jit(solution)/shard_map/all_to_all | solution.py:128
  10.1 2.7 %hold_blocks.1 = (s32[84]{0:T(128)S(4)}, bf16[8,256,256]{2,1,0:T(8,128)(2,1)S(1)}, bf16[7,3,256,256]{3,2,1,0:T(8,128)(2,1)S(1)}) custom-call(s32[84]{0:T(128)S(1)} %reshape.3.refs_0_, bf16[8,1,256,256]{3,2,1,0:T(8,128)(2,1)} %refs_1_.3, bf16[7,1,3,256,256]{4,3,2,1,0:T(8,128)(2,1)} %refs_2_.1), custom_call_target="tpu_custom_call" | custom-call | bytes 16777216 | tf_op jit(solution)/shard_map/hold_blocks/pallas_call | solution.py:90
  13.9 5.7 %all-to-all-done.refs_3_ = f32[32,8,256]{2,1,0:T(8,128)S(1)} async-done(((f32[32,8,256]{2,1,0:T(8,128)}), f32[32,8,256]{2,1,0:T(8,128)S(1)}, u32[]{:S(2)}, u32[]{:S(2)}) %all-to-all-start) | async-done | bytes 262176 | tf_op jit(solution)/shard_map/all_to_all | solution.py:128
  23.2 1.5 %collective-permute-start = (f32[4,256]{1,0:T(4,128)S(1)}, f32[4,256]{1,0:T(4,128)S(1)}, u32[]{:S(2)}, u32[]{:S(2)}) collective-permute-start(f32[4,256]{1,0:T(4,128)S(1)} %get-tuple-element.45), channel_id=1, source_target_pairs={{0,8},{8,0},{16,24},{24,16},{1,9},{9,1},{17,25},{25,17},{2,10},{10... | collective-permute-start | bytes 12296 | tf_op jit(solution)/shard_map/ppermute | solution.py:123
  36.1 1.5 %collective-permute-start.6 = (f32[4,256]{1,0:T(4,128)S(1)}, f32[4,256]{1,0:T(4,128)S(1)}, u32[]{:S(2)}, u32[]{:S(2)}) collective-permute-start(f32[4,256]{1,0:T(4,128)S(1)} %get-tuple-element.49), channel_id=1, source_target_pairs={{0,8},{8,0},{16,24},{24,16},{1,9},{9,1},{17,25},{25,17},{2,10},{10... | collective-permute-start | bytes 12296 | tf_op jit(solution)/shard_map/ppermute | solution.py:123
  41.6 1.5 %collective-permute-start.10 = (f32[4,256]{1,0:T(4,128)S(1)}, f32[4,256]{1,0:T(4,128)S(1)}, u32[]{:S(2)}, u32[]{:S(2)}) collective-permute-start(f32[4,256]{1,0:T(4,128)S(1)} %get-tuple-element.51), channel_id=1, source_target_pairs={{0,16},{8,24},{16,0},{24,8},{1,17},{9,25},{17,1},{25,9},{2,18},{10... | collective-permute-start | bytes 12296 | tf_op jit(solution)/shard_map/ppermute | solution.py:123
  45.2 1.5 %collective-permute-done.9.refs_4_ = f32[4,256]{1,0:T(4,128)S(1)} collective-permute-done((f32[4,256]{1,0:T(4,128)S(1)}, f32[4,256]{1,0:T(4,128)S(1)}, u32[]{:S(2)}, u32[]{:S(2)}) %collective-permute-start.9) | collective-permute-done | bytes 4128 | tf_op jit(solution)/shard_map/ppermute | solution.py:123
  49.0 1.5 %collective-permute-start.12 = (f32[4,256]{1,0:T(4,128)S(1)}, f32[4,256]{1,0:T(4,128)S(1)}, u32[]{:S(2)}, u32[]{:S(2)}) collective-permute-start(f32[4,256]{1,0:T(4,128)S(1)} %get-tuple-element.53), channel_id=1, source_target_pairs={{0,8},{8,0},{16,24},{24,16},{1,9},{9,1},{17,25},{25,17},{2,10},{10... | collective-permute-start | bytes 12296 | tf_op jit(solution)/shard_map/ppermute | solution.py:123
  54.5 1.6 %collective-permute-start.16 = (f32[4,256]{1,0:T(4,128)S(1)}, f32[4,256]{1,0:T(4,128)S(1)}, u32[]{:S(2)}, u32[]{:S(2)}) collective-permute-start(f32[4,256]{1,0:T(4,128)S(1)} %get-tuple-element.55), channel_id=1, source_target_pairs={{0,16},{8,24},{16,0},{24,8},{1,17},{9,25},{17,1},{25,9},{2,18},{10... | collective-permute-start | bytes 12296 | tf_op jit(solution)/shard_map/ppermute | solution.py:123
  58.1 1.6 %collective-permute-done.15.refs_4_ = f32[4,256]{1,0:T(4,128)S(1)} collective-permute-done((f32[4,256]{1,0:T(4,128)S(1)}, f32[4,256]{1,0:T(4,128)S(1)}, u32[]{:S(2)}, u32[]{:S(2)}) %collective-permute-start.15) | collective-permute-done | bytes 4128 | tf_op jit(solution)/shard_map/ppermute | solution.py:123
  62.3 1.6 %collective-permute-start.18 = (f32[3,4,256]{2,1,0:T(4,128)S(1)}, f32[3,4,256]{2,1,0:T(4,128)S(1)}, u32[]{:S(2)}, u32[]{:S(2)}) collective-permute-start(f32[3,4,256]{2,1,0:T(4,128)S(1)} %get-tuple-element.58), channel_id=1, source_target_pairs={{0,8},{8,0},{16,24},{24,16},{1,9},{9,1},{17,25},{25,17},{2,10},{10... | collective-permute-start | bytes 36872 | tf_op jit(solution)/shard_map/ppermute | solution.py:123
  66.3 1.5 %collective-permute-start.23 = (f32[3,4,256]{2,1,0:T(4,128)S(1)}, f32[3,4,256]{2,1,0:T(4,128)S(1)}, u32[]{:S(2)}, u32[]{:S(2)}) collective-permute-start(f32[3,4,256]{2,1,0:T(4,128)S(1)} %get-tuple-element.61), channel_id=1, source_target_pairs={{0,24},{8,16},{16,8},{24,0},{1,25},{9,17},{17,9},{25,1},{2,26},{10... | collective-permute-start | bytes 36872 | tf_op jit(solution)/shard_map/ppermute | solution.py:123
  67.9 1.6 %collective-permute-start.22 = (f32[3,4,256]{2,1,0:T(4,128)S(1)}, f32[3,4,256]{2,1,0:T(4,128)S(1)}, u32[]{:S(2)}, u32[]{:S(2)}) collective-permute-start(f32[3,4,256]{2,1,0:T(4,128)S(1)} %get-tuple-element.61), channel_id=1, source_target_pairs={{0,16},{8,24},{16,0},{24,8},{1,17},{9,25},{17,1},{25,9},{2,18},{10... | collective-permute-start | bytes 36872 | tf_op jit(solution)/shard_map/ppermute | solution.py:123
  71.6 1.6 %collective-permute-done.21.refs_4_ = f32[3,4,256]{2,1,0:T(4,128)S(1)} collective-permute-done((f32[3,4,256]{2,1,0:T(4,128)S(1)}, f32[3,4,256]{2,1,0:T(4,128)S(1)}, u32[]{:S(2)}, u32[]{:S(2)}) %collective-permute-start.21) | collective-permute-done | bytes 12320 | tf_op jit(solution)/shard_map/ppermute | solution.py:123
  75.4 1.6 %collective-permute-start.24 = (f32[3,4,256]{2,1,0:T(4,128)S(1)}, f32[3,4,256]{2,1,0:T(4,128)S(1)}, u32[]{:S(2)}, u32[]{:S(2)}) collective-permute-start(f32[3,4,256]{2,1,0:T(4,128)S(1)} %get-tuple-element.64), channel_id=1, source_target_pairs={{0,8},{8,0},{16,24},{24,16},{1,9},{9,1},{17,25},{25,17},{2,10},{10... | collective-permute-start | bytes 36872 | tf_op jit(solution)/shard_map/ppermute | solution.py:123
  79.4 1.6 %collective-permute-start.29 = (f32[3,4,256]{2,1,0:T(4,128)S(1)}, f32[3,4,256]{2,1,0:T(4,128)S(1)}, u32[]{:S(2)}, u32[]{:S(2)}) collective-permute-start(f32[3,4,256]{2,1,0:T(4,128)S(1)} %get-tuple-element.67), channel_id=1, source_target_pairs={{0,24},{8,16},{16,8},{24,0},{1,25},{9,17},{17,9},{25,1},{2,26},{10... | collective-permute-start | bytes 36872 | tf_op jit(solution)/shard_map/ppermute | solution.py:123
  81.0 1.5 %collective-permute-start.28 = (f32[3,4,256]{2,1,0:T(4,128)S(1)}, f32[3,4,256]{2,1,0:T(4,128)S(1)}, u32[]{:S(2)}, u32[]{:S(2)}) collective-permute-start(f32[3,4,256]{2,1,0:T(4,128)S(1)} %get-tuple-element.67), channel_id=1, source_target_pairs={{0,16},{8,24},{16,0},{24,8},{1,17},{9,25},{17,1},{25,9},{2,18},{10... | collective-permute-start | bytes 36872 | tf_op jit(solution)/shard_map/ppermute | solution.py:123
  84.7 1.5 %collective-permute-done.27.refs_4_ = f32[3,4,256]{2,1,0:T(4,128)S(1)} collective-permute-done((f32[3,4,256]{2,1,0:T(4,128)S(1)}, f32[3,4,256]{2,1,0:T(4,128)S(1)}, u32[]{:S(2)}, u32[]{:S(2)}) %collective-permute-start.27) | collective-permute-done | bytes 12320 | tf_op jit(solution)/shard_map/ppermute | solution.py:123
  88.5 1.6 %collective-permute-start.30 = (f32[3,4,256]{2,1,0:T(4,128)S(1)}, f32[3,4,256]{2,1,0:T(4,128)S(1)}, u32[]{:S(2)}, u32[]{:S(2)}) collective-permute-start(f32[3,4,256]{2,1,0:T(4,128)S(1)} %get-tuple-element.70), channel_id=1, source_target_pairs={{0,8},{8,0},{16,24},{24,16},{1,9},{9,1},{17,25},{25,17},{2,10},{10... | collective-permute-start | bytes 36872 | tf_op jit(solution)/shard_map/ppermute | solution.py:123
  92.5 1.6 %collective-permute-start.35 = (f32[3,4,256]{2,1,0:T(4,128)S(1)}, f32[3,4,256]{2,1,0:T(4,128)S(1)}, u32[]{:S(2)}, u32[]{:S(2)}) collective-permute-start(f32[3,4,256]{2,1,0:T(4,128)S(1)} %get-tuple-element.73), channel_id=1, source_target_pairs={{0,24},{8,16},{16,8},{24,0},{1,25},{9,17},{17,9},{25,1},{2,26},{10... | collective-permute-start | bytes 36872 | tf_op jit(solution)/shard_map/ppermute | solution.py:123
  94.1 1.5 %collective-permute-start.34 = (f32[3,4,256]{2,1,0:T(4,128)S(1)}, f32[3,4,256]{2,1,0:T(4,128)S(1)}, u32[]{:S(2)}, u32[]{:S(2)}) collective-permute-start(f32[3,4,256]{2,1,0:T(4,128)S(1)} %get-tuple-element.73), channel_id=1, source_target_pairs={{0,16},{8,24},{16,0},{24,8},{1,17},{9,25},{17,1},{25,9},{2,18},{10... | collective-permute-start | bytes 36872 | tf_op jit(solution)/shard_map/ppermute | solution.py:123
  97.8 1.5 %collective-permute-done.33.refs_4_ = f32[3,4,256]{2,1,0:T(4,128)S(1)} collective-permute-done((f32[3,4,256]{2,1,0:T(4,128)S(1)}, f32[3,4,256]{2,1,0:T(4,128)S(1)}, u32[]{:S(2)}, u32[]{:S(2)}) %collective-permute-start.33) | collective-permute-done | bytes 12320 | tf_op jit(solution)/shard_map/ppermute | solution.py:123
  99.7 12.6 %all_to_all.10.refs_1_ = f32[32,8,256]{2,1,0:T(8,128)S(1)} all-to-all(f32[32,8,256]{2,1,0:T(8,128)S(1)} %get-tuple-element.76), channel_id=1, replica_groups=mesh['row'=4,'col'=8] {'row','col'}, dimensions={0} | all-to-all | bytes 524288 | tf_op jit(solution)/shard_map/all_to_all | solution.py:128
  (73 shorter events, 53.3 us)
Async XLA Ops:
  1.9 17.7 %all-to-all-start = ((f32[32,8,256]{2,1,0:T(8,128)}), f32[32,8,256]{2,1,0:T(8,128)S(1)}, u32[]{:S(2)}, u32[]{:S(2)}) async-start(f32[32,8,256]{2,1,0:T(8,128)} %send_level_0.1), calls=%async_computation | async-start | bytes 524288 | tf_op jit(solution)/shard_map/all_to_all | solution.py:128
  21.2 4.6 %collective-permute-start.2 = (f32[4,256]{1,0:T(4,128)S(1)}, f32[4,256]{1,0:T(4,128)S(1)}, u32[]{:S(2)}, u32[]{:S(2)}) collective-permute-start(f32[4,256]{1,0:T(4,128)S(1)} %get-tuple-element.45), channel_id=1, source_target_pairs={{0,24},{8,16},{16,8},{24,0},{1,25},{9,17},{17,9},{25,1},{2,26},{10... | collective-permute-start | bytes 12296 | tf_op jit(solution)/shard_map/ppermute | solution.py:123
  22.0 3.7 %collective-permute-start.1 = (f32[4,256]{1,0:T(4,128)S(1)}, f32[4,256]{1,0:T(4,128)S(1)}, u32[]{:S(2)}, u32[]{:S(2)}) collective-permute-start(f32[4,256]{1,0:T(4,128)S(1)} %get-tuple-element.45), channel_id=1, source_target_pairs={{0,16},{8,24},{16,0},{24,8},{1,17},{9,25},{17,1},{25,9},{2,18},{10... | collective-permute-start | bytes 12296 | tf_op jit(solution)/shard_map/ppermute | solution.py:123
  27.2 4.5 %collective-permute-start.5 = (f32[4,256]{1,0:T(4,128)S(1)}, f32[4,256]{1,0:T(4,128)S(1)}, u32[]{:S(2)}, u32[]{:S(2)}) collective-permute-start(f32[4,256]{1,0:T(4,128)S(1)} %get-tuple-element.47), channel_id=1, source_target_pairs={{0,24},{8,16},{16,8},{24,0},{1,25},{9,17},{17,9},{25,1},{2,26},{10... | collective-permute-start | bytes 12296 | tf_op jit(solution)/shard_map/ppermute | solution.py:123
  34.2 4.5 %collective-permute-start.8 = (f32[4,256]{1,0:T(4,128)S(1)}, f32[4,256]{1,0:T(4,128)S(1)}, u32[]{:S(2)}, u32[]{:S(2)}) collective-permute-start(f32[4,256]{1,0:T(4,128)S(1)} %get-tuple-element.49), channel_id=1, source_target_pairs={{0,24},{8,16},{16,8},{24,0},{1,25},{9,17},{17,9},{25,1},{2,26},{10... | collective-permute-start | bytes 12296 | tf_op jit(solution)/shard_map/ppermute | solution.py:123
  34.9 3.8 %collective-permute-start.7 = (f32[4,256]{1,0:T(4,128)S(1)}, f32[4,256]{1,0:T(4,128)S(1)}, u32[]{:S(2)}, u32[]{:S(2)}) collective-permute-start(f32[4,256]{1,0:T(4,128)S(1)} %get-tuple-element.49), channel_id=1, source_target_pairs={{0,16},{8,24},{16,0},{24,8},{1,17},{9,25},{17,1},{25,9},{2,18},{10... | collective-permute-start | bytes 12296 | tf_op jit(solution)/shard_map/ppermute | solution.py:123
  40.1 4.5 %collective-permute-start.11 = (f32[4,256]{1,0:T(4,128)S(1)}, f32[4,256]{1,0:T(4,128)S(1)}, u32[]{:S(2)}, u32[]{:S(2)}) collective-permute-start(f32[4,256]{1,0:T(4,128)S(1)} %get-tuple-element.51), channel_id=1, source_target_pairs={{0,24},{8,16},{16,8},{24,0},{1,25},{9,17},{17,9},{25,1},{2,26},{10... | collective-permute-start | bytes 12296 | tf_op jit(solution)/shard_map/ppermute | solution.py:123
  47.1 4.5 %collective-permute-start.14 = (f32[4,256]{1,0:T(4,128)S(1)}, f32[4,256]{1,0:T(4,128)S(1)}, u32[]{:S(2)}, u32[]{:S(2)}) collective-permute-start(f32[4,256]{1,0:T(4,128)S(1)} %get-tuple-element.53), channel_id=1, source_target_pairs={{0,24},{8,16},{16,8},{24,0},{1,25},{9,17},{17,9},{25,1},{2,26},{10... | collective-permute-start | bytes 12296 | tf_op jit(solution)/shard_map/ppermute | solution.py:123
  47.9 3.8 %collective-permute-start.13 = (f32[4,256]{1,0:T(4,128)S(1)}, f32[4,256]{1,0:T(4,128)S(1)}, u32[]{:S(2)}, u32[]{:S(2)}) collective-permute-start(f32[4,256]{1,0:T(4,128)S(1)} %get-tuple-element.53), channel_id=1, source_target_pairs={{0,16},{8,24},{16,0},{24,8},{1,17},{9,25},{17,1},{25,9},{2,18},{10... | collective-permute-start | bytes 12296 | tf_op jit(solution)/shard_map/ppermute | solution.py:123
  53.0 4.5 %collective-permute-start.17 = (f32[4,256]{1,0:T(4,128)S(1)}, f32[4,256]{1,0:T(4,128)S(1)}, u32[]{:S(2)}, u32[]{:S(2)}) collective-permute-start(f32[4,256]{1,0:T(4,128)S(1)} %get-tuple-element.55), channel_id=1, source_target_pairs={{0,24},{8,16},{16,8},{24,0},{1,25},{9,17},{17,9},{25,1},{2,26},{10... | collective-permute-start | bytes 12296 | tf_op jit(solution)/shard_map/ppermute | solution.py:123
  60.3 4.6 %collective-permute-start.20 = (f32[3,4,256]{2,1,0:T(4,128)S(1)}, f32[3,4,256]{2,1,0:T(4,128)S(1)}, u32[]{:S(2)}, u32[]{:S(2)}) collective-permute-start(f32[3,4,256]{2,1,0:T(4,128)S(1)} %get-tuple-element.58), channel_id=1, source_target_pairs={{0,24},{8,16},{16,8},{24,0},{1,25},{9,17},{17,9},{25,1},{2,26},{10... | collective-permute-start | bytes 36872 | tf_op jit(solution)/shard_map/ppermute | solution.py:123
  61.1 3.9 %collective-permute-start.19 = (f32[3,4,256]{2,1,0:T(4,128)S(1)}, f32[3,4,256]{2,1,0:T(4,128)S(1)}, u32[]{:S(2)}, u32[]{:S(2)}) collective-permute-start(f32[3,4,256]{2,1,0:T(4,128)S(1)} %get-tuple-element.58), channel_id=1, source_target_pairs={{0,16},{8,24},{16,0},{24,8},{1,17},{9,25},{17,1},{25,9},{2,18},{10... | collective-permute-start | bytes 36872 | tf_op jit(solution)/shard_map/ppermute | solution.py:123
  62.3 3.7 %collective-permute-start.18 = (f32[3,4,256]{2,1,0:T(4,128)S(1)}, f32[3,4,256]{2,1,0:T(4,128)S(1)}, u32[]{:S(2)}, u32[]{:S(2)}) collective-permute-start(f32[3,4,256]{2,1,0:T(4,128)S(1)} %get-tuple-element.58), channel_id=1, source_target_pairs={{0,8},{8,0},{16,24},{24,16},{1,9},{9,1},{17,25},{25,17},{2,10},{10... | collective-permute-start | bytes 36872 | tf_op jit(solution)/shard_map/ppermute | solution.py:123
  66.3 4.6 %collective-permute-start.23 = (f32[3,4,256]{2,1,0:T(4,128)S(1)}, f32[3,4,256]{2,1,0:T(4,128)S(1)}, u32[]{:S(2)}, u32[]{:S(2)}) collective-permute-start(f32[3,4,256]{2,1,0:T(4,128)S(1)} %get-tuple-element.61), channel_id=1, source_target_pairs={{0,24},{8,16},{16,8},{24,0},{1,25},{9,17},{17,9},{25,1},{2,26},{10... | collective-permute-start | bytes 36872 | tf_op jit(solution)/shard_map/ppermute | solution.py:123
  67.9 3.7 %collective-permute-start.22 = (f32[3,4,256]{2,1,0:T(4,128)S(1)}, f32[3,4,256]{2,1,0:T(4,128)S(1)}, u32[]{:S(2)}, u32[]{:S(2)}) collective-permute-start(f32[3,4,256]{2,1,0:T(4,128)S(1)} %get-tuple-element.61), channel_id=1, source_target_pairs={{0,16},{8,24},{16,0},{24,8},{1,17},{9,25},{17,1},{25,9},{2,18},{10... | collective-permute-start | bytes 36872 | tf_op jit(solution)/shard_map/ppermute | solution.py:123
  69.4 3.7 %collective-permute-start.21 = (f32[3,4,256]{2,1,0:T(4,128)S(1)}, f32[3,4,256]{2,1,0:T(4,128)S(1)}, u32[]{:S(2)}, u32[]{:S(2)}) collective-permute-start(f32[3,4,256]{2,1,0:T(4,128)S(1)} %get-tuple-element.61), channel_id=1, source_target_pairs={{0,8},{8,0},{16,24},{24,16},{1,9},{9,1},{17,25},{25,17},{2,10},{10... | collective-permute-start | bytes 36872 | tf_op jit(solution)/shard_map/ppermute | solution.py:123
  73.4 4.6 %collective-permute-start.26 = (f32[3,4,256]{2,1,0:T(4,128)S(1)}, f32[3,4,256]{2,1,0:T(4,128)S(1)}, u32[]{:S(2)}, u32[]{:S(2)}) collective-permute-start(f32[3,4,256]{2,1,0:T(4,128)S(1)} %get-tuple-element.64), channel_id=1, source_target_pairs={{0,24},{8,16},{16,8},{24,0},{1,25},{9,17},{17,9},{25,1},{2,26},{10... | collective-permute-start | bytes 36872 | tf_op jit(solution)/shard_map/ppermute | solution.py:123
  74.2 3.9 %collective-permute-start.25 = (f32[3,4,256]{2,1,0:T(4,128)S(1)}, f32[3,4,256]{2,1,0:T(4,128)S(1)}, u32[]{:S(2)}, u32[]{:S(2)}) collective-permute-start(f32[3,4,256]{2,1,0:T(4,128)S(1)} %get-tuple-element.64), channel_id=1, source_target_pairs={{0,16},{8,24},{16,0},{24,8},{1,17},{9,25},{17,1},{25,9},{2,18},{10... | collective-permute-start | bytes 36872 | tf_op jit(solution)/shard_map/ppermute | solution.py:123
  75.4 3.7 %collective-permute-start.24 = (f32[3,4,256]{2,1,0:T(4,128)S(1)}, f32[3,4,256]{2,1,0:T(4,128)S(1)}, u32[]{:S(2)}, u32[]{:S(2)}) collective-permute-start(f32[3,4,256]{2,1,0:T(4,128)S(1)} %get-tuple-element.64), channel_id=1, source_target_pairs={{0,8},{8,0},{16,24},{24,16},{1,9},{9,1},{17,25},{25,17},{2,10},{10... | collective-permute-start | bytes 36872 | tf_op jit(solution)/shard_map/ppermute | solution.py:123
  79.4 4.6 %collective-permute-start.29 = (f32[3,4,256]{2,1,0:T(4,128)S(1)}, f32[3,4,256]{2,1,0:T(4,128)S(1)}, u32[]{:S(2)}, u32[]{:S(2)}) collective-permute-start(f32[3,4,256]{2,1,0:T(4,128)S(1)} %get-tuple-element.67), channel_id=1, source_target_pairs={{0,24},{8,16},{16,8},{24,0},{1,25},{9,17},{17,9},{25,1},{2,26},{10... | collective-permute-start | bytes 36872 | tf_op jit(solution)/shard_map/ppermute | solution.py:123
  86.5 4.6 %collective-permute-start.32 = (f32[3,4,256]{2,1,0:T(4,128)S(1)}, f32[3,4,256]{2,1,0:T(4,128)S(1)}, u32[]{:S(2)}, u32[]{:S(2)}) collective-permute-start(f32[3,4,256]{2,1,0:T(4,128)S(1)} %get-tuple-element.70), channel_id=1, source_target_pairs={{0,24},{8,16},{16,8},{24,0},{1,25},{9,17},{17,9},{25,1},{2,26},{10... | collective-permute-start | bytes 36872 | tf_op jit(solution)/shard_map/ppermute | solution.py:123
  87.3 3.9 %collective-permute-start.31 = (f32[3,4,256]{2,1,0:T(4,128)S(1)}, f32[3,4,256]{2,1,0:T(4,128)S(1)}, u32[]{:S(2)}, u32[]{:S(2)}) collective-permute-start(f32[3,4,256]{2,1,0:T(4,128)S(1)} %get-tuple-element.70), channel_id=1, source_target_pairs={{0,16},{8,24},{16,0},{24,8},{1,17},{9,25},{17,1},{25,9},{2,18},{10... | collective-permute-start | bytes 36872 | tf_op jit(solution)/shard_map/ppermute | solution.py:123
  92.5 4.6 %collective-permute-start.35 = (f32[3,4,256]{2,1,0:T(4,128)S(1)}, f32[3,4,256]{2,1,0:T(4,128)S(1)}, u32[]{:S(2)}, u32[]{:S(2)}) collective-permute-start(f32[3,4,256]{2,1,0:T(4,128)S(1)} %get-tuple-element.73), channel_id=1, source_target_pairs={{0,24},{8,16},{16,8},{24,0},{1,25},{9,17},{17,9},{25,1},{2,26},{10... | collective-permute-start | bytes 36872 | tf_op jit(solution)/shard_map/ppermute | solution.py:123
  95.6 3.7 %collective-permute-start.33 = (f32[3,4,256]{2,1,0:T(4,128)S(1)}, f32[3,4,256]{2,1,0:T(4,128)S(1)}, u32[]{:S(2)}, u32[]{:S(2)}) collective-permute-start(f32[3,4,256]{2,1,0:T(4,128)S(1)} %get-tuple-element.73), channel_id=1, source_target_pairs={{0,8},{8,0},{16,24},{24,16},{1,9},{9,1},{17,25},{25,17},{2,10},{10... | collective-permute-start | bytes 36872 | tf_op jit(solution)/shard_map/ppermute | solution.py:123
  (15 other events, 49.5 us)

commit v3 on v0

v3 whole, which is shorter than its diff:
```python
import types

import jax
import jax.numpy as jnp
from jax import lax
from jax.experimental import pallas as pl
from jax.experimental.pallas import tpu as pltpu
from jax.sharding import PartitionSpec as P

VMEM = pltpu.VMEM
SMEM = pltpu.SMEM
F32 = jnp.float32
BF16 = jnp.bfloat16
CORES = 2
FAR = ("residual", "diag_inverse", "lower_blocks")


def two_parts(rows):
    high = rows.astype(BF16).astype(F32)
    return jnp.concatenate([high, rows - high], axis=0).astype(BF16)


def times(rows, block, transposed):
    contract = 1 if transposed else 0
    product = lax.dot_general(
        two_parts(rows), block, (((1,), (contract,)), ((), ())), preferred_element_type=F32
    )
    count = rows.shape[0]
    return product[:count] + product[count:]


def lane_group(shape, width):
    return lax.broadcasted_iota(jnp.int32, shape, 1) // width


def regroup(pieces, width):
    rows, size = pieces[0].shape
    groups = size // width
    stacked = jnp.concatenate(pieces, axis=0)
    rolled = [stacked if d == 0 else pltpu.roll(stacked, d * width, 1) for d in range(groups)]
    group = lane_group((rows, size), width)

    def result(b):
        total = jnp.zeros((rows, size), F32)
        for a in range(len(pieces)):
            moved = rolled[(a - b) % groups][a * rows : (a + 1) * rows]
            total = jnp.where(group == a, moved, total)
        return total

    return result


def regroup_one(pieces, width, b):
    rows, size = pieces[0].shape
    groups = size // width
    group = lane_group((rows, size), width)
    total = jnp.zeros((rows, size), F32)
    for a, piece in enumerate(pieces):
        shift = (a - b) % groups
        total = jnp.where(group == a, pltpu.roll(piece, shift * width, 1) if shift else piece, total)
    return total


def routes(count):
    order = [mask for mask in (1, 3, 2) if mask < count] + list(range(4, count))
    return [tuple(order[i : i + 2]) for i in range(0, len(order) - 1, 2)], order[-1]


def placed_in(key, array):
    if key == "listed":
        return array
    space = SMEM if key == "lists" else pltpu.HBM if key in FAR else VMEM
    return pltpu.with_memory_space_constraint(array, space)


def call(name, body, reads, updates=None, makes=None, scratch=None, cost=None):
    updates, makes, scratch = updates or {}, makes or {}, scratch or {}
    ins = {**reads, **updates}
    outs = {key: VMEM(value.shape, value.dtype) for key, value in updates.items()} | makes
    in_names, out_names, scratch_names = list(ins), list(outs), list(scratch)

    def kernel(*refs):
        space = types.SimpleNamespace()
        for key, ref in zip(in_names + out_names + scratch_names, refs, strict=True):
            setattr(space, key, ref)
        column = lax.axis_index("col")
        space.row, space.z, space.core = lax.axis_index("row"), lax.div(column, CORES), lax.rem(column, CORES)
        body(space)

    def spec(key):
        if key in ("lists", "listed"):
            return pl.BlockSpec(memory_space=SMEM)
        return pl.BlockSpec(memory_space=pltpu.HBM if key in FAR else VMEM)

    results = pl.pallas_call(
        kernel,
        in_specs=[spec(key) for key in in_names],
        out_specs=[spec(key) for key in out_names],
        out_shape=[outs[key] for key in out_names],
        input_output_aliases={in_names.index(key): out_names.index(key) for key in updates},
        scratch_shapes=list(scratch.values()),
        compiler_params=pltpu.CompilerParams(vmem_limit_bytes=24 * 2**20),
        cost_estimate=cost,
        name=name,
    )(*[placed_in(key, value) for key, value in ins.items()])
    return dict(zip(out_names, results, strict=True))


def shards(residual_in, diag_inverse, lower_blocks, column_lists):
    levels, _, probes, width = residual_in.shape
    size = diag_inverse.shape[-1]
    owners, columns = lax.axis_size("row"), lax.axis_size("col")
    layers = columns // CORES
    each = probes // layers
    blocks = column_lists.shape[2]
    rows = VMEM((each, size), F32)
    own_rows = VMEM((levels, each, size), F32)
    all_rows = VMEM((levels * owners, each, size), F32)
    packed_rows = VMEM((columns, each, size), F32)
    row_routes, layer_routes = routes(owners), routes(layers)
    dma = pltpu.SemaphoreType.DMA

    def swap(array):
        return lax.ppermute(array, "col", [(c, c ^ 1) for c in range(columns)])

    def exchange(axis, paired, single):
        pairs, last = row_routes if axis == "row" else layer_routes

        def send(array, masks):
            steps = []
            for row in range(owners):
                for column in range(columns):
                    mask = masks[column % CORES]
                    to = (row ^ mask, column) if axis == "row" else (row, column ^ (CORES * mask))
                    steps.append((row * columns + column, to[0] * columns + to[1]))
            return lax.ppermute(array, ("row", "col"), steps)

        got = {}
        for i, masks in enumerate(pairs):
            got[f"direct_{i}"] = send(paired[i], masks)
        got["single"] = send(single, (last, last))
        for i in range(len(pairs)):
            got[f"passed_{i}"] = swap(got[f"direct_{i}"])
        return got

    def partners(r, axis):
        pairs, last = row_routes if axis == "row" else layer_routes
        here = r.row if axis == "row" else r.z
        found = []
        for i, (one, other) in enumerate(pairs):
            found.append((f"direct_{i}", here ^ jnp.where(r.core == 0, one, other)))
            found.append((f"passed_{i}", here ^ jnp.where(r.core == 0, other, one)))
        return found + [("single", here ^ last)]

    def outgoing(r, axis):
        return [(f"to_{name}", to) for name, to in partners(r, axis) if not name.startswith("passed")]

    def exchanged(axis, state):
        pairs, _ = row_routes if axis == "row" else layer_routes
        return exchange(axis, [state[f"to_direct_{i}"] for i in range(len(pairs))], state["to_single"])

    def messages(axis, paired, single):
        pairs, _ = row_routes if axis == "row" else layer_routes
        return {f"to_direct_{i}": VMEM(paired, F32) for i in range(len(pairs))} | {"to_single": VMEM(single, F32)}

    def column_of(r, level, k):
        return r.lists[((level - 1) * owners + r.row) * blocks + k]

    def chip_rows(z):
        return pl.ds(pl.multiple_of(z * each, each), each)

    def pack_body(r):
        copy = pltpu.make_async_copy(r.residual, r.near, r.sems.at[0])
        copy.start()
        copy.wait()
        total = jnp.zeros((probes, size), F32)
        for level in range(levels):
            wide = jnp.concatenate([r.near[level, 0], jnp.zeros((probes, size - width), F32)], axis=1)
            total = total + (pltpu.roll(wide, level * width, 1) if level else wide)
        r.packed[...] = total

    def spread_body(r):
        for name, z in outgoing(r, "layer"):
            message = getattr(r, name)
            message[r.core] = r.packed[chip_rows(z)]
            message[1 - r.core] = r.other[chip_rows(z)]

    def hold_body(r):
        first = pltpu.make_async_copy(r.diag_inverse.at[:, 0], r.inverses, r.sems.at[0])
        second = pltpu.make_async_copy(r.lower_blocks.at[:, 0], r.lowers, r.sems.at[1])
        first.start()
        second.start()
        for i in range(r.lists.shape[0]):
            r.lists[i] = r.listed[i]
        first.wait()
        second.wait()

    def begin_body(r):
        r.pieces[CORES * r.z + r.core] = r.packed[chip_rows(r.z)]
        r.pieces[CORES * r.z + 1 - r.core] = r.other[chip_rows(r.z)]
        for name, z in partners(r, "layer"):
            for core in range(CORES):
                r.pieces[CORES * z + core] = getattr(r, name)[core]
        answer = times(regroup_one([r.pieces[c] for c in range(columns)], width, 0), r.inverses[0], True)
        r.finished[r.row] = answer
        r.solved[...] = answer

    def source_body(r):
        moved = regroup([r.pieces[c] for c in range(columns)], width)
        for level in range(1, levels):
            r.source[level] = moved(level)

    def forward_body(level):
        def body(r):
            for name, owner in partners(r, "row"):
                r.finished[(level - 1) * owners + owner] = getattr(r, name)[...]
            total = r.source[level]
            for k in range(blocks):
                total = total - times(r.finished[column_of(r, level, k)], r.lowers[level - 1, k], True)
            answer = times(total, r.inverses[level], True)
            r.finished[level * owners + r.row] = answer
            if level < levels - 1:
                r.solved[...] = answer
            else:
                r.accumulated[...] = jnp.zeros_like(r.accumulated)
                r.answers[...] = jnp.zeros_like(r.answers)
                backward(r, level, answer)

        return body

    def backward(r, level, source):
        answer = times(source, r.inverses[level], False)
        r.answers[level] = answer
        for k in range(blocks):
            r.accumulated[column_of(r, level, k)] += times(answer, r.lowers[level - 1, k], False)
        for name, owner in outgoing(r, "row"):
            getattr(r, name)[...] = r.accumulated[(level - 1) * owners + owner]

    def source_of(r, level):
        row = level * owners + r.row
        total = r.finished[row] - r.accumulated[row]
        for name, _ in partners(r, "row"):
            total = total - getattr(r, name)[...]
        return total

    def last_body(r):
        r.answers[0] = times(source_of(r, 0), r.inverses[0], False)
        moved = regroup([r.answers[level] for level in range(levels)], width)
        for column in range(columns):
            r.pieces[column] = moved(column)
        for name, z in outgoing(r, "layer"):
            if name == "to_single":
                r.to_single[...] = r.pieces[CORES * z + r.core]
            else:
                for core in range(CORES):
                    getattr(r, name)[core] = r.pieces[CORES * z + core]
        r.kept[...] = r.pieces[CORES * r.z + r.core]

    def out_body(r):
        r.whole[chip_rows(r.z)] = r.kept[...]
        for name, z in partners(r, "layer"):
            message = getattr(r, name)
            r.whole[chip_rows(z)] = message[...] if name == "single" else message[r.core]
        whole = r.whole[...]
        for level in range(levels):
            moved = pltpu.roll(whole, size - level * width, 1) if level else whole
            r.out[level, 0] = moved[:, :width]

    packed = call(
        "pack", pack_body, {"residual": residual_in}, makes={"packed": VMEM((probes, size), F32)},
        scratch={"near": VMEM(residual_in.shape, F32), "sems": dma((1,))},
    )["packed"]
    other = swap(packed)
    held = call(
        "hold_blocks", hold_body,
        {"listed": column_lists.reshape(-1), "diag_inverse": diag_inverse, "lower_blocks": lower_blocks},
        makes={
            "lists": SMEM((column_lists.size,), jnp.int32),
            "inverses": VMEM((levels, size, size), BF16),
            "lowers": VMEM((levels - 1, blocks, size, size), BF16),
        },
        scratch={"sems": dma((2,))},
        cost=pl.CostEstimate(flops=0, bytes_accessed=16 * 2**20, transcendentals=0),
    )
    both = (CORES, each, size)
    spread = call("spread", spread_body, {"packed": packed, "other": other}, makes=messages("layer", both, both))
    begun = call(
        "forward_0", begin_body,
        {"packed": packed, "other": other, "inverses": held["inverses"], **exchanged("layer", spread)},
        makes={"pieces": packed_rows, "finished": all_rows, "solved": rows},
    )
    source = call("source", source_body, {"pieces": begun["pieces"]}, makes={"source": own_rows})["source"]
    finished, solved = begun["finished"], begun["solved"]
    to_owners = messages("row", (each, size), (each, size))
    for level in range(1, levels):
        last = level == levels - 1
        state = call(
            f"forward_{level}", forward_body(level),
            {**held, "source": source, **exchange("row", [solved] * len(row_routes[0]), solved)},
            {"finished": finished},
            {"accumulated": all_rows, "answers": own_rows, **to_owners} if last else {"solved": rows},
        )
        finished, solved = state["finished"], state.get("solved")
    for level in reversed(range(1, levels - 1)):
        state = call(
            f"backward_{level}", lambda r, level=level: backward(r, level, source_of(r, level)),
            {**held, "finished": finished, **exchanged("row", state)},
            {"accumulated": state["accumulated"], "answers": state["answers"]}, to_owners,
        )
    ended = call(
        "backward_0", last_body,
        {
            "inverses": held["inverses"], "finished": finished, "accumulated": state["accumulated"],
            **exchanged("row", state),
        },
        {"answers": state["answers"]},
        {"kept": rows, **messages("layer", both, (each, size))},
        {"pieces": packed_rows},
    )
    return call(
        "out", out_body, {"kept": ended["kept"], **exchanged("layer", ended)},
        makes={"out": jax.ShapeDtypeStruct(residual_in.shape, F32)},
        scratch={"whole": VMEM((probes, size), F32)},
    )["out"]


def solution(mesh):
    placed = (
        P(None, "row", None, "col"),
        P(None, "row", None, None),
        P(None, "row", None, None, None),
        P(),
    )
    return jax.shard_map(
        shards, mesh=mesh, in_specs=placed, out_specs=P(None, "row", None, "col"), check_vma=False
    )
```

time: 182 us -> 95.7 us (0.53)
  blocking collectives: 117 us -> 0 us
  starting transfers between devices: 6.33 us -> 47.7 us
  matrix products: 38.3 us -> 0 us
  waiting for transfers between devices: 4.95 us -> 37.3 us
  local copies, waits for them, and re-layouts: 11.5 us -> 0.9 us
  Pallas kernels: 0 us -> 9.52 us
  other arithmetic: 2.43 us -> 0 us
    all_gather x14 -> x0, blocking collectives: 109 us -> none  [the longest x7 54.6 us: backward_step(): arrived = lax.all_gather(contributions[None], 'row', axis=0, tiled=True)]
    ppermute x0 -> x49, starting transfers between devices: none -> 47.7 us  [the longest x32 45.7 us: send(): return lax.ppermute(array, ('row', 'col'), steps)]
    dot_general x37 -> x0, matrix products: 38.3 us -> none  [the longest x7 9.65 us: forward_step(): jnp.einsum('kpc,kdc->pd', pulled, factor_blocks, precision=highest)]
    ppermute x0 -> x49, waiting for transfers between devices: none -> 37.3 us  [the longest x32 36.4 us: send(): return lax.ppermute(array, ('row', 'col'), steps)]
    pallas_call x0 -> x20, Pallas kernels: none -> 9.52 us  [call(): pl.pallas_call(kernel, in_specs=[spec(key) for key in in_names], out_spec...]
    all_to_all x1 -> x0, blocking collectives: 8.12 us -> none  [shards(): lax.all_to_all(backward[:, None], 'col', split_axis=3, concat_axis=2, til...]
    all_to_all x1 -> x0, starting transfers between devices: 6.33 us -> none  [shards(): lax.all_to_all(residual_in, 'col', split_axis=2, concat_axis=3, tiled=True)]
    all_to_all x1 -> x0, waiting for transfers between devices: 4.95 us -> none  [shards(): lax.all_to_all(residual_in, 'col', split_axis=2, concat_axis=3, tiled=True)]
  transfers between devices with their start and end apart: 1 -> 49, of which waited for: 1 -> 31; matrix products, arithmetic and copies ran while one was open for 0% -> 1% of each run, Pallas kernels for 0% -> 3%
where the time goes in v3:
time: 95.7 us; the launch traced here: 95.6 us
  starting transfers between devices  47.7 us (50%)
  waiting for transfers between devices  37.3 us (39%)
  Pallas kernels  9.52 us (10%)
    ppermute x32, starting transfers between devices, send(): return lax.ppermute(array, ('row', 'col'), steps)  45.7 us
    ppermute x32, waiting for transfers between devices, send(): return lax.ppermute(array, ('row', 'col'), steps)  36.4 us
    pallas_call x20, Pallas kernels, call(): pl.pallas_call(kernel, in_specs=[spec(key) for key in in_names], out_spec...  9.52 us
    ppermute x17, starting transfers between devices, swap(): return lax.ppermute(array, 'col', [(c, c ^ 1) for c in range(columns)])  2.02 us
  transfers between devices with their start and end apart: 49, of which 31 were waited for; matrix products, arithmetic and copies ran while one was open for 1% of the time, Pallas kernels for 3%

profile of v3, /device:TPU:0, one launch (start us, length us, event | category | flops | bytes accessed | tf_op | source)
XLA Modules:
  0.0 95.6 jit_solution(6067251353419302973)
XLA Ops:
  2.4 2.9 %collective-permute-start.1 = (f32[2,8,256]{2,1,0:T(8,128)S(1)}, f32[2,8,256]{2,1,0:T(8,128)S(1)}, u32[]{:S(2)}, u32[]{:S(2)}) collective-permute-start(f32[2,8,256]{2,1,0:T(8,128)S(1)} %get-tuple-element.60), channel_id=1, source_target_pairs={{0,2},{1,7},{2,0},{3,5},{4,6},{5,3},{6,4},{7,1},{8,10},{9,15},{10,... | collective-permute-start | bytes 49160 | tf_op jit(solution)/shard_map/ppermute | solution.py:136
  5.3 2.6 %collective-permute-start.2 = (f32[2,8,256]{2,1,0:T(8,128)S(1)}, f32[2,8,256]{2,1,0:T(8,128)S(1)}, u32[]{:S(2)}, u32[]{:S(2)}) collective-permute-start(f32[2,8,256]{2,1,0:T(8,128)S(1)} %get-tuple-element.61), channel_id=1, source_target_pairs={{0,4},{1,5},{2,6},{3,7},{4,0},{5,1},{6,2},{7,3},{8,12},{9,13},{10,... | collective-permute-start | bytes 49160 | tf_op jit(solution)/shard_map/ppermute | solution.py:136
  9.3 2.7 %hold_blocks.1 = (s32[84]{0:T(128)S(4)}, bf16[8,256,256]{2,1,0:T(8,128)(2,1)S(1)}, bf16[7,3,256,256]{3,2,1,0:T(8,128)(2,1)S(1)}) custom-call(s32[84]{0:T(128)S(1)} %reshape.3.refs_0_, bf16[8,1,256,256]{3,2,1,0:T(8,128)(2,1)} %refs_1_.1, bf16[7,1,3,256,256]{4,3,2,1,0:T(8,128)(2,1)} %refs_2_.1), custom_call_target="tpu_custom_call" | custom-call | bytes 16777216 | tf_op jit(solution)/shard_map/hold_blocks/pallas_call | solution.py:95
  12.2 1.5 %collective-permute-start.4 = (f32[8,256]{1,0:T(8,128)S(1)}, f32[8,256]{1,0:T(8,128)S(1)}, u32[]{:S(2)}, u32[]{:S(2)}) collective-permute-start(f32[8,256]{1,0:T(8,128)S(1)} %get-tuple-element.63), channel_id=1, source_target_pairs={{0,8},{1,25},{2,10},{3,27},{4,12},{5,29},{6,14},{7,31},{8,0},{9,17... | collective-permute-start | bytes 24584 | tf_op jit(solution)/shard_map/ppermute | solution.py:136
  13.7 1.5 %collective-permute-start.5 = (f32[8,256]{1,0:T(8,128)S(1)}, f32[8,256]{1,0:T(8,128)S(1)}, u32[]{:S(2)}, u32[]{:S(2)}) collective-permute-start(f32[8,256]{1,0:T(8,128)S(1)} %get-tuple-element.63), channel_id=1, source_target_pairs={{0,16},{1,17},{2,18},{3,19},{4,20},{5,21},{6,22},{7,23},{8,24},{9,... | collective-permute-start | bytes 24584 | tf_op jit(solution)/shard_map/ppermute | solution.py:136
  16.0 1.3 %collective-permute-done.5.refs_5_ = f32[8,256]{1,0:T(8,128)S(1)} collective-permute-done((f32[8,256]{1,0:T(8,128)S(1)}, f32[8,256]{1,0:T(8,128)S(1)}, u32[]{:S(2)}, u32[]{:S(2)}) %collective-permute-start.5) | collective-permute-done | bytes 8224 | tf_op jit(solution)/shard_map/ppermute | solution.py:136
  18.9 1.5 %collective-permute-start.8 = (f32[8,256]{1,0:T(8,128)S(1)}, f32[8,256]{1,0:T(8,128)S(1)}, u32[]{:S(2)}, u32[]{:S(2)}) collective-permute-start(f32[8,256]{1,0:T(8,128)S(1)} %get-tuple-element.65), channel_id=1, source_target_pairs={{0,16},{1,17},{2,18},{3,19},{4,20},{5,21},{6,22},{7,23},{8,24},{9,... | collective-permute-start | bytes 24584 | tf_op jit(solution)/shard_map/ppermute | solution.py:136
  24.1 1.5 %collective-permute-start.11 = (f32[8,256]{1,0:T(8,128)S(1)}, f32[8,256]{1,0:T(8,128)S(1)}, u32[]{:S(2)}, u32[]{:S(2)}) collective-permute-start(f32[8,256]{1,0:T(8,128)S(1)} %get-tuple-element.67), channel_id=1, source_target_pairs={{0,16},{1,17},{2,18},{3,19},{4,20},{5,21},{6,22},{7,23},{8,24},{9,... | collective-permute-start | bytes 24584 | tf_op jit(solution)/shard_map/ppermute | solution.py:136
  29.3 1.5 %collective-permute-start.14 = (f32[8,256]{1,0:T(8,128)S(1)}, f32[8,256]{1,0:T(8,128)S(1)}, u32[]{:S(2)}, u32[]{:S(2)}) collective-permute-start(f32[8,256]{1,0:T(8,128)S(1)} %get-tuple-element.69), channel_id=1, source_target_pairs={{0,16},{1,17},{2,18},{3,19},{4,20},{5,21},{6,22},{7,23},{8,24},{9,... | collective-permute-start | bytes 24584 | tf_op jit(solution)/shard_map/ppermute | solution.py:136
  34.5 1.5 %collective-permute-start.17 = (f32[8,256]{1,0:T(8,128)S(1)}, f32[8,256]{1,0:T(8,128)S(1)}, u32[]{:S(2)}, u32[]{:S(2)}) collective-permute-start(f32[8,256]{1,0:T(8,128)S(1)} %get-tuple-element.71), channel_id=1, source_target_pairs={{0,16},{1,17},{2,18},{3,19},{4,20},{5,21},{6,22},{7,23},{8,24},{9,... | collective-permute-start | bytes 24584 | tf_op jit(solution)/shard_map/ppermute | solution.py:136
  39.7 1.5 %collective-permute-start.20 = (f32[8,256]{1,0:T(8,128)S(1)}, f32[8,256]{1,0:T(8,128)S(1)}, u32[]{:S(2)}, u32[]{:S(2)}) collective-permute-start(f32[8,256]{1,0:T(8,128)S(1)} %get-tuple-element.73), channel_id=1, source_target_pairs={{0,16},{1,17},{2,18},{3,19},{4,20},{5,21},{6,22},{7,23},{8,24},{9,... | collective-permute-start | bytes 24584 | tf_op jit(solution)/shard_map/ppermute | solution.py:136
  44.9 1.5 %collective-permute-start.23 = (f32[8,256]{1,0:T(8,128)S(1)}, f32[8,256]{1,0:T(8,128)S(1)}, u32[]{:S(2)}, u32[]{:S(2)}) collective-permute-start(f32[8,256]{1,0:T(8,128)S(1)} %get-tuple-element.75), channel_id=1, source_target_pairs={{0,16},{1,17},{2,18},{3,19},{4,20},{5,21},{6,22},{7,23},{8,24},{9,... | collective-permute-start | bytes 24584 | tf_op jit(solution)/shard_map/ppermute | solution.py:136
  49.2 1.2 %collective-permute-start.25 = (f32[8,256]{1,0:T(8,128)S(1)}, f32[8,256]{1,0:T(8,128)S(1)}, u32[]{:S(2)}, u32[]{:S(2)}) collective-permute-start(f32[8,256]{1,0:T(8,128)S(1)} %get-tuple-element.78), channel_id=1, source_target_pairs={{0,8},{1,25},{2,10},{3,27},{4,12},{5,29},{6,14},{7,31},{8,0},{9,17... | collective-permute-start | bytes 24584 | tf_op jit(solution)/shard_map/ppermute | solution.py:136
  50.4 1.5 %collective-permute-start.26 = (f32[8,256]{1,0:T(8,128)S(1)}, f32[8,256]{1,0:T(8,128)S(1)}, u32[]{:S(2)}, u32[]{:S(2)}) collective-permute-start(f32[8,256]{1,0:T(8,128)S(1)} %get-tuple-element.79), channel_id=1, source_target_pairs={{0,16},{1,17},{2,18},{3,19},{4,20},{5,21},{6,22},{7,23},{8,24},{9,... | collective-permute-start | bytes 24584 | tf_op jit(solution)/shard_map/ppermute | solution.py:136
  54.4 1.2 %collective-permute-start.28 = (f32[8,256]{1,0:T(8,128)S(1)}, f32[8,256]{1,0:T(8,128)S(1)}, u32[]{:S(2)}, u32[]{:S(2)}) collective-permute-start(f32[8,256]{1,0:T(8,128)S(1)} %get-tuple-element.82), channel_id=1, source_target_pairs={{0,8},{1,25},{2,10},{3,27},{4,12},{5,29},{6,14},{7,31},{8,0},{9,17... | collective-permute-start | bytes 24584 | tf_op jit(solution)/shard_map/ppermute | solution.py:136
  55.6 1.5 %collective-permute-start.29 = (f32[8,256]{1,0:T(8,128)S(1)}, f32[8,256]{1,0:T(8,128)S(1)}, u32[]{:S(2)}, u32[]{:S(2)}) collective-permute-start(f32[8,256]{1,0:T(8,128)S(1)} %get-tuple-element.83), channel_id=1, source_target_pairs={{0,16},{1,17},{2,18},{3,19},{4,20},{5,21},{6,22},{7,23},{8,24},{9,... | collective-permute-start | bytes 24584 | tf_op jit(solution)/shard_map/ppermute | solution.py:136
  60.8 1.5 %collective-permute-start.32 = (f32[8,256]{1,0:T(8,128)S(1)}, f32[8,256]{1,0:T(8,128)S(1)}, u32[]{:S(2)}, u32[]{:S(2)}) collective-permute-start(f32[8,256]{1,0:T(8,128)S(1)} %get-tuple-element.87), channel_id=1, source_target_pairs={{0,16},{1,17},{2,18},{3,19},{4,20},{5,21},{6,22},{7,23},{8,24},{9,... | collective-permute-start | bytes 24584 | tf_op jit(solution)/shard_map/ppermute | solution.py:136
  66.0 1.5 %collective-permute-start.35 = (f32[8,256]{1,0:T(8,128)S(1)}, f32[8,256]{1,0:T(8,128)S(1)}, u32[]{:S(2)}, u32[]{:S(2)}) collective-permute-start(f32[8,256]{1,0:T(8,128)S(1)} %get-tuple-element.91), channel_id=1, source_target_pairs={{0,16},{1,17},{2,18},{3,19},{4,20},{5,21},{6,22},{7,23},{8,24},{9,... | collective-permute-start | bytes 24584 | tf_op jit(solution)/shard_map/ppermute | solution.py:136
  71.1 1.5 %collective-permute-start.38 = (f32[8,256]{1,0:T(8,128)S(1)}, f32[8,256]{1,0:T(8,128)S(1)}, u32[]{:S(2)}, u32[]{:S(2)}) collective-permute-start(f32[8,256]{1,0:T(8,128)S(1)} %get-tuple-element.95), channel_id=1, source_target_pairs={{0,16},{1,17},{2,18},{3,19},{4,20},{5,21},{6,22},{7,23},{8,24},{9,... | collective-permute-start | bytes 24584 | tf_op jit(solution)/shard_map/ppermute | solution.py:136
  76.3 1.5 %collective-permute-start.41 = (f32[8,256]{1,0:T(8,128)S(1)}, f32[8,256]{1,0:T(8,128)S(1)}, u32[]{:S(2)}, u32[]{:S(2)}) collective-permute-start(f32[8,256]{1,0:T(8,128)S(1)} %get-tuple-element.99), channel_id=1, source_target_pairs={{0,16},{1,17},{2,18},{3,19},{4,20},{5,21},{6,22},{7,23},{8,24},{9,... | collective-permute-start | bytes 24584 | tf_op jit(solution)/shard_map/ppermute | solution.py:136
  81.5 1.5 %collective-permute-start.44 = (f32[8,256]{1,0:T(8,128)S(1)}, f32[8,256]{1,0:T(8,128)S(1)}, u32[]{:S(2)}, u32[]{:S(2)}) collective-permute-start(f32[8,256]{1,0:T(8,128)S(1)} %get-tuple-element.104), channel_id=1, source_target_pairs={{0,16},{1,17},{2,18},{3,19},{4,20},{5,21},{6,22},{7,23},{8,24},{9,... | collective-permute-start | bytes 24584 | tf_op jit(solution)/shard_map/ppermute | solution.py:136
  86.2 3.0 %collective-permute-done.46.refs_1_ = f32[2,8,256]{2,1,0:T(8,128)S(1)} collective-permute-done((f32[2,8,256]{2,1,0:T(8,128)S(1)}, f32[2,8,256]{2,1,0:T(8,128)S(1)}, u32[]{:S(2)}, u32[]{:S(2)}) %collective-permute-start.46) | collective-permute-done | bytes 16416 | tf_op jit(solution)/shard_map/ppermute | solution.py:136
  90.2 1.3 %collective-permute-start.47 = (f32[8,256]{1,0:T(8,128)S(1)}, f32[8,256]{1,0:T(8,128)S(1)}, u32[]{:S(2)}, u32[]{:S(2)}) collective-permute-start(f32[8,256]{1,0:T(8,128)S(1)} %get-tuple-element.108), channel_id=1, source_target_pairs={{0,4},{1,5},{2,6},{3,7},{4,0},{5,1},{6,2},{7,3},{8,12},{9,13},{10,... | collective-permute-start | bytes 24584 | tf_op jit(solution)/shard_map/ppermute | solution.py:136
  91.5 3.3 %collective-permute-done.47.refs_2_ = f32[8,256]{1,0:T(8,128)S(1)} collective-permute-done((f32[8,256]{1,0:T(8,128)S(1)}, f32[8,256]{1,0:T(8,128)S(1)}, u32[]{:S(2)}, u32[]{:S(2)}) %collective-permute-start.47) | collective-permute-done | bytes 8224 | tf_op jit(solution)/shard_map/ppermute | solution.py:136
  (96 shorter events, 53.5 us)
Async XLA Ops:
  2.4 5.5 %collective-permute-start.1 = (f32[2,8,256]{2,1,0:T(8,128)S(1)}, f32[2,8,256]{2,1,0:T(8,128)S(1)}, u32[]{:S(2)}, u32[]{:S(2)}) collective-permute-start(f32[2,8,256]{2,1,0:T(8,128)S(1)} %get-tuple-element.60), channel_id=1, source_target_pairs={{0,2},{1,7},{2,0},{3,5},{4,6},{5,3},{6,4},{7,1},{8,10},{9,15},{10,... | collective-permute-start | bytes 49160 | tf_op jit(solution)/shard_map/ppermute | solution.py:136
  5.3 6.6 %collective-permute-start.2 = (f32[2,8,256]{2,1,0:T(8,128)S(1)}, f32[2,8,256]{2,1,0:T(8,128)S(1)}, u32[]{:S(2)}, u32[]{:S(2)}) collective-permute-start(f32[2,8,256]{2,1,0:T(8,128)S(1)} %get-tuple-element.61), channel_id=1, source_target_pairs={{0,4},{1,5},{2,6},{3,7},{4,0},{5,1},{6,2},{7,3},{8,12},{9,13},{10,... | collective-permute-start | bytes 49160 | tf_op jit(solution)/shard_map/ppermute | solution.py:136
  7.9 4.0 %collective-permute-start.3 = (f32[2,8,256]{2,1,0:T(8,128)S(1)}, f32[2,8,256]{2,1,0:T(8,128)S(1)}, u32[]{:S(2)}, u32[]{:S(2)}) collective-permute-start(f32[2,8,256]{2,1,0:T(8,128)S(1)} %collective-permute-done.1.refs_3_), channel_id=1, source_target_pairs={{0,1},{1,0},{2,3},{3,2},{4,5},{5,4},{6,7},{7,6},{8,9},{9,8},{10,11... | collective-permute-start | bytes 49160 | tf_op jit(solution)/shard_map/ppermute | solution.py:124
  12.2 3.7 %collective-permute-start.4 = (f32[8,256]{1,0:T(8,128)S(1)}, f32[8,256]{1,0:T(8,128)S(1)}, u32[]{:S(2)}, u32[]{:S(2)}) collective-permute-start(f32[8,256]{1,0:T(8,128)S(1)} %get-tuple-element.63), channel_id=1, source_target_pairs={{0,8},{1,25},{2,10},{3,27},{4,12},{5,29},{6,14},{7,31},{8,0},{9,17... | collective-permute-start | bytes 24584 | tf_op jit(solution)/shard_map/ppermute | solution.py:136
  13.7 3.7 %collective-permute-start.5 = (f32[8,256]{1,0:T(8,128)S(1)}, f32[8,256]{1,0:T(8,128)S(1)}, u32[]{:S(2)}, u32[]{:S(2)}) collective-permute-start(f32[8,256]{1,0:T(8,128)S(1)} %get-tuple-element.63), channel_id=1, source_target_pairs={{0,16},{1,17},{2,18},{3,19},{4,20},{5,21},{6,22},{7,23},{8,24},{9,... | collective-permute-start | bytes 24584 | tf_op jit(solution)/shard_map/ppermute | solution.py:136
  17.7 3.7 %collective-permute-start.7 = (f32[8,256]{1,0:T(8,128)S(1)}, f32[8,256]{1,0:T(8,128)S(1)}, u32[]{:S(2)}, u32[]{:S(2)}) collective-permute-start(f32[8,256]{1,0:T(8,128)S(1)} %get-tuple-element.65), channel_id=1, source_target_pairs={{0,8},{1,25},{2,10},{3,27},{4,12},{5,29},{6,14},{7,31},{8,0},{9,17... | collective-permute-start | bytes 24584 | tf_op jit(solution)/shard_map/ppermute | solution.py:136
  22.9 3.7 %collective-permute-start.10 = (f32[8,256]{1,0:T(8,128)S(1)}, f32[8,256]{1,0:T(8,128)S(1)}, u32[]{:S(2)}, u32[]{:S(2)}) collective-permute-start(f32[8,256]{1,0:T(8,128)S(1)} %get-tuple-element.67), channel_id=1, source_target_pairs={{0,8},{1,25},{2,10},{3,27},{4,12},{5,29},{6,14},{7,31},{8,0},{9,17... | collective-permute-start | bytes 24584 | tf_op jit(solution)/shard_map/ppermute | solution.py:136
  28.1 3.7 %collective-permute-start.13 = (f32[8,256]{1,0:T(8,128)S(1)}, f32[8,256]{1,0:T(8,128)S(1)}, u32[]{:S(2)}, u32[]{:S(2)}) collective-permute-start(f32[8,256]{1,0:T(8,128)S(1)} %get-tuple-element.69), channel_id=1, source_target_pairs={{0,8},{1,25},{2,10},{3,27},{4,12},{5,29},{6,14},{7,31},{8,0},{9,17... | collective-permute-start | bytes 24584 | tf_op jit(solution)/shard_map/ppermute | solution.py:136
  33.3 3.7 %collective-permute-start.16 = (f32[8,256]{1,0:T(8,128)S(1)}, f32[8,256]{1,0:T(8,128)S(1)}, u32[]{:S(2)}, u32[]{:S(2)}) collective-permute-start(f32[8,256]{1,0:T(8,128)S(1)} %get-tuple-element.71), channel_id=1, source_target_pairs={{0,8},{1,25},{2,10},{3,27},{4,12},{5,29},{6,14},{7,31},{8,0},{9,17... | collective-permute-start | bytes 24584 | tf_op jit(solution)/shard_map/ppermute | solution.py:136
  38.5 3.7 %collective-permute-start.19 = (f32[8,256]{1,0:T(8,128)S(1)}, f32[8,256]{1,0:T(8,128)S(1)}, u32[]{:S(2)}, u32[]{:S(2)}) collective-permute-start(f32[8,256]{1,0:T(8,128)S(1)} %get-tuple-element.73), channel_id=1, source_target_pairs={{0,8},{1,25},{2,10},{3,27},{4,12},{5,29},{6,14},{7,31},{8,0},{9,17... | collective-permute-start | bytes 24584 | tf_op jit(solution)/shard_map/ppermute | solution.py:136
  43.7 3.7 %collective-permute-start.22 = (f32[8,256]{1,0:T(8,128)S(1)}, f32[8,256]{1,0:T(8,128)S(1)}, u32[]{:S(2)}, u32[]{:S(2)}) collective-permute-start(f32[8,256]{1,0:T(8,128)S(1)} %get-tuple-element.75), channel_id=1, source_target_pairs={{0,8},{1,25},{2,10},{3,27},{4,12},{5,29},{6,14},{7,31},{8,0},{9,17... | collective-permute-start | bytes 24584 | tf_op jit(solution)/shard_map/ppermute | solution.py:136
  49.2 3.7 %collective-permute-start.25 = (f32[8,256]{1,0:T(8,128)S(1)}, f32[8,256]{1,0:T(8,128)S(1)}, u32[]{:S(2)}, u32[]{:S(2)}) collective-permute-start(f32[8,256]{1,0:T(8,128)S(1)} %get-tuple-element.78), channel_id=1, source_target_pairs={{0,8},{1,25},{2,10},{3,27},{4,12},{5,29},{6,14},{7,31},{8,0},{9,17... | collective-permute-start | bytes 24584 | tf_op jit(solution)/shard_map/ppermute | solution.py:136
  54.4 3.7 %collective-permute-start.28 = (f32[8,256]{1,0:T(8,128)S(1)}, f32[8,256]{1,0:T(8,128)S(1)}, u32[]{:S(2)}, u32[]{:S(2)}) collective-permute-start(f32[8,256]{1,0:T(8,128)S(1)} %get-tuple-element.82), channel_id=1, source_target_pairs={{0,8},{1,25},{2,10},{3,27},{4,12},{5,29},{6,14},{7,31},{8,0},{9,17... | collective-permute-start | bytes 24584 | tf_op jit(solution)/shard_map/ppermute | solution.py:136
  59.6 3.7 %collective-permute-start.31 = (f32[8,256]{1,0:T(8,128)S(1)}, f32[8,256]{1,0:T(8,128)S(1)}, u32[]{:S(2)}, u32[]{:S(2)}) collective-permute-start(f32[8,256]{1,0:T(8,128)S(1)} %get-tuple-element.86), channel_id=1, source_target_pairs={{0,8},{1,25},{2,10},{3,27},{4,12},{5,29},{6,14},{7,31},{8,0},{9,17... | collective-permute-start | bytes 24584 | tf_op jit(solution)/shard_map/ppermute | solution.py:136
  60.8 3.7 %collective-permute-start.32 = (f32[8,256]{1,0:T(8,128)S(1)}, f32[8,256]{1,0:T(8,128)S(1)}, u32[]{:S(2)}, u32[]{:S(2)}) collective-permute-start(f32[8,256]{1,0:T(8,128)S(1)} %get-tuple-element.87), channel_id=1, source_target_pairs={{0,16},{1,17},{2,18},{3,19},{4,20},{5,21},{6,22},{7,23},{8,24},{9,... | collective-permute-start | bytes 24584 | tf_op jit(solution)/shard_map/ppermute | solution.py:136
  64.7 3.7 %collective-permute-start.34 = (f32[8,256]{1,0:T(8,128)S(1)}, f32[8,256]{1,0:T(8,128)S(1)}, u32[]{:S(2)}, u32[]{:S(2)}) collective-permute-start(f32[8,256]{1,0:T(8,128)S(1)} %get-tuple-element.90), channel_id=1, source_target_pairs={{0,8},{1,25},{2,10},{3,27},{4,12},{5,29},{6,14},{7,31},{8,0},{9,17... | collective-permute-start | bytes 24584 | tf_op jit(solution)/shard_map/ppermute | solution.py:136
  66.0 3.7 %collective-permute-start.35 = (f32[8,256]{1,0:T(8,128)S(1)}, f32[8,256]{1,0:T(8,128)S(1)}, u32[]{:S(2)}, u32[]{:S(2)}) collective-permute-start(f32[8,256]{1,0:T(8,128)S(1)} %get-tuple-element.91), channel_id=1, source_target_pairs={{0,16},{1,17},{2,18},{3,19},{4,20},{5,21},{6,22},{7,23},{8,24},{9,... | collective-permute-start | bytes 24584 | tf_op jit(solution)/shard_map/ppermute | solution.py:136
  69.9 3.7 %collective-permute-start.37 = (f32[8,256]{1,0:T(8,128)S(1)}, f32[8,256]{1,0:T(8,128)S(1)}, u32[]{:S(2)}, u32[]{:S(2)}) collective-permute-start(f32[8,256]{1,0:T(8,128)S(1)} %get-tuple-element.94), channel_id=1, source_target_pairs={{0,8},{1,25},{2,10},{3,27},{4,12},{5,29},{6,14},{7,31},{8,0},{9,17... | collective-permute-start | bytes 24584 | tf_op jit(solution)/shard_map/ppermute | solution.py:136
  71.1 3.7 %collective-permute-start.38 = (f32[8,256]{1,0:T(8,128)S(1)}, f32[8,256]{1,0:T(8,128)S(1)}, u32[]{:S(2)}, u32[]{:S(2)}) collective-permute-start(f32[8,256]{1,0:T(8,128)S(1)} %get-tuple-element.95), channel_id=1, source_target_pairs={{0,16},{1,17},{2,18},{3,19},{4,20},{5,21},{6,22},{7,23},{8,24},{9,... | collective-permute-start | bytes 24584 | tf_op jit(solution)/shard_map/ppermute | solution.py:136
  75.1 3.7 %collective-permute-start.40 = (f32[8,256]{1,0:T(8,128)S(1)}, f32[8,256]{1,0:T(8,128)S(1)}, u32[]{:S(2)}, u32[]{:S(2)}) collective-permute-start(f32[8,256]{1,0:T(8,128)S(1)} %get-tuple-element.98), channel_id=1, source_target_pairs={{0,8},{1,25},{2,10},{3,27},{4,12},{5,29},{6,14},{7,31},{8,0},{9,17... | collective-permute-start | bytes 24584 | tf_op jit(solution)/shard_map/ppermute | solution.py:136
  80.3 3.7 %collective-permute-start.43 = (f32[8,256]{1,0:T(8,128)S(1)}, f32[8,256]{1,0:T(8,128)S(1)}, u32[]{:S(2)}, u32[]{:S(2)}) collective-permute-start(f32[8,256]{1,0:T(8,128)S(1)} %get-tuple-element.103), channel_id=1, source_target_pairs={{0,8},{1,25},{2,10},{3,27},{4,12},{5,29},{6,14},{7,31},{8,0},{9,17... | collective-permute-start | bytes 24584 | tf_op jit(solution)/shard_map/ppermute | solution.py:136
  85.4 3.8 %collective-permute-start.46 = (f32[2,8,256]{2,1,0:T(8,128)S(1)}, f32[2,8,256]{2,1,0:T(8,128)S(1)}, u32[]{:S(2)}, u32[]{:S(2)}) collective-permute-start(f32[2,8,256]{2,1,0:T(8,128)S(1)} %get-tuple-element.107), channel_id=1, source_target_pairs={{0,2},{1,7},{2,0},{3,5},{4,6},{5,3},{6,4},{7,1},{8,10},{9,15},{10,... | collective-permute-start | bytes 49160 | tf_op jit(solution)/shard_map/ppermute | solution.py:136
  89.2 5.6 %collective-permute-start.48 = (f32[2,8,256]{2,1,0:T(8,128)S(1)}, f32[2,8,256]{2,1,0:T(8,128)S(1)}, u32[]{:S(2)}, u32[]{:S(2)}) collective-permute-start(f32[2,8,256]{2,1,0:T(8,128)S(1)} %collective-permute-done.46.refs_1_), channel_id=1, source_target_pairs={{0,1},{1,0},{2,3},{3,2},{4,5},{5,4},{6,7},{7,6},{8,9},{9,8},{10,11... | collective-permute-start | bytes 49160 | tf_op jit(solution)/shard_map/ppermute | solution.py:124
  90.2 4.6 %collective-permute-start.47 = (f32[8,256]{1,0:T(8,128)S(1)}, f32[8,256]{1,0:T(8,128)S(1)}, u32[]{:S(2)}, u32[]{:S(2)}) collective-permute-start(f32[8,256]{1,0:T(8,128)S(1)} %get-tuple-element.108), channel_id=1, source_target_pairs={{0,4},{1,5},{2,6},{3,7},{4,0},{5,1},{6,2},{7,3},{8,12},{9,13},{10,... | collective-permute-start | bytes 24584 | tf_op jit(solution)/shard_map/ppermute | solution.py:136
  (25 other events, 54.6 us)

commit v4 on v3

--- a/solution.py
+++ b/solution.py
@@ -12,7 +12,7 @@
 F32 = jnp.float32
 BF16 = jnp.bfloat16
 CORES = 2
-FAR = ("residual", "diag_inverse", "lower_blocks")
+FAR = ("residual", "diag_inverse", "lower_blocks", "listed")
 
 
 def two_parts(rows):
@@ -67,8 +67,6 @@
 
 
 def placed_in(key, array):
-    if key == "listed":
-        return array
     space = SMEM if key == "lists" else pltpu.HBM if key in FAR else VMEM
     return pltpu.with_memory_space_constraint(array, space)
 
@@ -169,31 +167,57 @@
     def chip_rows(z):
         return pl.ds(pl.multiple_of(z * each, each), each)
 
+    def packed(residual):
+        total = jnp.zeros((probes, size), F32)
+        for level in range(levels):
+            wide = jnp.concatenate([residual[level, 0], jnp.zeros((probes, size - width), F32)], axis=1)
+            total = total + (pltpu.roll(wide, level * width, 1) if level else wide)
+        return total
+
     def pack_body(r):
         copy = pltpu.make_async_copy(r.residual, r.near, r.sems.at[0])
+        block = pltpu.make_async_copy(r.diag_inverse.at[0, 0], r.inverse_0, r.sems.at[1])
         copy.start()
+        block.start()
         copy.wait()
-        total = jnp.zeros((probes, size), F32)
-        for level in range(levels):
-            wide = jnp.concatenate([r.near[level, 0], jnp.zeros((probes, size - width), F32)], axis=1)
-            total = total + (pltpu.roll(wide, level * width, 1) if level else wide)
-        r.packed[...] = total
+        r.packed[...] = packed(r.near)
+        block.wait()
 
     def spread_body(r):
+        r.other[...] = packed(r.passed)
         for name, z in outgoing(r, "layer"):
             message = getattr(r, name)
             message[r.core] = r.packed[chip_rows(z)]
             message[1 - r.core] = r.other[chip_rows(z)]
 
+    def lists_body(r):
+        for level in range(levels - 1):
+            for owner in range(owners):
+                for k in range(blocks):
+                    r.lists[(level * owners + owner) * blocks + k] = r.listed[k, owner, level]
+
     def hold_body(r):
         first = pltpu.make_async_copy(r.diag_inverse.at[:, 0], r.inverses, r.sems.at[0])
-        second = pltpu.make_async_copy(r.lower_blocks.at[:, 0], r.lowers, r.sems.at[1])
+        second = pltpu.make_async_copy(r.lower_blocks.at[:1, 0], r.lowers_1, r.sems.at[1])
         first.start()
         second.start()
-        for i in range(r.lists.shape[0]):
-            r.lists[i] = r.listed[i]
         first.wait()
         second.wait()
+
+    def hold_part_body(part):
+        def body(r):
+            source = r.lower_blocks.at[part[0] - 1 : part[-1], 0]
+            copy = pltpu.make_async_copy(source, getattr(r, f"lowers_{part[0]}"), r.sems.at[0])
+            copy.start()
+            copy.wait()
+
+        return body
+
+    parts = [range(1, 2), range(2, levels // 2 + 1), range(levels // 2 + 1, levels)]
+
+    def lower(r, level, k):
+        part = next(part for part in parts if level in part)
+        return getattr(r, f"lowers_{part[0]}")[level - part[0], k]
 
     def begin_body(r):
         r.pieces[CORES * r.z + r.core] = r.packed[chip_rows(r.z)]
@@ -201,7 +225,7 @@
         for name, z in partners(r, "layer"):
             for core in range(CORES):
                 r.pieces[CORES * z + core] = getattr(r, name)[core]
-        answer = times(regroup_one([r.pieces[c] for c in range(columns)], width, 0), r.inverses[0], True)
+        answer = times(regroup_one([r.pieces[c] for c in range(columns)], width, 0), r.inverse_0[...], True)
         r.finished[r.row] = answer
         r.solved[...] = answer
 
@@ -216,7 +240,7 @@
                 r.finished[(level - 1) * owners + owner] = getattr(r, name)[...]
             total = r.source[level]
             for k in range(blocks):
-                total = total - times(r.finished[column_of(r, level, k)], r.lowers[level - 1, k], True)
+                total = total - times(r.finished[column_of(r, level, k)], lower(r, level, k), True)
             answer = times(total, r.inverses[level], True)
             r.finished[level * owners + r.row] = answer
             if level < levels - 1:
@@ -232,7 +256,7 @@
         answer = times(source, r.inverses[level], False)
         r.answers[level] = answer
         for k in range(blocks):
-            r.accumulated[column_of(r, level, k)] += times(answer, r.lowers[level - 1, k], False)
+            r.accumulated[column_of(r, level, k)] += times(answer, lower(r, level, k), False)
         for name, owner in outgoing(r, "row"):
             getattr(r, name)[...] = r.accumulated[(level - 1) * owners + owner]
 
@@ -249,51 +273,60 @@
         for column in range(columns):
             r.pieces[column] = moved(column)
         for name, z in outgoing(r, "layer"):
-            if name == "to_single":
-                r.to_single[...] = r.pieces[CORES * z + r.core]
-            else:
-                for core in range(CORES):
-                    getattr(r, name)[core] = r.pieces[CORES * z + core]
+            for core in range(CORES):
+                getattr(r, name)[core] = r.pieces[CORES * z + core]
         r.kept[...] = r.pieces[CORES * r.z + r.core]
 
     def out_body(r):
         r.whole[chip_rows(r.z)] = r.kept[...]
         for name, z in partners(r, "layer"):
-            message = getattr(r, name)
-            r.whole[chip_rows(z)] = message[...] if name == "single" else message[r.core]
+            r.whole[chip_rows(z)] = getattr(r, name)[r.core]
         whole = r.whole[...]
         for level in range(levels):
             moved = pltpu.roll(whole, size - level * width, 1) if level else whole
             r.out[level, 0] = moved[:, :width]
 
-    packed = call(
-        "pack", pack_body, {"residual": residual_in}, makes={"packed": VMEM((probes, size), F32)},
-        scratch={"near": VMEM(residual_in.shape, F32), "sems": dma((1,))},
-    )["packed"]
-    other = swap(packed)
-    held = call(
-        "hold_blocks", hold_body,
-        {"listed": column_lists.reshape(-1), "diag_inverse": diag_inverse, "lower_blocks": lower_blocks},
-        makes={
-            "lists": SMEM((column_lists.size,), jnp.int32),
-            "inverses": VMEM((levels, size, size), BF16),
-            "lowers": VMEM((levels - 1, blocks, size, size), BF16),
-        },
-        scratch={"sems": dma((2,))},
-        cost=pl.CostEstimate(flops=0, bytes_accessed=16 * 2**20, transcendentals=0),
+    blocks_in = {"diag_inverse": diag_inverse, "lower_blocks": lower_blocks}
+    begun = call(
+        "pack", pack_body, {"residual": residual_in, "diag_inverse": diag_inverse},
+        makes={"packed": VMEM((probes, size), F32), "inverse_0": VMEM((size, size), BF16)},
+        scratch={"near": VMEM(residual_in.shape, F32), "sems": dma((2,))},
     )
     both = (CORES, each, size)
-    spread = call("spread", spread_body, {"packed": packed, "other": other}, makes=messages("layer", both, both))
+    spread = call(
+        "spread", spread_body, {"packed": begun["packed"], "passed": swap(residual_in)},
+        makes={"other": VMEM((probes, size), F32), **messages("layer", both, both)},
+    )
+    arrived = exchanged("layer", spread)
+    lists = call(
+        "lists", lists_body, {"listed": column_lists.transpose(2, 1, 0), "after": arrived["direct_0"]},
+        makes={"lists": SMEM((column_lists.size,), jnp.int32)},
+    )["lists"]
     begun = call(
         "forward_0", begin_body,
-        {"packed": packed, "other": other, "inverses": held["inverses"], **exchanged("layer", spread)},
+        {
+            "packed": begun["packed"], "other": spread["other"], "inverse_0": begun["inverse_0"], "lists": lists,
+            **arrived,
+        },
         makes={"pieces": packed_rows, "finished": all_rows, "solved": rows},
+    )
+    held = {"lists": lists} | call(
+        "hold", hold_body, {**blocks_in, "after": begun["solved"]},
+        makes={"inverses": VMEM((levels, size, size), BF16), "lowers_1": VMEM((1, blocks, size, size), BF16)},
+        scratch={"sems": dma((2,))},
     )
     source = call("source", source_body, {"pieces": begun["pieces"]}, makes={"source": own_rows})["source"]
     finished, solved = begun["finished"], begun["solved"]
     to_owners = messages("row", (each, size), (each, size))
     for level in range(1, levels):
         last = level == levels - 1
+        if level in (2, 3):
+            part = parts[level - 1]
+            held |= call(
+                f"hold_{level}", hold_part_body(part), {"lower_blocks": lower_blocks, "after": solved},
+                makes={f"lowers_{part[0]}": VMEM((len(part), blocks, size, size), BF16)},
+                scratch={"sems": dma((1,))},
+            )
         state = call(
             f"forward_{level}", forward_body(level),
             {**held, "source": source, **exchange("row", [solved] * len(row_routes[0]), solved)},
@@ -314,7 +347,7 @@
             **exchanged("row", state),
         },
         {"answers": state["answers"]},
-        {"kept": rows, **messages("layer", both, (each, size))},
+        {"kept": rows, **messages("layer", both, both)},
         {"pieces": packed_rows},
     )
     return call(

time: 95.7 us -> 90.8 us (0.949)
  waiting for transfers between devices: 37.3 us -> 28.7 us
  Pallas kernels: 9.52 us -> 11.7 us
  starting transfers between devices: 47.7 us -> 49.8 us
    ppermute x32, waiting for transfers between devices: 36.4 us -> 27.9 us  [send(): return lax.ppermute(array, ('row', 'col'), steps)]
    pallas_call x20 -> x23, Pallas kernels: 9.52 us -> 11.7 us  [call(): pl.pallas_call(kernel, in_specs=[spec(key) for key in in_names], out_spec...]
    ppermute x32, starting transfers between devices: 45.7 us -> 47.4 us  [send(): return lax.ppermute(array, ('row', 'col'), steps)]
  transfers between devices with their start and end apart: 49 -> 49, of which waited for: 31 -> 31; matrix products, arithmetic and copies ran while one was open for 1% -> 0% of each run, Pallas kernels for 3% -> 6%
where the time goes in v4:
time: 90.8 us; the launch traced here: 90.4 us
  starting transfers between devices  49.8 us (55%)
  waiting for transfers between devices  28.7 us (32%)
  Pallas kernels  11.7 us (13%)
    ppermute x32, starting transfers between devices, send(): return lax.ppermute(array, ('row', 'col'), steps)  47.4 us
    ppermute x32, waiting for transfers between devices, send(): return lax.ppermute(array, ('row', 'col'), steps)  27.9 us
    pallas_call x23, Pallas kernels, call(): pl.pallas_call(kernel, in_specs=[spec(key) for key in in_names], out_spec...  11.7 us
    ppermute x17, starting transfers between devices, swap(): return lax.ppermute(array, 'col', [(c, c ^ 1) for c in range(columns)])  2.39 us
  transfers between devices with their start and end apart: 49, of which 31 were waited for; matrix products, arithmetic and copies ran while one was open for 0% of the time, Pallas kernels for 6%

profile of v4, /device:TPU:0, one launch (start us, length us, event | category | flops | bytes accessed | tf_op | source)
XLA Modules:
  0.0 90.4 jit_solution(12305725802955220819)
XLA Ops:
  1.8 3.0 %collective-permute-start.1 = (f32[2,8,256]{2,1,0:T(8,128)S(1)}, f32[2,8,256]{2,1,0:T(8,128)S(1)}, u32[]{:S(2)}, u32[]{:S(2)}) collective-permute-start(f32[2,8,256]{2,1,0:T(8,128)S(1)} %get-tuple-element.62), channel_id=1, source_target_pairs={{0,2},{1,7},{2,0},{3,5},{4,6},{5,3},{6,4},{7,1},{8,10},{9,15},{10,... | collective-permute-start | bytes 49160 | tf_op jit(solution)/shard_map/ppermute | solution.py:134
  4.8 2.6 %collective-permute-start.2 = (f32[2,8,256]{2,1,0:T(8,128)S(1)}, f32[2,8,256]{2,1,0:T(8,128)S(1)}, u32[]{:S(2)}, u32[]{:S(2)}) collective-permute-start(f32[2,8,256]{2,1,0:T(8,128)S(1)} %get-tuple-element.63), channel_id=1, source_target_pairs={{0,4},{1,5},{2,6},{3,7},{4,0},{5,1},{6,2},{7,3},{8,12},{9,13},{10,... | collective-permute-start | bytes 49160 | tf_op jit(solution)/shard_map/ppermute | solution.py:134
  9.7 1.6 %collective-permute-start.4 = (f32[8,256]{1,0:T(8,128)S(1)}, f32[8,256]{1,0:T(8,128)S(1)}, u32[]{:S(2)}, u32[]{:S(2)}) collective-permute-start(f32[8,256]{1,0:T(8,128)S(1)} %get-tuple-element.64.refs_2_), channel_id=1, source_target_pairs={{0,8},{1,25},{2,10},{3,27},{4,12},{5,29},{6,14},{7,31},{8,0},{9,17... | collective-permute-start | bytes 24584 | tf_op jit(solution)/shard_map/ppermute | solution.py:134
  11.3 1.5 %collective-permute-start.5 = (f32[8,256]{1,0:T(8,128)S(1)}, f32[8,256]{1,0:T(8,128)S(1)}, u32[]{:S(2)}, u32[]{:S(2)}) collective-permute-start(f32[8,256]{1,0:T(8,128)S(1)} %get-tuple-element.64.refs_2_), channel_id=1, source_target_pairs={{0,16},{1,17},{2,18},{3,19},{4,20},{5,21},{6,22},{7,23},{8,24},{9,... | collective-permute-start | bytes 24584 | tf_op jit(solution)/shard_map/ppermute | solution.py:134
  13.9 1.3 %hold.1 = (bf16[8,256,256]{2,1,0:T(8,128)(2,1)S(1)}, bf16[1,3,256,256]{3,2,1,0:T(8,128)(2,1)S(1)}) custom-call(bf16[8,1,256,256]{3,2,1,0:T(8,128)(2,1)} %refs_0_.5, bf16[7,1,3,256,256]{4,3,2,1,0:T(8,128)(2,1)} %refs_0_.7, f32[8,256]{1,0:T(8,128)S(1)} %get-tuple-element.64.refs_2_), custom_call_target="tpu_custom_call" | custom-call | tf_op jit(solution)/shard_map/hold/pallas_call | solution.py:93
  15.6 1.5 %collective-permute-start.7 = (f32[8,256]{1,0:T(8,128)S(1)}, f32[8,256]{1,0:T(8,128)S(1)}, u32[]{:S(2)}, u32[]{:S(2)}) collective-permute-start(f32[8,256]{1,0:T(8,128)S(1)} %get-tuple-element.69.refs_1_), channel_id=1, source_target_pairs={{0,8},{1,25},{2,10},{3,27},{4,12},{5,29},{6,14},{7,31},{8,0},{9,17... | collective-permute-start | bytes 24584 | tf_op jit(solution)/shard_map/ppermute | solution.py:134
  17.2 1.5 %collective-permute-start.8 = (f32[8,256]{1,0:T(8,128)S(1)}, f32[8,256]{1,0:T(8,128)S(1)}, u32[]{:S(2)}, u32[]{:S(2)}) collective-permute-start(f32[8,256]{1,0:T(8,128)S(1)} %get-tuple-element.69.refs_1_), channel_id=1, source_target_pairs={{0,16},{1,17},{2,18},{3,19},{4,20},{5,21},{6,22},{7,23},{8,24},{9,... | collective-permute-start | bytes 24584 | tf_op jit(solution)/shard_map/ppermute | solution.py:134
  19.3 1.3 %hold_2.1.refs_3_ = bf16[3,3,256,256]{3,2,1,0:T(8,128)(2,1)S(1)} custom-call(bf16[7,1,3,256,256]{4,3,2,1,0:T(8,128)(2,1)} %refs_0_.7, f32[8,256]{1,0:T(8,128)S(1)} %get-tuple-element.69.refs_1_), custom_call_target="tpu_custom_call" | custom-call | tf_op jit(solution)/shard_map/hold_2/pallas_call | solution.py:93
  21.2 1.3 %collective-permute-start.10 = (f32[8,256]{1,0:T(8,128)S(1)}, f32[8,256]{1,0:T(8,128)S(1)}, u32[]{:S(2)}, u32[]{:S(2)}) collective-permute-start(f32[8,256]{1,0:T(8,128)S(1)} %get-tuple-element.71.refs_1_), channel_id=1, source_target_pairs={{0,8},{1,25},{2,10},{3,27},{4,12},{5,29},{6,14},{7,31},{8,0},{9,17... | collective-permute-start | bytes 24584 | tf_op jit(solution)/shard_map/ppermute | solution.py:134
  22.5 1.5 %collective-permute-start.11 = (f32[8,256]{1,0:T(8,128)S(1)}, f32[8,256]{1,0:T(8,128)S(1)}, u32[]{:S(2)}, u32[]{:S(2)}) collective-permute-start(f32[8,256]{1,0:T(8,128)S(1)} %get-tuple-element.71.refs_1_), channel_id=1, source_target_pairs={{0,16},{1,17},{2,18},{3,19},{4,20},{5,21},{6,22},{7,23},{8,24},{9,... | collective-permute-start | bytes 24584 | tf_op jit(solution)/shard_map/ppermute | solution.py:134
  26.5 1.6 %collective-permute-start.13 = (f32[8,256]{1,0:T(8,128)S(1)}, f32[8,256]{1,0:T(8,128)S(1)}, u32[]{:S(2)}, u32[]{:S(2)}) collective-permute-start(f32[8,256]{1,0:T(8,128)S(1)} %get-tuple-element.73), channel_id=1, source_target_pairs={{0,8},{1,25},{2,10},{3,27},{4,12},{5,29},{6,14},{7,31},{8,0},{9,17... | collective-permute-start | bytes 24584 | tf_op jit(solution)/shard_map/ppermute | solution.py:134
  28.1 1.5 %collective-permute-start.14 = (f32[8,256]{1,0:T(8,128)S(1)}, f32[8,256]{1,0:T(8,128)S(1)}, u32[]{:S(2)}, u32[]{:S(2)}) collective-permute-start(f32[8,256]{1,0:T(8,128)S(1)} %get-tuple-element.73), channel_id=1, source_target_pairs={{0,16},{1,17},{2,18},{3,19},{4,20},{5,21},{6,22},{7,23},{8,24},{9,... | collective-permute-start | bytes 24584 | tf_op jit(solution)/shard_map/ppermute | solution.py:134
  30.4 1.3 %collective-permute-done.14.refs_7_ = f32[8,256]{1,0:T(8,128)S(1)} collective-permute-done((f32[8,256]{1,0:T(8,128)S(1)}, f32[8,256]{1,0:T(8,128)S(1)}, u32[]{:S(2)}, u32[]{:S(2)}) %collective-permute-start.14) | collective-permute-done | bytes 8224 | tf_op jit(solution)/shard_map/ppermute | solution.py:134
  33.3 1.5 %collective-permute-start.17 = (f32[8,256]{1,0:T(8,128)S(1)}, f32[8,256]{1,0:T(8,128)S(1)}, u32[]{:S(2)}, u32[]{:S(2)}) collective-permute-start(f32[8,256]{1,0:T(8,128)S(1)} %get-tuple-element.75), channel_id=1, source_target_pairs={{0,16},{1,17},{2,18},{3,19},{4,20},{5,21},{6,22},{7,23},{8,24},{9,... | collective-permute-start | bytes 24584 | tf_op jit(solution)/shard_map/ppermute | solution.py:134
  38.5 1.5 %collective-permute-start.20 = (f32[8,256]{1,0:T(8,128)S(1)}, f32[8,256]{1,0:T(8,128)S(1)}, u32[]{:S(2)}, u32[]{:S(2)}) collective-permute-start(f32[8,256]{1,0:T(8,128)S(1)} %get-tuple-element.77), channel_id=1, source_target_pairs={{0,16},{1,17},{2,18},{3,19},{4,20},{5,21},{6,22},{7,23},{8,24},{9,... | collective-permute-start | bytes 24584 | tf_op jit(solution)/shard_map/ppermute | solution.py:134
  43.7 1.5 %collective-permute-start.23 = (f32[8,256]{1,0:T(8,128)S(1)}, f32[8,256]{1,0:T(8,128)S(1)}, u32[]{:S(2)}, u32[]{:S(2)}) collective-permute-start(f32[8,256]{1,0:T(8,128)S(1)} %get-tuple-element.79), channel_id=1, source_target_pairs={{0,16},{1,17},{2,18},{3,19},{4,20},{5,21},{6,22},{7,23},{8,24},{9,... | collective-permute-start | bytes 24584 | tf_op jit(solution)/shard_map/ppermute | solution.py:134
  49.2 1.5 %collective-permute-start.26 = (f32[8,256]{1,0:T(8,128)S(1)}, f32[8,256]{1,0:T(8,128)S(1)}, u32[]{:S(2)}, u32[]{:S(2)}) collective-permute-start(f32[8,256]{1,0:T(8,128)S(1)} %get-tuple-element.83), channel_id=1, source_target_pairs={{0,16},{1,17},{2,18},{3,19},{4,20},{5,21},{6,22},{7,23},{8,24},{9,... | collective-permute-start | bytes 24584 | tf_op jit(solution)/shard_map/ppermute | solution.py:134
  54.4 1.5 %collective-permute-start.29 = (f32[8,256]{1,0:T(8,128)S(1)}, f32[8,256]{1,0:T(8,128)S(1)}, u32[]{:S(2)}, u32[]{:S(2)}) collective-permute-start(f32[8,256]{1,0:T(8,128)S(1)} %get-tuple-element.87), channel_id=1, source_target_pairs={{0,16},{1,17},{2,18},{3,19},{4,20},{5,21},{6,22},{7,23},{8,24},{9,... | collective-permute-start | bytes 24584 | tf_op jit(solution)/shard_map/ppermute | solution.py:134
  59.6 1.5 %collective-permute-start.32 = (f32[8,256]{1,0:T(8,128)S(1)}, f32[8,256]{1,0:T(8,128)S(1)}, u32[]{:S(2)}, u32[]{:S(2)}) collective-permute-start(f32[8,256]{1,0:T(8,128)S(1)} %get-tuple-element.91), channel_id=1, source_target_pairs={{0,16},{1,17},{2,18},{3,19},{4,20},{5,21},{6,22},{7,23},{8,24},{9,... | collective-permute-start | bytes 24584 | tf_op jit(solution)/shard_map/ppermute | solution.py:134
  64.7 1.5 %collective-permute-start.35 = (f32[8,256]{1,0:T(8,128)S(1)}, f32[8,256]{1,0:T(8,128)S(1)}, u32[]{:S(2)}, u32[]{:S(2)}) collective-permute-start(f32[8,256]{1,0:T(8,128)S(1)} %get-tuple-element.95), channel_id=1, source_target_pairs={{0,16},{1,17},{2,18},{3,19},{4,20},{5,21},{6,22},{7,23},{8,24},{9,... | collective-permute-start | bytes 24584 | tf_op jit(solution)/shard_map/ppermute | solution.py:134
  69.9 1.5 %collective-permute-start.38 = (f32[8,256]{1,0:T(8,128)S(1)}, f32[8,256]{1,0:T(8,128)S(1)}, u32[]{:S(2)}, u32[]{:S(2)}) collective-permute-start(f32[8,256]{1,0:T(8,128)S(1)} %get-tuple-element.99), channel_id=1, source_target_pairs={{0,16},{1,17},{2,18},{3,19},{4,20},{5,21},{6,22},{7,23},{8,24},{9,... | collective-permute-start | bytes 24584 | tf_op jit(solution)/shard_map/ppermute | solution.py:134
  75.1 1.5 %collective-permute-start.41 = (f32[8,256]{1,0:T(8,128)S(1)}, f32[8,256]{1,0:T(8,128)S(1)}, u32[]{:S(2)}, u32[]{:S(2)}) collective-permute-start(f32[8,256]{1,0:T(8,128)S(1)} %get-tuple-element.103), channel_id=1, source_target_pairs={{0,16},{1,17},{2,18},{3,19},{4,20},{5,21},{6,22},{7,23},{8,24},{9,... | collective-permute-start | bytes 24584 | tf_op jit(solution)/shard_map/ppermute | solution.py:134
  80.3 1.5 %collective-permute-start.44 = (f32[8,256]{1,0:T(8,128)S(1)}, f32[8,256]{1,0:T(8,128)S(1)}, u32[]{:S(2)}, u32[]{:S(2)}) collective-permute-start(f32[8,256]{1,0:T(8,128)S(1)} %get-tuple-element.108), channel_id=1, source_target_pairs={{0,16},{1,17},{2,18},{3,19},{4,20},{5,21},{6,22},{7,23},{8,24},{9,... | collective-permute-start | bytes 24584 | tf_op jit(solution)/shard_map/ppermute | solution.py:134
  84.6 2.6 %collective-permute-start.47 = (f32[2,8,256]{2,1,0:T(8,128)S(1)}, f32[2,8,256]{2,1,0:T(8,128)S(1)}, u32[]{:S(2)}, u32[]{:S(2)}) collective-permute-start(f32[2,8,256]{2,1,0:T(8,128)S(1)} %get-tuple-element.112), channel_id=1, source_target_pairs={{0,4},{1,5},{2,6},{3,7},{4,0},{5,1},{6,2},{7,3},{8,12},{9,13},{10,... | collective-permute-start | bytes 49160 | tf_op jit(solution)/shard_map/ppermute | solution.py:134
  (97 shorter events, 51.3 us)
Async XLA Ops:
  1.8 5.6 %collective-permute-start.1 = (f32[2,8,256]{2,1,0:T(8,128)S(1)}, f32[2,8,256]{2,1,0:T(8,128)S(1)}, u32[]{:S(2)}, u32[]{:S(2)}) collective-permute-start(f32[2,8,256]{2,1,0:T(8,128)S(1)} %get-tuple-element.62), channel_id=1, source_target_pairs={{0,2},{1,7},{2,0},{3,5},{4,6},{5,3},{6,4},{7,1},{8,10},{9,15},{10,... | collective-permute-start | bytes 49160 | tf_op jit(solution)/shard_map/ppermute | solution.py:134
  4.8 4.7 %collective-permute-start.2 = (f32[2,8,256]{2,1,0:T(8,128)S(1)}, f32[2,8,256]{2,1,0:T(8,128)S(1)}, u32[]{:S(2)}, u32[]{:S(2)}) collective-permute-start(f32[2,8,256]{2,1,0:T(8,128)S(1)} %get-tuple-element.63), channel_id=1, source_target_pairs={{0,4},{1,5},{2,6},{3,7},{4,0},{5,1},{6,2},{7,3},{8,12},{9,13},{10,... | collective-permute-start | bytes 49160 | tf_op jit(solution)/shard_map/ppermute | solution.py:134
  9.7 3.7 %collective-permute-start.4 = (f32[8,256]{1,0:T(8,128)S(1)}, f32[8,256]{1,0:T(8,128)S(1)}, u32[]{:S(2)}, u32[]{:S(2)}) collective-permute-start(f32[8,256]{1,0:T(8,128)S(1)} %get-tuple-element.64.refs_2_), channel_id=1, source_target_pairs={{0,8},{1,25},{2,10},{3,27},{4,12},{5,29},{6,14},{7,31},{8,0},{9,17... | collective-permute-start | bytes 24584 | tf_op jit(solution)/shard_map/ppermute | solution.py:134
  11.3 3.9 %collective-permute-start.5 = (f32[8,256]{1,0:T(8,128)S(1)}, f32[8,256]{1,0:T(8,128)S(1)}, u32[]{:S(2)}, u32[]{:S(2)}) collective-permute-start(f32[8,256]{1,0:T(8,128)S(1)} %get-tuple-element.64.refs_2_), channel_id=1, source_target_pairs={{0,16},{1,17},{2,18},{3,19},{4,20},{5,21},{6,22},{7,23},{8,24},{9,... | collective-permute-start | bytes 24584 | tf_op jit(solution)/shard_map/ppermute | solution.py:134
  15.6 3.7 %collective-permute-start.7 = (f32[8,256]{1,0:T(8,128)S(1)}, f32[8,256]{1,0:T(8,128)S(1)}, u32[]{:S(2)}, u32[]{:S(2)}) collective-permute-start(f32[8,256]{1,0:T(8,128)S(1)} %get-tuple-element.69.refs_1_), channel_id=1, source_target_pairs={{0,8},{1,25},{2,10},{3,27},{4,12},{5,29},{6,14},{7,31},{8,0},{9,17... | collective-permute-start | bytes 24584 | tf_op jit(solution)/shard_map/ppermute | solution.py:134
  17.2 3.7 %collective-permute-start.8 = (f32[8,256]{1,0:T(8,128)S(1)}, f32[8,256]{1,0:T(8,128)S(1)}, u32[]{:S(2)}, u32[]{:S(2)}) collective-permute-start(f32[8,256]{1,0:T(8,128)S(1)} %get-tuple-element.69.refs_1_), channel_id=1, source_target_pairs={{0,16},{1,17},{2,18},{3,19},{4,20},{5,21},{6,22},{7,23},{8,24},{9,... | collective-permute-start | bytes 24584 | tf_op jit(solution)/shard_map/ppermute | solution.py:134
  21.2 3.7 %collective-permute-start.10 = (f32[8,256]{1,0:T(8,128)S(1)}, f32[8,256]{1,0:T(8,128)S(1)}, u32[]{:S(2)}, u32[]{:S(2)}) collective-permute-start(f32[8,256]{1,0:T(8,128)S(1)} %get-tuple-element.71.refs_1_), channel_id=1, source_target_pairs={{0,8},{1,25},{2,10},{3,27},{4,12},{5,29},{6,14},{7,31},{8,0},{9,17... | collective-permute-start | bytes 24584 | tf_op jit(solution)/shard_map/ppermute | solution.py:134
  22.5 3.7 %collective-permute-start.11 = (f32[8,256]{1,0:T(8,128)S(1)}, f32[8,256]{1,0:T(8,128)S(1)}, u32[]{:S(2)}, u32[]{:S(2)}) collective-permute-start(f32[8,256]{1,0:T(8,128)S(1)} %get-tuple-element.71.refs_1_), channel_id=1, source_target_pairs={{0,16},{1,17},{2,18},{3,19},{4,20},{5,21},{6,22},{7,23},{8,24},{9,... | collective-permute-start | bytes 24584 | tf_op jit(solution)/shard_map/ppermute | solution.py:134
  26.5 3.7 %collective-permute-start.13 = (f32[8,256]{1,0:T(8,128)S(1)}, f32[8,256]{1,0:T(8,128)S(1)}, u32[]{:S(2)}, u32[]{:S(2)}) collective-permute-start(f32[8,256]{1,0:T(8,128)S(1)} %get-tuple-element.73), channel_id=1, source_target_pairs={{0,8},{1,25},{2,10},{3,27},{4,12},{5,29},{6,14},{7,31},{8,0},{9,17... | collective-permute-start | bytes 24584 | tf_op jit(solution)/shard_map/ppermute | solution.py:134
  28.1 3.7 %collective-permute-start.14 = (f32[8,256]{1,0:T(8,128)S(1)}, f32[8,256]{1,0:T(8,128)S(1)}, u32[]{:S(2)}, u32[]{:S(2)}) collective-permute-start(f32[8,256]{1,0:T(8,128)S(1)} %get-tuple-element.73), channel_id=1, source_target_pairs={{0,16},{1,17},{2,18},{3,19},{4,20},{5,21},{6,22},{7,23},{8,24},{9,... | collective-permute-start | bytes 24584 | tf_op jit(solution)/shard_map/ppermute | solution.py:134
  32.1 3.7 %collective-permute-start.16 = (f32[8,256]{1,0:T(8,128)S(1)}, f32[8,256]{1,0:T(8,128)S(1)}, u32[]{:S(2)}, u32[]{:S(2)}) collective-permute-start(f32[8,256]{1,0:T(8,128)S(1)} %get-tuple-element.75), channel_id=1, source_target_pairs={{0,8},{1,25},{2,10},{3,27},{4,12},{5,29},{6,14},{7,31},{8,0},{9,17... | collective-permute-start | bytes 24584 | tf_op jit(solution)/shard_map/ppermute | solution.py:134
  33.3 3.7 %collective-permute-start.17 = (f32[8,256]{1,0:T(8,128)S(1)}, f32[8,256]{1,0:T(8,128)S(1)}, u32[]{:S(2)}, u32[]{:S(2)}) collective-permute-start(f32[8,256]{1,0:T(8,128)S(1)} %get-tuple-element.75), channel_id=1, source_target_pairs={{0,16},{1,17},{2,18},{3,19},{4,20},{5,21},{6,22},{7,23},{8,24},{9,... | collective-permute-start | bytes 24584 | tf_op jit(solution)/shard_map/ppermute | solution.py:134
  37.3 3.7 %collective-permute-start.19 = (f32[8,256]{1,0:T(8,128)S(1)}, f32[8,256]{1,0:T(8,128)S(1)}, u32[]{:S(2)}, u32[]{:S(2)}) collective-permute-start(f32[8,256]{1,0:T(8,128)S(1)} %get-tuple-element.77), channel_id=1, source_target_pairs={{0,8},{1,25},{2,10},{3,27},{4,12},{5,29},{6,14},{7,31},{8,0},{9,17... | collective-permute-start | bytes 24584 | tf_op jit(solution)/shard_map/ppermute | solution.py:134
  42.5 3.7 %collective-permute-start.22 = (f32[8,256]{1,0:T(8,128)S(1)}, f32[8,256]{1,0:T(8,128)S(1)}, u32[]{:S(2)}, u32[]{:S(2)}) collective-permute-start(f32[8,256]{1,0:T(8,128)S(1)} %get-tuple-element.79), channel_id=1, source_target_pairs={{0,8},{1,25},{2,10},{3,27},{4,12},{5,29},{6,14},{7,31},{8,0},{9,17... | collective-permute-start | bytes 24584 | tf_op jit(solution)/shard_map/ppermute | solution.py:134
  43.7 3.7 %collective-permute-start.23 = (f32[8,256]{1,0:T(8,128)S(1)}, f32[8,256]{1,0:T(8,128)S(1)}, u32[]{:S(2)}, u32[]{:S(2)}) collective-permute-start(f32[8,256]{1,0:T(8,128)S(1)} %get-tuple-element.79), channel_id=1, source_target_pairs={{0,16},{1,17},{2,18},{3,19},{4,20},{5,21},{6,22},{7,23},{8,24},{9,... | collective-permute-start | bytes 24584 | tf_op jit(solution)/shard_map/ppermute | solution.py:134
  48.0 3.7 %collective-permute-start.25 = (f32[8,256]{1,0:T(8,128)S(1)}, f32[8,256]{1,0:T(8,128)S(1)}, u32[]{:S(2)}, u32[]{:S(2)}) collective-permute-start(f32[8,256]{1,0:T(8,128)S(1)} %get-tuple-element.82), channel_id=1, source_target_pairs={{0,8},{1,25},{2,10},{3,27},{4,12},{5,29},{6,14},{7,31},{8,0},{9,17... | collective-permute-start | bytes 24584 | tf_op jit(solution)/shard_map/ppermute | solution.py:134
  53.2 3.7 %collective-permute-start.28 = (f32[8,256]{1,0:T(8,128)S(1)}, f32[8,256]{1,0:T(8,128)S(1)}, u32[]{:S(2)}, u32[]{:S(2)}) collective-permute-start(f32[8,256]{1,0:T(8,128)S(1)} %get-tuple-element.86), channel_id=1, source_target_pairs={{0,8},{1,25},{2,10},{3,27},{4,12},{5,29},{6,14},{7,31},{8,0},{9,17... | collective-permute-start | bytes 24584 | tf_op jit(solution)/shard_map/ppermute | solution.py:134
  58.4 3.7 %collective-permute-start.31 = (f32[8,256]{1,0:T(8,128)S(1)}, f32[8,256]{1,0:T(8,128)S(1)}, u32[]{:S(2)}, u32[]{:S(2)}) collective-permute-start(f32[8,256]{1,0:T(8,128)S(1)} %get-tuple-element.90), channel_id=1, source_target_pairs={{0,8},{1,25},{2,10},{3,27},{4,12},{5,29},{6,14},{7,31},{8,0},{9,17... | collective-permute-start | bytes 24584 | tf_op jit(solution)/shard_map/ppermute | solution.py:134
  63.5 3.7 %collective-permute-start.34 = (f32[8,256]{1,0:T(8,128)S(1)}, f32[8,256]{1,0:T(8,128)S(1)}, u32[]{:S(2)}, u32[]{:S(2)}) collective-permute-start(f32[8,256]{1,0:T(8,128)S(1)} %get-tuple-element.94), channel_id=1, source_target_pairs={{0,8},{1,25},{2,10},{3,27},{4,12},{5,29},{6,14},{7,31},{8,0},{9,17... | collective-permute-start | bytes 24584 | tf_op jit(solution)/shard_map/ppermute | solution.py:134
  68.7 3.7 %collective-permute-start.37 = (f32[8,256]{1,0:T(8,128)S(1)}, f32[8,256]{1,0:T(8,128)S(1)}, u32[]{:S(2)}, u32[]{:S(2)}) collective-permute-start(f32[8,256]{1,0:T(8,128)S(1)} %get-tuple-element.98), channel_id=1, source_target_pairs={{0,8},{1,25},{2,10},{3,27},{4,12},{5,29},{6,14},{7,31},{8,0},{9,17... | collective-permute-start | bytes 24584 | tf_op jit(solution)/shard_map/ppermute | solution.py:134
  73.9 3.7 %collective-permute-start.40 = (f32[8,256]{1,0:T(8,128)S(1)}, f32[8,256]{1,0:T(8,128)S(1)}, u32[]{:S(2)}, u32[]{:S(2)}) collective-permute-start(f32[8,256]{1,0:T(8,128)S(1)} %get-tuple-element.102), channel_id=1, source_target_pairs={{0,8},{1,25},{2,10},{3,27},{4,12},{5,29},{6,14},{7,31},{8,0},{9,17... | collective-permute-start | bytes 24584 | tf_op jit(solution)/shard_map/ppermute | solution.py:134
  79.1 3.7 %collective-permute-start.43 = (f32[8,256]{1,0:T(8,128)S(1)}, f32[8,256]{1,0:T(8,128)S(1)}, u32[]{:S(2)}, u32[]{:S(2)}) collective-permute-start(f32[8,256]{1,0:T(8,128)S(1)} %get-tuple-element.107), channel_id=1, source_target_pairs={{0,8},{1,25},{2,10},{3,27},{4,12},{5,29},{6,14},{7,31},{8,0},{9,17... | collective-permute-start | bytes 24584 | tf_op jit(solution)/shard_map/ppermute | solution.py:134
  84.2 3.8 %collective-permute-start.46 = (f32[2,8,256]{2,1,0:T(8,128)S(1)}, f32[2,8,256]{2,1,0:T(8,128)S(1)}, u32[]{:S(2)}, u32[]{:S(2)}) collective-permute-start(f32[2,8,256]{2,1,0:T(8,128)S(1)} %get-tuple-element.111), channel_id=1, source_target_pairs={{0,2},{1,7},{2,0},{3,5},{4,6},{5,3},{6,4},{7,1},{8,10},{9,15},{10,... | collective-permute-start | bytes 49160 | tf_op jit(solution)/shard_map/ppermute | solution.py:134
  84.6 4.6 %collective-permute-start.47 = (f32[2,8,256]{2,1,0:T(8,128)S(1)}, f32[2,8,256]{2,1,0:T(8,128)S(1)}, u32[]{:S(2)}, u32[]{:S(2)}) collective-permute-start(f32[2,8,256]{2,1,0:T(8,128)S(1)} %get-tuple-element.112), channel_id=1, source_target_pairs={{0,4},{1,5},{2,6},{3,7},{4,0},{5,1},{6,2},{7,3},{8,12},{9,13},{10,... | collective-permute-start | bytes 49160 | tf_op jit(solution)/shard_map/ppermute | solution.py:134
  (25 other events, 52.7 us)

commit v5 on v4

--- a/solution.py
+++ b/solution.py
@@ -133,10 +133,9 @@
                     steps.append((row * columns + column, to[0] * columns + to[1]))
             return lax.ppermute(array, ("row", "col"), steps)
 
-        got = {}
+        got = {"single": send(single, (last, last))}
         for i, masks in enumerate(pairs):
             got[f"direct_{i}"] = send(paired[i], masks)
-        got["single"] = send(single, (last, last))
         for i in range(len(pairs)):
             got[f"passed_{i}"] = swap(got[f"direct_{i}"])
         return got
@@ -176,12 +175,20 @@
 
     def pack_body(r):
         copy = pltpu.make_async_copy(r.residual, r.near, r.sems.at[0])
+        copy.start()
         block = pltpu.make_async_copy(r.diag_inverse.at[0, 0], r.inverse_0, r.sems.at[1])
-        copy.start()
         block.start()
+        others = [
+            pltpu.make_async_copy(r.diag_inverse.at[1, 0], r.inverse_1, r.sems.at[2]),
+            pltpu.make_async_copy(r.lower_blocks.at[0, 0], r.lower_1, r.sems.at[3]),
+        ]
+        for other in others:
+            other.start()
         copy.wait()
         r.packed[...] = packed(r.near)
         block.wait()
+        for other in others:
+            other.wait()
 
     def spread_body(r):
         r.other[...] = packed(r.passed)
@@ -196,28 +203,11 @@
                 for k in range(blocks):
                     r.lists[(level * owners + owner) * blocks + k] = r.listed[k, owner, level]
 
-    def hold_body(r):
-        first = pltpu.make_async_copy(r.diag_inverse.at[:, 0], r.inverses, r.sems.at[0])
-        second = pltpu.make_async_copy(r.lower_blocks.at[:1, 0], r.lowers_1, r.sems.at[1])
-        first.start()
-        second.start()
-        first.wait()
-        second.wait()
-
-    def hold_part_body(part):
-        def body(r):
-            source = r.lower_blocks.at[part[0] - 1 : part[-1], 0]
-            copy = pltpu.make_async_copy(source, getattr(r, f"lowers_{part[0]}"), r.sems.at[0])
-            copy.start()
-            copy.wait()
-
-        return body
-
-    parts = [range(1, 2), range(2, levels // 2 + 1), range(levels // 2 + 1, levels)]
+    def inverse(r, level):
+        return r.inverse_1[...] if level == 1 else r.inverses[level, 0]
 
     def lower(r, level, k):
-        part = next(part for part in parts if level in part)
-        return getattr(r, f"lowers_{part[0]}")[level - part[0], k]
+        return r.lower_1[k] if level == 1 else r.lowers[level - 1, 0, k]
 
     def begin_body(r):
         r.pieces[CORES * r.z + r.core] = r.packed[chip_rows(r.z)]
@@ -241,7 +231,7 @@
             total = r.source[level]
             for k in range(blocks):
                 total = total - times(r.finished[column_of(r, level, k)], lower(r, level, k), True)
-            answer = times(total, r.inverses[level], True)
+            answer = times(total, inverse(r, level), True)
             r.finished[level * owners + r.row] = answer
             if level < levels - 1:
                 r.solved[...] = answer
@@ -253,7 +243,7 @@
         return body
 
     def backward(r, level, source):
-        answer = times(source, r.inverses[level], False)
+        answer = times(source, inverse(r, level), False)
         r.answers[level] = answer
         for k in range(blocks):
             r.accumulated[column_of(r, level, k)] += times(answer, lower(r, level, k), False)
@@ -268,7 +258,7 @@
         return total
 
     def last_body(r):
-        r.answers[0] = times(source_of(r, 0), r.inverses[0], False)
+        r.answers[0] = times(source_of(r, 0), r.inverse_0[...], False)
         moved = regroup([r.answers[level] for level in range(levels)], width)
         for column in range(columns):
             r.pieces[column] = moved(column)
@@ -287,14 +277,15 @@
             r.out[level, 0] = moved[:, :width]
 
     blocks_in = {"diag_inverse": diag_inverse, "lower_blocks": lower_blocks}
-    begun = call(
-        "pack", pack_body, {"residual": residual_in, "diag_inverse": diag_inverse},
-        makes={"packed": VMEM((probes, size), F32), "inverse_0": VMEM((size, size), BF16)},
-        scratch={"near": VMEM(residual_in.shape, F32), "sems": dma((2,))},
+    first_blocks = {"inverse_1": VMEM((size, size), BF16), "lower_1": VMEM((blocks, size, size), BF16)}
+    at_start = call(
+        "pack", pack_body, {"residual": residual_in, **blocks_in},
+        makes={"packed": VMEM((probes, size), F32), "inverse_0": VMEM((size, size), BF16), **first_blocks},
+        scratch={"near": VMEM(residual_in.shape, F32), "sems": dma((4,))},
     )
     both = (CORES, each, size)
     spread = call(
-        "spread", spread_body, {"packed": begun["packed"], "passed": swap(residual_in)},
+        "spread", spread_body, {"packed": at_start["packed"], "passed": swap(residual_in)},
         makes={"other": VMEM((probes, size), F32), **messages("layer", both, both)},
     )
     arrived = exchanged("layer", spread)
@@ -305,31 +296,22 @@
     begun = call(
         "forward_0", begin_body,
         {
-            "packed": begun["packed"], "other": spread["other"], "inverse_0": begun["inverse_0"], "lists": lists,
+            "packed": at_start["packed"], "other": spread["other"], "inverse_0": at_start["inverse_0"], "lists": lists,
             **arrived,
         },
         makes={"pieces": packed_rows, "finished": all_rows, "solved": rows},
     )
-    held = {"lists": lists} | call(
-        "hold", hold_body, {**blocks_in, "after": begun["solved"]},
-        makes={"inverses": VMEM((levels, size, size), BF16), "lowers_1": VMEM((1, blocks, size, size), BF16)},
-        scratch={"sems": dma((2,))},
-    )
+    held = {1: {key: at_start[key] for key in first_blocks}}
     source = call("source", source_body, {"pieces": begun["pieces"]}, makes={"source": own_rows})["source"]
     finished, solved = begun["finished"], begun["solved"]
     to_owners = messages("row", (each, size), (each, size))
     for level in range(1, levels):
         last = level == levels - 1
-        if level in (2, 3):
-            part = parts[level - 1]
-            held |= call(
-                f"hold_{level}", hold_part_body(part), {"lower_blocks": lower_blocks, "after": solved},
-                makes={f"lowers_{part[0]}": VMEM((len(part), blocks, size, size), BF16)},
-                scratch={"sems": dma((1,))},
-            )
+        arrived = exchange("row", [solved] * len(row_routes[0]), solved)
+        held.setdefault(level, {"inverses": diag_inverse, "lowers": lower_blocks})
         state = call(
             f"forward_{level}", forward_body(level),
-            {**held, "source": source, **exchange("row", [solved] * len(row_routes[0]), solved)},
+            {"lists": lists, **held[level], "source": source, **arrived},
             {"finished": finished},
             {"accumulated": all_rows, "answers": own_rows, **to_owners} if last else {"solved": rows},
         )
@@ -337,13 +319,13 @@
     for level in reversed(range(1, levels - 1)):
         state = call(
             f"backward_{level}", lambda r, level=level: backward(r, level, source_of(r, level)),
-            {**held, "finished": finished, **exchanged("row", state)},
+            {"lists": lists, **held[level], "finished": finished, **exchanged("row", state)},
             {"accumulated": state["accumulated"], "answers": state["answers"]}, to_owners,
         )
     ended = call(
         "backward_0", last_body,
         {
-            "inverses": held["inverses"], "finished": finished, "accumulated": state["accumulated"],
+            "inverse_0": at_start["inverse_0"], "finished": finished, "accumulated": state["accumulated"],
             **exchanged("row", state),
         },
         {"answers": state["answers"]},

time: 90.8 us -> 90.1 us (level)
  waiting for transfers between devices: 28.7 us -> 33.8 us
  Pallas kernels: 11.7 us -> 8.21 us
  starting transfers between devices: 49.8 us -> 47.8 us
    pallas_call x23 -> x20, Pallas kernels: 11.7 us -> 8.21 us  [call(): pl.pallas_call(kernel, in_specs=[spec(key) for key in in_names], out_spec...]
    ppermute x32, waiting for transfers between devices: 27.9 us -> 30.9 us  [send(): return lax.ppermute(array, ('row', 'col'), steps)]
    ppermute x32, starting transfers between devices: 47.4 us -> 44.6 us  [send(): return lax.ppermute(array, ('row', 'col'), steps)]
    ppermute x17, waiting for transfers between devices: 0.79 us -> 2.89 us  [swap(): return lax.ppermute(array, 'col', [(c, c ^ 1) for c in range(columns)])]
  transfers between devices with their start and end apart: 49 -> 49, of which waited for: 31 -> 45; matrix products, arithmetic and copies ran while one was open for 0% -> 0% of each run, Pallas kernels for 6% -> 3%
where the time goes in v5:
time: 90.1 us; the launch traced here: 89.9 us
  starting transfers between devices  47.8 us (53%)
  waiting for transfers between devices  33.8 us (38%)
  Pallas kernels  8.21 us (9%)
    ppermute x32, starting transfers between devices, send(): return lax.ppermute(array, ('row', 'col'), steps)  44.6 us
    ppermute x32, waiting for transfers between devices, send(): return lax.ppermute(array, ('row', 'col'), steps)  30.9 us
    pallas_call x20, Pallas kernels, call(): pl.pallas_call(kernel, in_specs=[spec(key) for key in in_names], out_spec...  8.21 us
    ppermute x17, starting transfers between devices, swap(): return lax.ppermute(array, 'col', [(c, c ^ 1) for c in range(columns)])  3.26 us
    ppermute x17, waiting for transfers between devices, swap(): return lax.ppermute(array, 'col', [(c, c ^ 1) for c in range(columns)])  2.89 us
  transfers between devices with their start and end apart: 49, of which 45 were waited for; matrix products, arithmetic and copies ran while one was open for 0% of the time, Pallas kernels for 3%

profile of v5, /device:TPU:0, one launch (start us, length us, event | category | flops | bytes accessed | tf_op | source)
XLA Modules:
  0.0 89.9 jit_solution(5139459539968604741)
XLA Ops:
  0.5 1.4 %pack.1 = (f32[32,256]{1,0:T(8,128)S(1)}, bf16[256,256]{1,0:T(8,128)(2,1)S(1)}, bf16[256,256]{1,0:T(8,128)(2,1)S(1)}, bf16[3,256,256]{2,1,0:T(8,128)(2,1)S(1)}) custom-call(f32[8,1,32,32]{3,2,1,0:T(8,128)} %refs_0_.1, bf16[8,1,256,256]{3,2,1,0:T(8,128)(2,1)} %refs_1_.23, bf16[7,1,3,256,256]{4,3,2,1,0:T(8,128)(2,1)} %refs_2_.23), custom_call_target="tpu_custom_call" | custom-call | tf_op jit(solution)/shard_map/pack/pallas_call | solution.py:93
  2.0 2.7 %collective-permute-start.1 = (f32[2,8,256]{2,1,0:T(8,128)S(1)}, f32[2,8,256]{2,1,0:T(8,128)S(1)}, u32[]{:S(2)}, u32[]{:S(2)}) collective-permute-start(f32[2,8,256]{2,1,0:T(8,128)S(1)} %get-tuple-element.61), channel_id=1, source_target_pairs={{0,2},{1,7},{2,0},{3,5},{4,6},{5,3},{6,4},{7,1},{8,10},{9,15},{10,... | collective-permute-start | bytes 49160 | tf_op jit(solution)/shard_map/ppermute | solution.py:134
  4.8 2.6 %collective-permute-start.2 = (f32[2,8,256]{2,1,0:T(8,128)S(1)}, f32[2,8,256]{2,1,0:T(8,128)S(1)}, u32[]{:S(2)}, u32[]{:S(2)}) collective-permute-start(f32[2,8,256]{2,1,0:T(8,128)S(1)} %get-tuple-element.63), channel_id=1, source_target_pairs={{0,4},{1,5},{2,6},{3,7},{4,0},{5,1},{6,2},{7,3},{8,12},{9,13},{10,... | collective-permute-start | bytes 49160 | tf_op jit(solution)/shard_map/ppermute | solution.py:134
  9.6 1.6 %collective-permute-start.5 = (f32[8,256]{1,0:T(8,128)S(1)}, f32[8,256]{1,0:T(8,128)S(1)}, u32[]{:S(2)}, u32[]{:S(2)}) collective-permute-start(f32[8,256]{1,0:T(8,128)S(1)} %get-tuple-element.67), channel_id=1, source_target_pairs={{0,8},{1,25},{2,10},{3,27},{4,12},{5,29},{6,14},{7,31},{8,0},{9,17... | collective-permute-start | bytes 24584 | tf_op jit(solution)/shard_map/ppermute | solution.py:134
  11.2 1.5 %collective-permute-start.4 = (f32[8,256]{1,0:T(8,128)S(1)}, f32[8,256]{1,0:T(8,128)S(1)}, u32[]{:S(2)}, u32[]{:S(2)}) collective-permute-start(f32[8,256]{1,0:T(8,128)S(1)} %get-tuple-element.67), channel_id=1, source_target_pairs={{0,16},{1,17},{2,18},{3,19},{4,20},{5,21},{6,22},{7,23},{8,24},{9,... | collective-permute-start | bytes 24584 | tf_op jit(solution)/shard_map/ppermute | solution.py:134
  15.4 1.5 %collective-permute-start.8 = (f32[8,256]{1,0:T(8,128)S(1)}, f32[8,256]{1,0:T(8,128)S(1)}, u32[]{:S(2)}, u32[]{:S(2)}) collective-permute-start(f32[8,256]{1,0:T(8,128)S(1)} %get-tuple-element.69), channel_id=1, source_target_pairs={{0,8},{1,25},{2,10},{3,27},{4,12},{5,29},{6,14},{7,31},{8,0},{9,17... | collective-permute-start | bytes 24584 | tf_op jit(solution)/shard_map/ppermute | solution.py:134
  16.9 1.5 %collective-permute-start.7 = (f32[8,256]{1,0:T(8,128)S(1)}, f32[8,256]{1,0:T(8,128)S(1)}, u32[]{:S(2)}, u32[]{:S(2)}) collective-permute-start(f32[8,256]{1,0:T(8,128)S(1)} %get-tuple-element.69), channel_id=1, source_target_pairs={{0,16},{1,17},{2,18},{3,19},{4,20},{5,21},{6,22},{7,23},{8,24},{9,... | collective-permute-start | bytes 24584 | tf_op jit(solution)/shard_map/ppermute | solution.py:134
  19.2 1.4 %collective-permute-done.7.refs_4_ = f32[8,256]{1,0:T(8,128)S(1)} collective-permute-done((f32[8,256]{1,0:T(8,128)S(1)}, f32[8,256]{1,0:T(8,128)S(1)}, u32[]{:S(2)}, u32[]{:S(2)}) %collective-permute-start.7) | collective-permute-done | bytes 8224 | tf_op jit(solution)/shard_map/ppermute | solution.py:134
  22.1 1.5 %collective-permute-start.10 = (f32[8,256]{1,0:T(8,128)S(1)}, f32[8,256]{1,0:T(8,128)S(1)}, u32[]{:S(2)}, u32[]{:S(2)}) collective-permute-start(f32[8,256]{1,0:T(8,128)S(1)} %get-tuple-element.71), channel_id=1, source_target_pairs={{0,16},{1,17},{2,18},{3,19},{4,20},{5,21},{6,22},{7,23},{8,24},{9,... | collective-permute-start | bytes 24584 | tf_op jit(solution)/shard_map/ppermute | solution.py:134
  27.3 1.5 %collective-permute-start.13 = (f32[8,256]{1,0:T(8,128)S(1)}, f32[8,256]{1,0:T(8,128)S(1)}, u32[]{:S(2)}, u32[]{:S(2)}) collective-permute-start(f32[8,256]{1,0:T(8,128)S(1)} %get-tuple-element.73), channel_id=1, source_target_pairs={{0,16},{1,17},{2,18},{3,19},{4,20},{5,21},{6,22},{7,23},{8,24},{9,... | collective-permute-start | bytes 24584 | tf_op jit(solution)/shard_map/ppermute | solution.py:134
  32.5 1.5 %collective-permute-start.16 = (f32[8,256]{1,0:T(8,128)S(1)}, f32[8,256]{1,0:T(8,128)S(1)}, u32[]{:S(2)}, u32[]{:S(2)}) collective-permute-start(f32[8,256]{1,0:T(8,128)S(1)} %get-tuple-element.75), channel_id=1, source_target_pairs={{0,16},{1,17},{2,18},{3,19},{4,20},{5,21},{6,22},{7,23},{8,24},{9,... | collective-permute-start | bytes 24584 | tf_op jit(solution)/shard_map/ppermute | solution.py:134
  34.0 1.2 %collective-permute-done.17.refs_5_ = f32[8,256]{1,0:T(8,128)S(1)} collective-permute-done((f32[8,256]{1,0:T(8,128)S(1)}, f32[8,256]{1,0:T(8,128)S(1)}, u32[]{:S(2)}, u32[]{:S(2)}) %collective-permute-start.17) | collective-permute-done | bytes 8224 | tf_op jit(solution)/shard_map/ppermute | solution.py:134
  37.7 1.5 %collective-permute-start.19 = (f32[8,256]{1,0:T(8,128)S(1)}, f32[8,256]{1,0:T(8,128)S(1)}, u32[]{:S(2)}, u32[]{:S(2)}) collective-permute-start(f32[8,256]{1,0:T(8,128)S(1)} %get-tuple-element.77), channel_id=1, source_target_pairs={{0,16},{1,17},{2,18},{3,19},{4,20},{5,21},{6,22},{7,23},{8,24},{9,... | collective-permute-start | bytes 24584 | tf_op jit(solution)/shard_map/ppermute | solution.py:134
  39.2 1.2 %collective-permute-done.20.refs_5_ = f32[8,256]{1,0:T(8,128)S(1)} collective-permute-done((f32[8,256]{1,0:T(8,128)S(1)}, f32[8,256]{1,0:T(8,128)S(1)}, u32[]{:S(2)}, u32[]{:S(2)}) %collective-permute-start.20) | collective-permute-done | bytes 8224 | tf_op jit(solution)/shard_map/ppermute | solution.py:134
  42.9 1.5 %collective-permute-start.22 = (f32[8,256]{1,0:T(8,128)S(1)}, f32[8,256]{1,0:T(8,128)S(1)}, u32[]{:S(2)}, u32[]{:S(2)}) collective-permute-start(f32[8,256]{1,0:T(8,128)S(1)} %get-tuple-element.79), channel_id=1, source_target_pairs={{0,16},{1,17},{2,18},{3,19},{4,20},{5,21},{6,22},{7,23},{8,24},{9,... | collective-permute-start | bytes 24584 | tf_op jit(solution)/shard_map/ppermute | solution.py:134
  44.4 1.2 %collective-permute-done.23.refs_5_ = f32[8,256]{1,0:T(8,128)S(1)} collective-permute-done((f32[8,256]{1,0:T(8,128)S(1)}, f32[8,256]{1,0:T(8,128)S(1)}, u32[]{:S(2)}, u32[]{:S(2)}) %collective-permute-start.23) | collective-permute-done | bytes 8224 | tf_op jit(solution)/shard_map/ppermute | solution.py:134
  48.4 1.5 %collective-permute-start.25 = (f32[8,256]{1,0:T(8,128)S(1)}, f32[8,256]{1,0:T(8,128)S(1)}, u32[]{:S(2)}, u32[]{:S(2)}) collective-permute-start(f32[8,256]{1,0:T(8,128)S(1)} %get-tuple-element.82), channel_id=1, source_target_pairs={{0,16},{1,17},{2,18},{3,19},{4,20},{5,21},{6,22},{7,23},{8,24},{9,... | collective-permute-start | bytes 24584 | tf_op jit(solution)/shard_map/ppermute | solution.py:134
  53.6 1.5 %collective-permute-start.28 = (f32[8,256]{1,0:T(8,128)S(1)}, f32[8,256]{1,0:T(8,128)S(1)}, u32[]{:S(2)}, u32[]{:S(2)}) collective-permute-start(f32[8,256]{1,0:T(8,128)S(1)} %get-tuple-element.86), channel_id=1, source_target_pairs={{0,16},{1,17},{2,18},{3,19},{4,20},{5,21},{6,22},{7,23},{8,24},{9,... | collective-permute-start | bytes 24584 | tf_op jit(solution)/shard_map/ppermute | solution.py:134
  58.8 1.5 %collective-permute-start.31 = (f32[8,256]{1,0:T(8,128)S(1)}, f32[8,256]{1,0:T(8,128)S(1)}, u32[]{:S(2)}, u32[]{:S(2)}) collective-permute-start(f32[8,256]{1,0:T(8,128)S(1)} %get-tuple-element.90), channel_id=1, source_target_pairs={{0,16},{1,17},{2,18},{3,19},{4,20},{5,21},{6,22},{7,23},{8,24},{9,... | collective-permute-start | bytes 24584 | tf_op jit(solution)/shard_map/ppermute | solution.py:134
  64.0 1.5 %collective-permute-start.34 = (f32[8,256]{1,0:T(8,128)S(1)}, f32[8,256]{1,0:T(8,128)S(1)}, u32[]{:S(2)}, u32[]{:S(2)}) collective-permute-start(f32[8,256]{1,0:T(8,128)S(1)} %get-tuple-element.94), channel_id=1, source_target_pairs={{0,16},{1,17},{2,18},{3,19},{4,20},{5,21},{6,22},{7,23},{8,24},{9,... | collective-permute-start | bytes 24584 | tf_op jit(solution)/shard_map/ppermute | solution.py:134
  69.1 1.5 %collective-permute-start.37 = (f32[8,256]{1,0:T(8,128)S(1)}, f32[8,256]{1,0:T(8,128)S(1)}, u32[]{:S(2)}, u32[]{:S(2)}) collective-permute-start(f32[8,256]{1,0:T(8,128)S(1)} %get-tuple-element.98), channel_id=1, source_target_pairs={{0,16},{1,17},{2,18},{3,19},{4,20},{5,21},{6,22},{7,23},{8,24},{9,... | collective-permute-start | bytes 24584 | tf_op jit(solution)/shard_map/ppermute | solution.py:134
  74.3 1.5 %collective-permute-start.40 = (f32[8,256]{1,0:T(8,128)S(1)}, f32[8,256]{1,0:T(8,128)S(1)}, u32[]{:S(2)}, u32[]{:S(2)}) collective-permute-start(f32[8,256]{1,0:T(8,128)S(1)} %get-tuple-element.102), channel_id=1, source_target_pairs={{0,16},{1,17},{2,18},{3,19},{4,20},{5,21},{6,22},{7,23},{8,24},{9,... | collective-permute-start | bytes 24584 | tf_op jit(solution)/shard_map/ppermute | solution.py:134
  79.5 1.5 %collective-permute-start.43 = (f32[8,256]{1,0:T(8,128)S(1)}, f32[8,256]{1,0:T(8,128)S(1)}, u32[]{:S(2)}, u32[]{:S(2)}) collective-permute-start(f32[8,256]{1,0:T(8,128)S(1)} %get-tuple-element.107), channel_id=1, source_target_pairs={{0,16},{1,17},{2,18},{3,19},{4,20},{5,21},{6,22},{7,23},{8,24},{9,... | collective-permute-start | bytes 24584 | tf_op jit(solution)/shard_map/ppermute | solution.py:134
  83.7 3.0 %collective-permute-start.46 = (f32[2,8,256]{2,1,0:T(8,128)S(1)}, f32[2,8,256]{2,1,0:T(8,128)S(1)}, u32[]{:S(2)}, u32[]{:S(2)}) collective-permute-start(f32[2,8,256]{2,1,0:T(8,128)S(1)} %get-tuple-element.111), channel_id=1, source_target_pairs={{0,4},{1,5},{2,6},{3,7},{4,0},{5,1},{6,2},{7,3},{8,12},{9,13},{10,... | collective-permute-start | bytes 49160 | tf_op jit(solution)/shard_map/ppermute | solution.py:134
  (98 shorter events, 51.4 us)
Async XLA Ops:
  2.0 5.3 %collective-permute-start.1 = (f32[2,8,256]{2,1,0:T(8,128)S(1)}, f32[2,8,256]{2,1,0:T(8,128)S(1)}, u32[]{:S(2)}, u32[]{:S(2)}) collective-permute-start(f32[2,8,256]{2,1,0:T(8,128)S(1)} %get-tuple-element.61), channel_id=1, source_target_pairs={{0,2},{1,7},{2,0},{3,5},{4,6},{5,3},{6,4},{7,1},{8,10},{9,15},{10,... | collective-permute-start | bytes 49160 | tf_op jit(solution)/shard_map/ppermute | solution.py:134
  4.8 4.6 %collective-permute-start.2 = (f32[2,8,256]{2,1,0:T(8,128)S(1)}, f32[2,8,256]{2,1,0:T(8,128)S(1)}, u32[]{:S(2)}, u32[]{:S(2)}) collective-permute-start(f32[2,8,256]{2,1,0:T(8,128)S(1)} %get-tuple-element.63), channel_id=1, source_target_pairs={{0,4},{1,5},{2,6},{3,7},{4,0},{5,1},{6,2},{7,3},{8,12},{9,13},{10,... | collective-permute-start | bytes 49160 | tf_op jit(solution)/shard_map/ppermute | solution.py:134
  9.6 3.7 %collective-permute-start.5 = (f32[8,256]{1,0:T(8,128)S(1)}, f32[8,256]{1,0:T(8,128)S(1)}, u32[]{:S(2)}, u32[]{:S(2)}) collective-permute-start(f32[8,256]{1,0:T(8,128)S(1)} %get-tuple-element.67), channel_id=1, source_target_pairs={{0,8},{1,25},{2,10},{3,27},{4,12},{5,29},{6,14},{7,31},{8,0},{9,17... | collective-permute-start | bytes 24584 | tf_op jit(solution)/shard_map/ppermute | solution.py:134
  11.2 3.7 %collective-permute-start.4 = (f32[8,256]{1,0:T(8,128)S(1)}, f32[8,256]{1,0:T(8,128)S(1)}, u32[]{:S(2)}, u32[]{:S(2)}) collective-permute-start(f32[8,256]{1,0:T(8,128)S(1)} %get-tuple-element.67), channel_id=1, source_target_pairs={{0,16},{1,17},{2,18},{3,19},{4,20},{5,21},{6,22},{7,23},{8,24},{9,... | collective-permute-start | bytes 24584 | tf_op jit(solution)/shard_map/ppermute | solution.py:134
  15.4 3.7 %collective-permute-start.8 = (f32[8,256]{1,0:T(8,128)S(1)}, f32[8,256]{1,0:T(8,128)S(1)}, u32[]{:S(2)}, u32[]{:S(2)}) collective-permute-start(f32[8,256]{1,0:T(8,128)S(1)} %get-tuple-element.69), channel_id=1, source_target_pairs={{0,8},{1,25},{2,10},{3,27},{4,12},{5,29},{6,14},{7,31},{8,0},{9,17... | collective-permute-start | bytes 24584 | tf_op jit(solution)/shard_map/ppermute | solution.py:134
  16.9 3.7 %collective-permute-start.7 = (f32[8,256]{1,0:T(8,128)S(1)}, f32[8,256]{1,0:T(8,128)S(1)}, u32[]{:S(2)}, u32[]{:S(2)}) collective-permute-start(f32[8,256]{1,0:T(8,128)S(1)} %get-tuple-element.69), channel_id=1, source_target_pairs={{0,16},{1,17},{2,18},{3,19},{4,20},{5,21},{6,22},{7,23},{8,24},{9,... | collective-permute-start | bytes 24584 | tf_op jit(solution)/shard_map/ppermute | solution.py:134
  21.0 3.7 %collective-permute-start.11 = (f32[8,256]{1,0:T(8,128)S(1)}, f32[8,256]{1,0:T(8,128)S(1)}, u32[]{:S(2)}, u32[]{:S(2)}) collective-permute-start(f32[8,256]{1,0:T(8,128)S(1)} %get-tuple-element.71), channel_id=1, source_target_pairs={{0,8},{1,25},{2,10},{3,27},{4,12},{5,29},{6,14},{7,31},{8,0},{9,17... | collective-permute-start | bytes 24584 | tf_op jit(solution)/shard_map/ppermute | solution.py:134
  22.1 3.7 %collective-permute-start.10 = (f32[8,256]{1,0:T(8,128)S(1)}, f32[8,256]{1,0:T(8,128)S(1)}, u32[]{:S(2)}, u32[]{:S(2)}) collective-permute-start(f32[8,256]{1,0:T(8,128)S(1)} %get-tuple-element.71), channel_id=1, source_target_pairs={{0,16},{1,17},{2,18},{3,19},{4,20},{5,21},{6,22},{7,23},{8,24},{9,... | collective-permute-start | bytes 24584 | tf_op jit(solution)/shard_map/ppermute | solution.py:134
  26.2 3.7 %collective-permute-start.14 = (f32[8,256]{1,0:T(8,128)S(1)}, f32[8,256]{1,0:T(8,128)S(1)}, u32[]{:S(2)}, u32[]{:S(2)}) collective-permute-start(f32[8,256]{1,0:T(8,128)S(1)} %get-tuple-element.73), channel_id=1, source_target_pairs={{0,8},{1,25},{2,10},{3,27},{4,12},{5,29},{6,14},{7,31},{8,0},{9,17... | collective-permute-start | bytes 24584 | tf_op jit(solution)/shard_map/ppermute | solution.py:134
  31.5 3.7 %collective-permute-start.17 = (f32[8,256]{1,0:T(8,128)S(1)}, f32[8,256]{1,0:T(8,128)S(1)}, u32[]{:S(2)}, u32[]{:S(2)}) collective-permute-start(f32[8,256]{1,0:T(8,128)S(1)} %get-tuple-element.75), channel_id=1, source_target_pairs={{0,8},{1,25},{2,10},{3,27},{4,12},{5,29},{6,14},{7,31},{8,0},{9,17... | collective-permute-start | bytes 24584 | tf_op jit(solution)/shard_map/ppermute | solution.py:134
  36.7 3.7 %collective-permute-start.20 = (f32[8,256]{1,0:T(8,128)S(1)}, f32[8,256]{1,0:T(8,128)S(1)}, u32[]{:S(2)}, u32[]{:S(2)}) collective-permute-start(f32[8,256]{1,0:T(8,128)S(1)} %get-tuple-element.77), channel_id=1, source_target_pairs={{0,8},{1,25},{2,10},{3,27},{4,12},{5,29},{6,14},{7,31},{8,0},{9,17... | collective-permute-start | bytes 24584 | tf_op jit(solution)/shard_map/ppermute | solution.py:134
  41.9 3.7 %collective-permute-start.23 = (f32[8,256]{1,0:T(8,128)S(1)}, f32[8,256]{1,0:T(8,128)S(1)}, u32[]{:S(2)}, u32[]{:S(2)}) collective-permute-start(f32[8,256]{1,0:T(8,128)S(1)} %get-tuple-element.79), channel_id=1, source_target_pairs={{0,8},{1,25},{2,10},{3,27},{4,12},{5,29},{6,14},{7,31},{8,0},{9,17... | collective-permute-start | bytes 24584 | tf_op jit(solution)/shard_map/ppermute | solution.py:134
  42.9 3.7 %collective-permute-start.22 = (f32[8,256]{1,0:T(8,128)S(1)}, f32[8,256]{1,0:T(8,128)S(1)}, u32[]{:S(2)}, u32[]{:S(2)}) collective-permute-start(f32[8,256]{1,0:T(8,128)S(1)} %get-tuple-element.79), channel_id=1, source_target_pairs={{0,16},{1,17},{2,18},{3,19},{4,20},{5,21},{6,22},{7,23},{8,24},{9,... | collective-permute-start | bytes 24584 | tf_op jit(solution)/shard_map/ppermute | solution.py:134
  47.4 3.7 %collective-permute-start.26 = (f32[8,256]{1,0:T(8,128)S(1)}, f32[8,256]{1,0:T(8,128)S(1)}, u32[]{:S(2)}, u32[]{:S(2)}) collective-permute-start(f32[8,256]{1,0:T(8,128)S(1)} %get-tuple-element.83), channel_id=1, source_target_pairs={{0,8},{1,25},{2,10},{3,27},{4,12},{5,29},{6,14},{7,31},{8,0},{9,17... | collective-permute-start | bytes 24584 | tf_op jit(solution)/shard_map/ppermute | solution.py:134
  48.4 3.7 %collective-permute-start.25 = (f32[8,256]{1,0:T(8,128)S(1)}, f32[8,256]{1,0:T(8,128)S(1)}, u32[]{:S(2)}, u32[]{:S(2)}) collective-permute-start(f32[8,256]{1,0:T(8,128)S(1)} %get-tuple-element.82), channel_id=1, source_target_pairs={{0,16},{1,17},{2,18},{3,19},{4,20},{5,21},{6,22},{7,23},{8,24},{9,... | collective-permute-start | bytes 24584 | tf_op jit(solution)/shard_map/ppermute | solution.py:134
  52.6 3.7 %collective-permute-start.29 = (f32[8,256]{1,0:T(8,128)S(1)}, f32[8,256]{1,0:T(8,128)S(1)}, u32[]{:S(2)}, u32[]{:S(2)}) collective-permute-start(f32[8,256]{1,0:T(8,128)S(1)} %get-tuple-element.87), channel_id=1, source_target_pairs={{0,8},{1,25},{2,10},{3,27},{4,12},{5,29},{6,14},{7,31},{8,0},{9,17... | collective-permute-start | bytes 24584 | tf_op jit(solution)/shard_map/ppermute | solution.py:134
  53.6 3.7 %collective-permute-start.28 = (f32[8,256]{1,0:T(8,128)S(1)}, f32[8,256]{1,0:T(8,128)S(1)}, u32[]{:S(2)}, u32[]{:S(2)}) collective-permute-start(f32[8,256]{1,0:T(8,128)S(1)} %get-tuple-element.86), channel_id=1, source_target_pairs={{0,16},{1,17},{2,18},{3,19},{4,20},{5,21},{6,22},{7,23},{8,24},{9,... | collective-permute-start | bytes 24584 | tf_op jit(solution)/shard_map/ppermute | solution.py:134
  57.7 3.7 %collective-permute-start.32 = (f32[8,256]{1,0:T(8,128)S(1)}, f32[8,256]{1,0:T(8,128)S(1)}, u32[]{:S(2)}, u32[]{:S(2)}) collective-permute-start(f32[8,256]{1,0:T(8,128)S(1)} %get-tuple-element.91), channel_id=1, source_target_pairs={{0,8},{1,25},{2,10},{3,27},{4,12},{5,29},{6,14},{7,31},{8,0},{9,17... | collective-permute-start | bytes 24584 | tf_op jit(solution)/shard_map/ppermute | solution.py:134
  62.9 3.7 %collective-permute-start.35 = (f32[8,256]{1,0:T(8,128)S(1)}, f32[8,256]{1,0:T(8,128)S(1)}, u32[]{:S(2)}, u32[]{:S(2)}) collective-permute-start(f32[8,256]{1,0:T(8,128)S(1)} %get-tuple-element.95), channel_id=1, source_target_pairs={{0,8},{1,25},{2,10},{3,27},{4,12},{5,29},{6,14},{7,31},{8,0},{9,17... | collective-permute-start | bytes 24584 | tf_op jit(solution)/shard_map/ppermute | solution.py:134
  68.1 3.7 %collective-permute-start.38 = (f32[8,256]{1,0:T(8,128)S(1)}, f32[8,256]{1,0:T(8,128)S(1)}, u32[]{:S(2)}, u32[]{:S(2)}) collective-permute-start(f32[8,256]{1,0:T(8,128)S(1)} %get-tuple-element.99), channel_id=1, source_target_pairs={{0,8},{1,25},{2,10},{3,27},{4,12},{5,29},{6,14},{7,31},{8,0},{9,17... | collective-permute-start | bytes 24584 | tf_op jit(solution)/shard_map/ppermute | solution.py:134
  73.3 3.7 %collective-permute-start.41 = (f32[8,256]{1,0:T(8,128)S(1)}, f32[8,256]{1,0:T(8,128)S(1)}, u32[]{:S(2)}, u32[]{:S(2)}) collective-permute-start(f32[8,256]{1,0:T(8,128)S(1)} %get-tuple-element.103), channel_id=1, source_target_pairs={{0,8},{1,25},{2,10},{3,27},{4,12},{5,29},{6,14},{7,31},{8,0},{9,17... | collective-permute-start | bytes 24584 | tf_op jit(solution)/shard_map/ppermute | solution.py:134
  78.5 3.7 %collective-permute-start.44 = (f32[8,256]{1,0:T(8,128)S(1)}, f32[8,256]{1,0:T(8,128)S(1)}, u32[]{:S(2)}, u32[]{:S(2)}) collective-permute-start(f32[8,256]{1,0:T(8,128)S(1)} %get-tuple-element.108), channel_id=1, source_target_pairs={{0,8},{1,25},{2,10},{3,27},{4,12},{5,29},{6,14},{7,31},{8,0},{9,17... | collective-permute-start | bytes 24584 | tf_op jit(solution)/shard_map/ppermute | solution.py:134
  83.6 3.8 %collective-permute-start.47 = (f32[2,8,256]{2,1,0:T(8,128)S(1)}, f32[2,8,256]{2,1,0:T(8,128)S(1)}, u32[]{:S(2)}, u32[]{:S(2)}) collective-permute-start(f32[2,8,256]{2,1,0:T(8,128)S(1)} %get-tuple-element.112), channel_id=1, source_target_pairs={{0,2},{1,7},{2,0},{3,5},{4,6},{5,3},{6,4},{7,1},{8,10},{9,15},{10,... | collective-permute-start | bytes 49160 | tf_op jit(solution)/shard_map/ppermute | solution.py:134
  83.7 4.9 %collective-permute-start.46 = (f32[2,8,256]{2,1,0:T(8,128)S(1)}, f32[2,8,256]{2,1,0:T(8,128)S(1)}, u32[]{:S(2)}, u32[]{:S(2)}) collective-permute-start(f32[2,8,256]{2,1,0:T(8,128)S(1)} %get-tuple-element.111), channel_id=1, source_target_pairs={{0,4},{1,5},{2,6},{3,7},{4,0},{5,1},{6,2},{7,3},{8,12},{9,13},{10,... | collective-permute-start | bytes 49160 | tf_op jit(solution)/shard_map/ppermute | solution.py:134
  (27 other events, 93.6 us)

commit v6 on v5

--- a/solution.py
+++ b/solution.py
@@ -209,6 +209,14 @@
     def lower(r, level, k):
         return r.lower_1[k] if level == 1 else r.lowers[level - 1, 0, k]
 
+    def turn_body(level):
+        def body(r):
+            r.turned[0] = r.inverses[level, 0].T
+            for k in range(blocks):
+                r.turned[1 + k] = r.lowers[level - 1, 0, k].T
+
+        return body
+
     def begin_body(r):
         r.pieces[CORES * r.z + r.core] = r.packed[chip_rows(r.z)]
         r.pieces[CORES * r.z + 1 - r.core] = r.other[chip_rows(r.z)]
@@ -230,8 +238,9 @@
                 r.finished[(level - 1) * owners + owner] = getattr(r, name)[...]
             total = r.source[level]
             for k in range(blocks):
-                total = total - times(r.finished[column_of(r, level, k)], lower(r, level, k), True)
-            answer = times(total, inverse(r, level), True)
+                block = r.turned[1 + k] if level > 1 else lower(r, level, k)
+                total = total - times(r.finished[column_of(r, level, k)], block, level == 1)
+            answer = times(total, r.turned[0] if level > 1 else inverse(r, level), level == 1)
             r.finished[level * owners + r.row] = answer
             if level < levels - 1:
                 r.solved[...] = answer
@@ -245,10 +254,15 @@
     def backward(r, level, source):
         answer = times(source, inverse(r, level), False)
         r.answers[level] = answer
+        products = [times(answer, lower(r, level, k), False) for k in range(blocks)]
+        for name, owner in outgoing(r, "row"):
+            row = (level - 1) * owners + owner
+            total = r.accumulated[row]
+            for k in range(blocks):
+                total = total + jnp.where(column_of(r, level, k) == row, products[k], 0.0)
+            getattr(r, name)[...] = total
         for k in range(blocks):
-            r.accumulated[column_of(r, level, k)] += times(answer, lower(r, level, k), False)
-        for name, owner in outgoing(r, "row"):
-            getattr(r, name)[...] = r.accumulated[(level - 1) * owners + owner]
+            r.accumulated[column_of(r, level, k)] += products[k]
 
     def source_of(r, level):
         row = level * owners + r.row
@@ -309,9 +323,15 @@
         last = level == levels - 1
         arrived = exchange("row", [solved] * len(row_routes[0]), solved)
         held.setdefault(level, {"inverses": diag_inverse, "lowers": lower_blocks})
+        turned = {}
+        if level > 1:
+            turned = call(
+                f"turn_{level}", turn_body(level), {**held[level], "after": solved},
+                makes={"turned": VMEM((1 + blocks, size, size), BF16)},
+            )
         state = call(
             f"forward_{level}", forward_body(level),
-            {"lists": lists, **held[level], "source": source, **arrived},
+            {"lists": lists, **held[level], **turned, "source": source, **arrived},
             {"finished": finished},
             {"accumulated": all_rows, "answers": own_rows, **to_owners} if last else {"solved": rows},
         )

time: 90.1 us -> 89.6 us (level)
  waiting for transfers between devices: 33.8 us -> 32.6 us
    ppermute x32, waiting for transfers between devices: 30.9 us -> 29.8 us  [send(): return lax.ppermute(array, ('row', 'col'), steps)]
    pallas_call x20 -> x26, Pallas kernels: 8.21 us -> 8.97 us  [call(): pl.pallas_call(kernel, in_specs=[spec(key) for key in in_names], out_spec...]
  transfers between devices with their start and end apart: 49 -> 49, of which waited for: 45 -> 45; matrix products, arithmetic and copies ran while one was open for 0% -> 0% of each run, Pallas kernels for 3% -> 4%
where the time goes in v6:
time: 89.6 us; the launch traced here: 89.4 us
  starting transfers between devices  47.7 us (53%)
  waiting for transfers between devices  32.6 us (36%)
  Pallas kernels  8.97 us (10%)
    ppermute x32, starting transfers between devices, send(): return lax.ppermute(array, ('row', 'col'), steps)  44.5 us
    ppermute x32, waiting for transfers between devices, send(): return lax.ppermute(array, ('row', 'col'), steps)  29.8 us
    pallas_call x26, Pallas kernels, call(): pl.pallas_call(kernel, in_specs=[spec(key) for key in in_names], out_spec...  8.97 us
    ppermute x17, starting transfers between devices, swap(): return lax.ppermute(array, 'col', [(c, c ^ 1) for c in range(columns)])  3.17 us
    ppermute x17, waiting for transfers between devices, swap(): return lax.ppermute(array, 'col', [(c, c ^ 1) for c in range(columns)])  2.76 us
  transfers between devices with their start and end apart: 49, of which 45 were waited for; matrix products, arithmetic and copies ran while one was open for 0% of the time, Pallas kernels for 4%

profile of v6, /device:TPU:0, one launch (start us, length us, event | category | flops | bytes accessed | tf_op | source)
XLA Modules:
  0.0 89.4 jit_solution(13101947560835741831)
XLA Ops:
  0.5 1.4 %pack.1 = (f32[32,256]{1,0:T(8,128)S(1)}, bf16[256,256]{1,0:T(8,128)(2,1)S(1)}, bf16[256,256]{1,0:T(8,128)(2,1)S(1)}, bf16[3,256,256]{2,1,0:T(8,128)(2,1)S(1)}) custom-call(f32[8,1,32,32]{3,2,1,0:T(8,128)} %refs_0_.7, bf16[8,1,256,256]{3,2,1,0:T(8,128)(2,1)} %refs_1_.35, bf16[7,1,3,256,256]{4,3,2,1,0:T(8,128)(2,1)} %refs_2_.23), custom_call_target="tpu_custom_call" | custom-call | tf_op jit(solution)/shard_map/pack/pallas_call | solution.py:93
  2.0 2.7 %collective-permute-start.1 = (f32[2,8,256]{2,1,0:T(8,128)S(1)}, f32[2,8,256]{2,1,0:T(8,128)S(1)}, u32[]{:S(2)}, u32[]{:S(2)}) collective-permute-start(f32[2,8,256]{2,1,0:T(8,128)S(1)} %get-tuple-element.61), channel_id=1, source_target_pairs={{0,2},{1,7},{2,0},{3,5},{4,6},{5,3},{6,4},{7,1},{8,10},{9,15},{10,... | collective-permute-start | bytes 49160 | tf_op jit(solution)/shard_map/ppermute | solution.py:134
  4.8 2.6 %collective-permute-start.2 = (f32[2,8,256]{2,1,0:T(8,128)S(1)}, f32[2,8,256]{2,1,0:T(8,128)S(1)}, u32[]{:S(2)}, u32[]{:S(2)}) collective-permute-start(f32[2,8,256]{2,1,0:T(8,128)S(1)} %get-tuple-element.65), channel_id=1, source_target_pairs={{0,4},{1,5},{2,6},{3,7},{4,0},{5,1},{6,2},{7,3},{8,12},{9,13},{10,... | collective-permute-start | bytes 49160 | tf_op jit(solution)/shard_map/ppermute | solution.py:134
  9.6 1.6 %collective-permute-start.5 = (f32[8,256]{1,0:T(8,128)S(1)}, f32[8,256]{1,0:T(8,128)S(1)}, u32[]{:S(2)}, u32[]{:S(2)}) collective-permute-start(f32[8,256]{1,0:T(8,128)S(1)} %get-tuple-element.67), channel_id=1, source_target_pairs={{0,8},{1,25},{2,10},{3,27},{4,12},{5,29},{6,14},{7,31},{8,0},{9,17... | collective-permute-start | bytes 24584 | tf_op jit(solution)/shard_map/ppermute | solution.py:134
  11.2 1.5 %collective-permute-start.4 = (f32[8,256]{1,0:T(8,128)S(1)}, f32[8,256]{1,0:T(8,128)S(1)}, u32[]{:S(2)}, u32[]{:S(2)}) collective-permute-start(f32[8,256]{1,0:T(8,128)S(1)} %get-tuple-element.67), channel_id=1, source_target_pairs={{0,16},{1,17},{2,18},{3,19},{4,20},{5,21},{6,22},{7,23},{8,24},{9,... | collective-permute-start | bytes 24584 | tf_op jit(solution)/shard_map/ppermute | solution.py:134
  15.4 1.5 %collective-permute-start.8 = (f32[8,256]{1,0:T(8,128)S(1)}, f32[8,256]{1,0:T(8,128)S(1)}, u32[]{:S(2)}, u32[]{:S(2)}) collective-permute-start(f32[8,256]{1,0:T(8,128)S(1)} %get-tuple-element.69.refs_2_), channel_id=1, source_target_pairs={{0,8},{1,25},{2,10},{3,27},{4,12},{5,29},{6,14},{7,31},{8,0},{9,17... | collective-permute-start | bytes 24584 | tf_op jit(solution)/shard_map/ppermute | solution.py:134
  16.9 1.5 %collective-permute-start.7 = (f32[8,256]{1,0:T(8,128)S(1)}, f32[8,256]{1,0:T(8,128)S(1)}, u32[]{:S(2)}, u32[]{:S(2)}) collective-permute-start(f32[8,256]{1,0:T(8,128)S(1)} %get-tuple-element.69.refs_2_), channel_id=1, source_target_pairs={{0,16},{1,17},{2,18},{3,19},{4,20},{5,21},{6,22},{7,23},{8,24},{9,... | collective-permute-start | bytes 24584 | tf_op jit(solution)/shard_map/ppermute | solution.py:134
  19.4 1.2 %collective-permute-done.7.refs_5_ = f32[8,256]{1,0:T(8,128)S(1)} collective-permute-done((f32[8,256]{1,0:T(8,128)S(1)}, f32[8,256]{1,0:T(8,128)S(1)}, u32[]{:S(2)}, u32[]{:S(2)}) %collective-permute-start.7) | collective-permute-done | bytes 8224 | tf_op jit(solution)/shard_map/ppermute | solution.py:134
  22.0 1.5 %collective-permute-start.10 = (f32[8,256]{1,0:T(8,128)S(1)}, f32[8,256]{1,0:T(8,128)S(1)}, u32[]{:S(2)}, u32[]{:S(2)}) collective-permute-start(f32[8,256]{1,0:T(8,128)S(1)} %get-tuple-element.71.refs_2_), channel_id=1, source_target_pairs={{0,16},{1,17},{2,18},{3,19},{4,20},{5,21},{6,22},{7,23},{8,24},{9,... | collective-permute-start | bytes 24584 | tf_op jit(solution)/shard_map/ppermute | solution.py:134
  27.2 1.5 %collective-permute-start.13 = (f32[8,256]{1,0:T(8,128)S(1)}, f32[8,256]{1,0:T(8,128)S(1)}, u32[]{:S(2)}, u32[]{:S(2)}) collective-permute-start(f32[8,256]{1,0:T(8,128)S(1)} %get-tuple-element.73.refs_2_), channel_id=1, source_target_pairs={{0,16},{1,17},{2,18},{3,19},{4,20},{5,21},{6,22},{7,23},{8,24},{9,... | collective-permute-start | bytes 24584 | tf_op jit(solution)/shard_map/ppermute | solution.py:134
  32.3 1.5 %collective-permute-start.16 = (f32[8,256]{1,0:T(8,128)S(1)}, f32[8,256]{1,0:T(8,128)S(1)}, u32[]{:S(2)}, u32[]{:S(2)}) collective-permute-start(f32[8,256]{1,0:T(8,128)S(1)} %get-tuple-element.75.refs_2_), channel_id=1, source_target_pairs={{0,16},{1,17},{2,18},{3,19},{4,20},{5,21},{6,22},{7,23},{8,24},{9,... | collective-permute-start | bytes 24584 | tf_op jit(solution)/shard_map/ppermute | solution.py:134
  37.4 1.5 %collective-permute-start.19 = (f32[8,256]{1,0:T(8,128)S(1)}, f32[8,256]{1,0:T(8,128)S(1)}, u32[]{:S(2)}, u32[]{:S(2)}) collective-permute-start(f32[8,256]{1,0:T(8,128)S(1)} %get-tuple-element.77.refs_2_), channel_id=1, source_target_pairs={{0,16},{1,17},{2,18},{3,19},{4,20},{5,21},{6,22},{7,23},{8,24},{9,... | collective-permute-start | bytes 24584 | tf_op jit(solution)/shard_map/ppermute | solution.py:134
  42.6 1.5 %collective-permute-start.22 = (f32[8,256]{1,0:T(8,128)S(1)}, f32[8,256]{1,0:T(8,128)S(1)}, u32[]{:S(2)}, u32[]{:S(2)}) collective-permute-start(f32[8,256]{1,0:T(8,128)S(1)} %get-tuple-element.79.refs_2_), channel_id=1, source_target_pairs={{0,16},{1,17},{2,18},{3,19},{4,20},{5,21},{6,22},{7,23},{8,24},{9,... | collective-permute-start | bytes 24584 | tf_op jit(solution)/shard_map/ppermute | solution.py:134
  44.0 1.2 %collective-permute-done.23.refs_6_ = f32[8,256]{1,0:T(8,128)S(1)} collective-permute-done((f32[8,256]{1,0:T(8,128)S(1)}, f32[8,256]{1,0:T(8,128)S(1)}, u32[]{:S(2)}, u32[]{:S(2)}) %collective-permute-start.23) | collective-permute-done | bytes 8224 | tf_op jit(solution)/shard_map/ppermute | solution.py:134
  48.0 1.5 %collective-permute-start.25 = (f32[8,256]{1,0:T(8,128)S(1)}, f32[8,256]{1,0:T(8,128)S(1)}, u32[]{:S(2)}, u32[]{:S(2)}) collective-permute-start(f32[8,256]{1,0:T(8,128)S(1)} %get-tuple-element.82), channel_id=1, source_target_pairs={{0,16},{1,17},{2,18},{3,19},{4,20},{5,21},{6,22},{7,23},{8,24},{9,... | collective-permute-start | bytes 24584 | tf_op jit(solution)/shard_map/ppermute | solution.py:134
  49.5 1.2 %collective-permute-done.26.refs_5_ = f32[8,256]{1,0:T(8,128)S(1)} collective-permute-done((f32[8,256]{1,0:T(8,128)S(1)}, f32[8,256]{1,0:T(8,128)S(1)}, u32[]{:S(2)}, u32[]{:S(2)}) %collective-permute-start.26) | collective-permute-done | bytes 8224 | tf_op jit(solution)/shard_map/ppermute | solution.py:134
  53.2 1.5 %collective-permute-start.28 = (f32[8,256]{1,0:T(8,128)S(1)}, f32[8,256]{1,0:T(8,128)S(1)}, u32[]{:S(2)}, u32[]{:S(2)}) collective-permute-start(f32[8,256]{1,0:T(8,128)S(1)} %get-tuple-element.86), channel_id=1, source_target_pairs={{0,16},{1,17},{2,18},{3,19},{4,20},{5,21},{6,22},{7,23},{8,24},{9,... | collective-permute-start | bytes 24584 | tf_op jit(solution)/shard_map/ppermute | solution.py:134
  54.7 1.2 %collective-permute-done.29.refs_5_ = f32[8,256]{1,0:T(8,128)S(1)} collective-permute-done((f32[8,256]{1,0:T(8,128)S(1)}, f32[8,256]{1,0:T(8,128)S(1)}, u32[]{:S(2)}, u32[]{:S(2)}) %collective-permute-start.29) | collective-permute-done | bytes 8224 | tf_op jit(solution)/shard_map/ppermute | solution.py:134
  58.4 1.5 %collective-permute-start.31 = (f32[8,256]{1,0:T(8,128)S(1)}, f32[8,256]{1,0:T(8,128)S(1)}, u32[]{:S(2)}, u32[]{:S(2)}) collective-permute-start(f32[8,256]{1,0:T(8,128)S(1)} %get-tuple-element.90), channel_id=1, source_target_pairs={{0,16},{1,17},{2,18},{3,19},{4,20},{5,21},{6,22},{7,23},{8,24},{9,... | collective-permute-start | bytes 24584 | tf_op jit(solution)/shard_map/ppermute | solution.py:134
  63.6 1.5 %collective-permute-start.34 = (f32[8,256]{1,0:T(8,128)S(1)}, f32[8,256]{1,0:T(8,128)S(1)}, u32[]{:S(2)}, u32[]{:S(2)}) collective-permute-start(f32[8,256]{1,0:T(8,128)S(1)} %get-tuple-element.94), channel_id=1, source_target_pairs={{0,16},{1,17},{2,18},{3,19},{4,20},{5,21},{6,22},{7,23},{8,24},{9,... | collective-permute-start | bytes 24584 | tf_op jit(solution)/shard_map/ppermute | solution.py:134
  68.7 1.5 %collective-permute-start.37 = (f32[8,256]{1,0:T(8,128)S(1)}, f32[8,256]{1,0:T(8,128)S(1)}, u32[]{:S(2)}, u32[]{:S(2)}) collective-permute-start(f32[8,256]{1,0:T(8,128)S(1)} %get-tuple-element.98), channel_id=1, source_target_pairs={{0,16},{1,17},{2,18},{3,19},{4,20},{5,21},{6,22},{7,23},{8,24},{9,... | collective-permute-start | bytes 24584 | tf_op jit(solution)/shard_map/ppermute | solution.py:134
  73.9 1.5 %collective-permute-start.40 = (f32[8,256]{1,0:T(8,128)S(1)}, f32[8,256]{1,0:T(8,128)S(1)}, u32[]{:S(2)}, u32[]{:S(2)}) collective-permute-start(f32[8,256]{1,0:T(8,128)S(1)} %get-tuple-element.102), channel_id=1, source_target_pairs={{0,16},{1,17},{2,18},{3,19},{4,20},{5,21},{6,22},{7,23},{8,24},{9,... | collective-permute-start | bytes 24584 | tf_op jit(solution)/shard_map/ppermute | solution.py:134
  79.1 1.5 %collective-permute-start.43 = (f32[8,256]{1,0:T(8,128)S(1)}, f32[8,256]{1,0:T(8,128)S(1)}, u32[]{:S(2)}, u32[]{:S(2)}) collective-permute-start(f32[8,256]{1,0:T(8,128)S(1)} %get-tuple-element.107), channel_id=1, source_target_pairs={{0,16},{1,17},{2,18},{3,19},{4,20},{5,21},{6,22},{7,23},{8,24},{9,... | collective-permute-start | bytes 24584 | tf_op jit(solution)/shard_map/ppermute | solution.py:134
  83.3 3.0 %collective-permute-start.46 = (f32[2,8,256]{2,1,0:T(8,128)S(1)}, f32[2,8,256]{2,1,0:T(8,128)S(1)}, u32[]{:S(2)}, u32[]{:S(2)}) collective-permute-start(f32[2,8,256]{2,1,0:T(8,128)S(1)} %get-tuple-element.111), channel_id=1, source_target_pairs={{0,4},{1,5},{2,6},{3,7},{4,0},{5,1},{6,2},{7,3},{8,12},{9,13},{10,... | collective-permute-start | bytes 49160 | tf_op jit(solution)/shard_map/ppermute | solution.py:134
  (104 shorter events, 51.1 us)
Async XLA Ops:
  2.0 5.3 %collective-permute-start.1 = (f32[2,8,256]{2,1,0:T(8,128)S(1)}, f32[2,8,256]{2,1,0:T(8,128)S(1)}, u32[]{:S(2)}, u32[]{:S(2)}) collective-permute-start(f32[2,8,256]{2,1,0:T(8,128)S(1)} %get-tuple-element.61), channel_id=1, source_target_pairs={{0,2},{1,7},{2,0},{3,5},{4,6},{5,3},{6,4},{7,1},{8,10},{9,15},{10,... | collective-permute-start | bytes 49160 | tf_op jit(solution)/shard_map/ppermute | solution.py:134
  4.8 4.6 %collective-permute-start.2 = (f32[2,8,256]{2,1,0:T(8,128)S(1)}, f32[2,8,256]{2,1,0:T(8,128)S(1)}, u32[]{:S(2)}, u32[]{:S(2)}) collective-permute-start(f32[2,8,256]{2,1,0:T(8,128)S(1)} %get-tuple-element.65), channel_id=1, source_target_pairs={{0,4},{1,5},{2,6},{3,7},{4,0},{5,1},{6,2},{7,3},{8,12},{9,13},{10,... | collective-permute-start | bytes 49160 | tf_op jit(solution)/shard_map/ppermute | solution.py:134
  9.6 3.7 %collective-permute-start.5 = (f32[8,256]{1,0:T(8,128)S(1)}, f32[8,256]{1,0:T(8,128)S(1)}, u32[]{:S(2)}, u32[]{:S(2)}) collective-permute-start(f32[8,256]{1,0:T(8,128)S(1)} %get-tuple-element.67), channel_id=1, source_target_pairs={{0,8},{1,25},{2,10},{3,27},{4,12},{5,29},{6,14},{7,31},{8,0},{9,17... | collective-permute-start | bytes 24584 | tf_op jit(solution)/shard_map/ppermute | solution.py:134
  15.4 3.7 %collective-permute-start.8 = (f32[8,256]{1,0:T(8,128)S(1)}, f32[8,256]{1,0:T(8,128)S(1)}, u32[]{:S(2)}, u32[]{:S(2)}) collective-permute-start(f32[8,256]{1,0:T(8,128)S(1)} %get-tuple-element.69.refs_2_), channel_id=1, source_target_pairs={{0,8},{1,25},{2,10},{3,27},{4,12},{5,29},{6,14},{7,31},{8,0},{9,17... | collective-permute-start | bytes 24584 | tf_op jit(solution)/shard_map/ppermute | solution.py:134
  16.9 3.7 %collective-permute-start.7 = (f32[8,256]{1,0:T(8,128)S(1)}, f32[8,256]{1,0:T(8,128)S(1)}, u32[]{:S(2)}, u32[]{:S(2)}) collective-permute-start(f32[8,256]{1,0:T(8,128)S(1)} %get-tuple-element.69.refs_2_), channel_id=1, source_target_pairs={{0,16},{1,17},{2,18},{3,19},{4,20},{5,21},{6,22},{7,23},{8,24},{9,... | collective-permute-start | bytes 24584 | tf_op jit(solution)/shard_map/ppermute | solution.py:134
  20.9 3.7 %collective-permute-start.11 = (f32[8,256]{1,0:T(8,128)S(1)}, f32[8,256]{1,0:T(8,128)S(1)}, u32[]{:S(2)}, u32[]{:S(2)}) collective-permute-start(f32[8,256]{1,0:T(8,128)S(1)} %get-tuple-element.71.refs_2_), channel_id=1, source_target_pairs={{0,8},{1,25},{2,10},{3,27},{4,12},{5,29},{6,14},{7,31},{8,0},{9,17... | collective-permute-start | bytes 24584 | tf_op jit(solution)/shard_map/ppermute | solution.py:134
  22.0 3.7 %collective-permute-start.10 = (f32[8,256]{1,0:T(8,128)S(1)}, f32[8,256]{1,0:T(8,128)S(1)}, u32[]{:S(2)}, u32[]{:S(2)}) collective-permute-start(f32[8,256]{1,0:T(8,128)S(1)} %get-tuple-element.71.refs_2_), channel_id=1, source_target_pairs={{0,16},{1,17},{2,18},{3,19},{4,20},{5,21},{6,22},{7,23},{8,24},{9,... | collective-permute-start | bytes 24584 | tf_op jit(solution)/shard_map/ppermute | solution.py:134
  26.1 3.7 %collective-permute-start.14 = (f32[8,256]{1,0:T(8,128)S(1)}, f32[8,256]{1,0:T(8,128)S(1)}, u32[]{:S(2)}, u32[]{:S(2)}) collective-permute-start(f32[8,256]{1,0:T(8,128)S(1)} %get-tuple-element.73.refs_2_), channel_id=1, source_target_pairs={{0,8},{1,25},{2,10},{3,27},{4,12},{5,29},{6,14},{7,31},{8,0},{9,17... | collective-permute-start | bytes 24584 | tf_op jit(solution)/shard_map/ppermute | solution.py:134
  31.3 3.7 %collective-permute-start.17 = (f32[8,256]{1,0:T(8,128)S(1)}, f32[8,256]{1,0:T(8,128)S(1)}, u32[]{:S(2)}, u32[]{:S(2)}) collective-permute-start(f32[8,256]{1,0:T(8,128)S(1)} %get-tuple-element.75.refs_2_), channel_id=1, source_target_pairs={{0,8},{1,25},{2,10},{3,27},{4,12},{5,29},{6,14},{7,31},{8,0},{9,17... | collective-permute-start | bytes 24584 | tf_op jit(solution)/shard_map/ppermute | solution.py:134
  32.3 3.7 %collective-permute-start.16 = (f32[8,256]{1,0:T(8,128)S(1)}, f32[8,256]{1,0:T(8,128)S(1)}, u32[]{:S(2)}, u32[]{:S(2)}) collective-permute-start(f32[8,256]{1,0:T(8,128)S(1)} %get-tuple-element.75.refs_2_), channel_id=1, source_target_pairs={{0,16},{1,17},{2,18},{3,19},{4,20},{5,21},{6,22},{7,23},{8,24},{9,... | collective-permute-start | bytes 24584 | tf_op jit(solution)/shard_map/ppermute | solution.py:134
  36.4 3.7 %collective-permute-start.20 = (f32[8,256]{1,0:T(8,128)S(1)}, f32[8,256]{1,0:T(8,128)S(1)}, u32[]{:S(2)}, u32[]{:S(2)}) collective-permute-start(f32[8,256]{1,0:T(8,128)S(1)} %get-tuple-element.77.refs_2_), channel_id=1, source_target_pairs={{0,8},{1,25},{2,10},{3,27},{4,12},{5,29},{6,14},{7,31},{8,0},{9,17... | collective-permute-start | bytes 24584 | tf_op jit(solution)/shard_map/ppermute | solution.py:134
  41.6 3.7 %collective-permute-start.23 = (f32[8,256]{1,0:T(8,128)S(1)}, f32[8,256]{1,0:T(8,128)S(1)}, u32[]{:S(2)}, u32[]{:S(2)}) collective-permute-start(f32[8,256]{1,0:T(8,128)S(1)} %get-tuple-element.79.refs_2_), channel_id=1, source_target_pairs={{0,8},{1,25},{2,10},{3,27},{4,12},{5,29},{6,14},{7,31},{8,0},{9,17... | collective-permute-start | bytes 24584 | tf_op jit(solution)/shard_map/ppermute | solution.py:134
  47.0 3.7 %collective-permute-start.26 = (f32[8,256]{1,0:T(8,128)S(1)}, f32[8,256]{1,0:T(8,128)S(1)}, u32[]{:S(2)}, u32[]{:S(2)}) collective-permute-start(f32[8,256]{1,0:T(8,128)S(1)} %get-tuple-element.83), channel_id=1, source_target_pairs={{0,8},{1,25},{2,10},{3,27},{4,12},{5,29},{6,14},{7,31},{8,0},{9,17... | collective-permute-start | bytes 24584 | tf_op jit(solution)/shard_map/ppermute | solution.py:134
  48.0 3.7 %collective-permute-start.25 = (f32[8,256]{1,0:T(8,128)S(1)}, f32[8,256]{1,0:T(8,128)S(1)}, u32[]{:S(2)}, u32[]{:S(2)}) collective-permute-start(f32[8,256]{1,0:T(8,128)S(1)} %get-tuple-element.82), channel_id=1, source_target_pairs={{0,16},{1,17},{2,18},{3,19},{4,20},{5,21},{6,22},{7,23},{8,24},{9,... | collective-permute-start | bytes 24584 | tf_op jit(solution)/shard_map/ppermute | solution.py:134
  52.1 3.7 %collective-permute-start.29 = (f32[8,256]{1,0:T(8,128)S(1)}, f32[8,256]{1,0:T(8,128)S(1)}, u32[]{:S(2)}, u32[]{:S(2)}) collective-permute-start(f32[8,256]{1,0:T(8,128)S(1)} %get-tuple-element.87), channel_id=1, source_target_pairs={{0,8},{1,25},{2,10},{3,27},{4,12},{5,29},{6,14},{7,31},{8,0},{9,17... | collective-permute-start | bytes 24584 | tf_op jit(solution)/shard_map/ppermute | solution.py:134
  53.2 3.7 %collective-permute-start.28 = (f32[8,256]{1,0:T(8,128)S(1)}, f32[8,256]{1,0:T(8,128)S(1)}, u32[]{:S(2)}, u32[]{:S(2)}) collective-permute-start(f32[8,256]{1,0:T(8,128)S(1)} %get-tuple-element.86), channel_id=1, source_target_pairs={{0,16},{1,17},{2,18},{3,19},{4,20},{5,21},{6,22},{7,23},{8,24},{9,... | collective-permute-start | bytes 24584 | tf_op jit(solution)/shard_map/ppermute | solution.py:134
  57.3 3.7 %collective-permute-start.32 = (f32[8,256]{1,0:T(8,128)S(1)}, f32[8,256]{1,0:T(8,128)S(1)}, u32[]{:S(2)}, u32[]{:S(2)}) collective-permute-start(f32[8,256]{1,0:T(8,128)S(1)} %get-tuple-element.91), channel_id=1, source_target_pairs={{0,8},{1,25},{2,10},{3,27},{4,12},{5,29},{6,14},{7,31},{8,0},{9,17... | collective-permute-start | bytes 24584 | tf_op jit(solution)/shard_map/ppermute | solution.py:134
  58.4 3.7 %collective-permute-start.31 = (f32[8,256]{1,0:T(8,128)S(1)}, f32[8,256]{1,0:T(8,128)S(1)}, u32[]{:S(2)}, u32[]{:S(2)}) collective-permute-start(f32[8,256]{1,0:T(8,128)S(1)} %get-tuple-element.90), channel_id=1, source_target_pairs={{0,16},{1,17},{2,18},{3,19},{4,20},{5,21},{6,22},{7,23},{8,24},{9,... | collective-permute-start | bytes 24584 | tf_op jit(solution)/shard_map/ppermute | solution.py:134
  62.5 3.7 %collective-permute-start.35 = (f32[8,256]{1,0:T(8,128)S(1)}, f32[8,256]{1,0:T(8,128)S(1)}, u32[]{:S(2)}, u32[]{:S(2)}) collective-permute-start(f32[8,256]{1,0:T(8,128)S(1)} %get-tuple-element.95), channel_id=1, source_target_pairs={{0,8},{1,25},{2,10},{3,27},{4,12},{5,29},{6,14},{7,31},{8,0},{9,17... | collective-permute-start | bytes 24584 | tf_op jit(solution)/shard_map/ppermute | solution.py:134
  67.7 3.7 %collective-permute-start.38 = (f32[8,256]{1,0:T(8,128)S(1)}, f32[8,256]{1,0:T(8,128)S(1)}, u32[]{:S(2)}, u32[]{:S(2)}) collective-permute-start(f32[8,256]{1,0:T(8,128)S(1)} %get-tuple-element.99), channel_id=1, source_target_pairs={{0,8},{1,25},{2,10},{3,27},{4,12},{5,29},{6,14},{7,31},{8,0},{9,17... | collective-permute-start | bytes 24584 | tf_op jit(solution)/shard_map/ppermute | solution.py:134
  72.9 3.7 %collective-permute-start.41 = (f32[8,256]{1,0:T(8,128)S(1)}, f32[8,256]{1,0:T(8,128)S(1)}, u32[]{:S(2)}, u32[]{:S(2)}) collective-permute-start(f32[8,256]{1,0:T(8,128)S(1)} %get-tuple-element.103), channel_id=1, source_target_pairs={{0,8},{1,25},{2,10},{3,27},{4,12},{5,29},{6,14},{7,31},{8,0},{9,17... | collective-permute-start | bytes 24584 | tf_op jit(solution)/shard_map/ppermute | solution.py:134
  78.1 3.7 %collective-permute-start.44 = (f32[8,256]{1,0:T(8,128)S(1)}, f32[8,256]{1,0:T(8,128)S(1)}, u32[]{:S(2)}, u32[]{:S(2)}) collective-permute-start(f32[8,256]{1,0:T(8,128)S(1)} %get-tuple-element.108), channel_id=1, source_target_pairs={{0,8},{1,25},{2,10},{3,27},{4,12},{5,29},{6,14},{7,31},{8,0},{9,17... | collective-permute-start | bytes 24584 | tf_op jit(solution)/shard_map/ppermute | solution.py:134
  83.2 3.8 %collective-permute-start.47 = (f32[2,8,256]{2,1,0:T(8,128)S(1)}, f32[2,8,256]{2,1,0:T(8,128)S(1)}, u32[]{:S(2)}, u32[]{:S(2)}) collective-permute-start(f32[2,8,256]{2,1,0:T(8,128)S(1)} %get-tuple-element.112), channel_id=1, source_target_pairs={{0,2},{1,7},{2,0},{3,5},{4,6},{5,3},{6,4},{7,1},{8,10},{9,15},{10,... | collective-permute-start | bytes 49160 | tf_op jit(solution)/shard_map/ppermute | solution.py:134
  83.3 4.9 %collective-permute-start.46 = (f32[2,8,256]{2,1,0:T(8,128)S(1)}, f32[2,8,256]{2,1,0:T(8,128)S(1)}, u32[]{:S(2)}, u32[]{:S(2)}) collective-permute-start(f32[2,8,256]{2,1,0:T(8,128)S(1)} %get-tuple-element.111), channel_id=1, source_target_pairs={{0,4},{1,5},{2,6},{3,7},{4,0},{5,1},{6,2},{7,3},{8,12},{9,13},{10,... | collective-permute-start | bytes 49160 | tf_op jit(solution)/shard_map/ppermute | solution.py:134
  (27 other events, 90.6 us)

commit v7 on v6

--- a/solution.py
+++ b/solution.py
@@ -211,9 +211,9 @@
 
     def turn_body(level):
         def body(r):
-            r.turned[0] = r.inverses[level, 0].T
+            r.turned[0] = inverse(r, level).T
             for k in range(blocks):
-                r.turned[1 + k] = r.lowers[level - 1, 0, k].T
+                r.turned[1 + k] = lower(r, level, k).T
 
         return body
 
@@ -238,9 +238,8 @@
                 r.finished[(level - 1) * owners + owner] = getattr(r, name)[...]
             total = r.source[level]
             for k in range(blocks):
-                block = r.turned[1 + k] if level > 1 else lower(r, level, k)
-                total = total - times(r.finished[column_of(r, level, k)], block, level == 1)
-            answer = times(total, r.turned[0] if level > 1 else inverse(r, level), level == 1)
+                total = total - times(r.finished[column_of(r, level, k)], r.turned[1 + k], False)
+            answer = times(total, r.turned[0], False)
             r.finished[level * owners + r.row] = answer
             if level < levels - 1:
                 r.solved[...] = answer
@@ -271,11 +270,17 @@
             total = total - getattr(r, name)[...]
         return total
 
-    def last_body(r):
-        r.answers[0] = times(source_of(r, 0), r.inverse_0[...], False)
-        moved = regroup([r.answers[level] for level in range(levels)], width)
+    def gather_body(r):
+        moved = regroup([jnp.zeros((each, size), F32)] + [r.answers[level] for level in range(1, levels)], width)
         for column in range(columns):
             r.pieces[column] = moved(column)
+
+    def last_body(r):
+        answer = times(source_of(r, 0), r.inverse_0[...], False)
+        first = lane_group((each, size), width) == 0
+        for column in range(columns):
+            moved = pltpu.roll(answer, size - column * width, 1) if column else answer
+            r.pieces[column] = jnp.where(first, moved, r.pieces[column])
         for name, z in outgoing(r, "layer"):
             for core in range(CORES):
                 getattr(r, name)[core] = r.pieces[CORES * z + core]
@@ -323,15 +328,13 @@
         last = level == levels - 1
         arrived = exchange("row", [solved] * len(row_routes[0]), solved)
         held.setdefault(level, {"inverses": diag_inverse, "lowers": lower_blocks})
-        turned = {}
-        if level > 1:
-            turned = call(
-                f"turn_{level}", turn_body(level), {**held[level], "after": solved},
-                makes={"turned": VMEM((1 + blocks, size, size), BF16)},
-            )
+        turned = call(
+            f"turn_{level}", turn_body(level), {**held[level], "after": solved},
+            makes={"turned": VMEM((1 + blocks, size, size), BF16)},
+        )
         state = call(
             f"forward_{level}", forward_body(level),
-            {"lists": lists, **held[level], **turned, "source": source, **arrived},
+            {"lists": lists, **(held[level] if last else {}), **turned, "source": source, **arrived},
             {"finished": finished},
             {"accumulated": all_rows, "answers": own_rows, **to_owners} if last else {"solved": rows},
         )
@@ -342,15 +345,15 @@
             {"lists": lists, **held[level], "finished": finished, **exchanged("row", state)},
             {"accumulated": state["accumulated"], "answers": state["answers"]}, to_owners,
         )
+    arrived = exchanged("row", state)
+    pieces = call("gather", gather_body, {"answers": state["answers"]}, makes={"pieces": packed_rows})["pieces"]
     ended = call(
         "backward_0", last_body,
         {
-            "inverse_0": at_start["inverse_0"], "finished": finished, "accumulated": state["accumulated"],
-            **exchanged("row", state),
+            "inverse_0": at_start["inverse_0"], "finished": finished, "accumulated": state["accumulated"], **arrived,
         },
-        {"answers": state["answers"]},
+        {"pieces": pieces},
         {"kept": rows, **messages("layer", both, both)},
-        {"pieces": packed_rows},
     )
     return call(
         "out", out_body, {"kept": ended["kept"], **exchanged("layer", ended)},

time: 89.6 us -> 89.5 us (level)
    pallas_call x26 -> x28, Pallas kernels: 8.97 us -> 9.18 us  [call(): pl.pallas_call(kernel, in_specs=[spec(key) for key in in_names], out_spec...]
where the time goes in v7:
time: 89.5 us; the launch traced here: 89.4 us
  starting transfers between devices  47.7 us (53%)
  waiting for transfers between devices  32.3 us (36%)
  Pallas kernels  9.18 us (10%)
    ppermute x32, starting transfers between devices, send(): return lax.ppermute(array, ('row', 'col'), steps)  44.5 us
    ppermute x32, waiting for transfers between devices, send(): return lax.ppermute(array, ('row', 'col'), steps)  29.4 us
    pallas_call x28, Pallas kernels, call(): pl.pallas_call(kernel, in_specs=[spec(key) for key in in_names], out_spec...  9.18 us
    ppermute x17, starting transfers between devices, swap(): return lax.ppermute(array, 'col', [(c, c ^ 1) for c in range(columns)])  3.26 us
    ppermute x17, waiting for transfers between devices, swap(): return lax.ppermute(array, 'col', [(c, c ^ 1) for c in range(columns)])  2.84 us
  transfers between devices with their start and end apart: 49, of which 45 were waited for; matrix products, arithmetic and copies ran while one was open for 0% of the time, Pallas kernels for 4%

profile of v7, /device:TPU:0, one launch (start us, length us, event | category | flops | bytes accessed | tf_op | source)
XLA Modules:
  0.0 89.4 jit_solution(10014968561441265666)
XLA Ops:
  0.5 1.4 %pack.1 = (f32[32,256]{1,0:T(8,128)S(1)}, bf16[256,256]{1,0:T(8,128)(2,1)S(1)}, bf16[256,256]{1,0:T(8,128)(2,1)S(1)}, bf16[3,256,256]{2,1,0:T(8,128)(2,1)S(1)}) custom-call(f32[8,1,32,32]{3,2,1,0:T(8,128)} %refs_0_.7, bf16[8,1,256,256]{3,2,1,0:T(8,128)(2,1)} %refs_1_.25, bf16[7,1,3,256,256]{4,3,2,1,0:T(8,128)(2,1)} %refs_2_.13), custom_call_target="tpu_custom_call" | custom-call | tf_op jit(solution)/shard_map/pack/pallas_call | solution.py:93
  2.0 2.7 %collective-permute-start.1 = (f32[2,8,256]{2,1,0:T(8,128)S(1)}, f32[2,8,256]{2,1,0:T(8,128)S(1)}, u32[]{:S(2)}, u32[]{:S(2)}) collective-permute-start(f32[2,8,256]{2,1,0:T(8,128)S(1)} %get-tuple-element.61), channel_id=1, source_target_pairs={{0,2},{1,7},{2,0},{3,5},{4,6},{5,3},{6,4},{7,1},{8,10},{9,15},{10,... | collective-permute-start | bytes 49160 | tf_op jit(solution)/shard_map/ppermute | solution.py:134
  4.8 2.6 %collective-permute-start.2 = (f32[2,8,256]{2,1,0:T(8,128)S(1)}, f32[2,8,256]{2,1,0:T(8,128)S(1)}, u32[]{:S(2)}, u32[]{:S(2)}) collective-permute-start(f32[2,8,256]{2,1,0:T(8,128)S(1)} %get-tuple-element.65), channel_id=1, source_target_pairs={{0,4},{1,5},{2,6},{3,7},{4,0},{5,1},{6,2},{7,3},{8,12},{9,13},{10,... | collective-permute-start | bytes 49160 | tf_op jit(solution)/shard_map/ppermute | solution.py:134
  9.6 1.6 %collective-permute-start.5 = (f32[8,256]{1,0:T(8,128)S(1)}, f32[8,256]{1,0:T(8,128)S(1)}, u32[]{:S(2)}, u32[]{:S(2)}) collective-permute-start(f32[8,256]{1,0:T(8,128)S(1)} %get-tuple-element.66.refs_2_), channel_id=1, source_target_pairs={{0,8},{1,25},{2,10},{3,27},{4,12},{5,29},{6,14},{7,31},{8,0},{9,17... | collective-permute-start | bytes 24584 | tf_op jit(solution)/shard_map/ppermute | solution.py:134
  11.2 1.5 %collective-permute-start.4 = (f32[8,256]{1,0:T(8,128)S(1)}, f32[8,256]{1,0:T(8,128)S(1)}, u32[]{:S(2)}, u32[]{:S(2)}) collective-permute-start(f32[8,256]{1,0:T(8,128)S(1)} %get-tuple-element.66.refs_2_), channel_id=1, source_target_pairs={{0,16},{1,17},{2,18},{3,19},{4,20},{5,21},{6,22},{7,23},{8,24},{9,... | collective-permute-start | bytes 24584 | tf_op jit(solution)/shard_map/ppermute | solution.py:134
  15.3 1.5 %collective-permute-start.8 = (f32[8,256]{1,0:T(8,128)S(1)}, f32[8,256]{1,0:T(8,128)S(1)}, u32[]{:S(2)}, u32[]{:S(2)}) collective-permute-start(f32[8,256]{1,0:T(8,128)S(1)} %get-tuple-element.69.refs_2_), channel_id=1, source_target_pairs={{0,8},{1,25},{2,10},{3,27},{4,12},{5,29},{6,14},{7,31},{8,0},{9,17... | collective-permute-start | bytes 24584 | tf_op jit(solution)/shard_map/ppermute | solution.py:134
  16.8 1.5 %collective-permute-start.7 = (f32[8,256]{1,0:T(8,128)S(1)}, f32[8,256]{1,0:T(8,128)S(1)}, u32[]{:S(2)}, u32[]{:S(2)}) collective-permute-start(f32[8,256]{1,0:T(8,128)S(1)} %get-tuple-element.69.refs_2_), channel_id=1, source_target_pairs={{0,16},{1,17},{2,18},{3,19},{4,20},{5,21},{6,22},{7,23},{8,24},{9,... | collective-permute-start | bytes 24584 | tf_op jit(solution)/shard_map/ppermute | solution.py:134
  19.3 1.2 %collective-permute-done.7.refs_3_ = f32[8,256]{1,0:T(8,128)S(1)} collective-permute-done((f32[8,256]{1,0:T(8,128)S(1)}, f32[8,256]{1,0:T(8,128)S(1)}, u32[]{:S(2)}, u32[]{:S(2)}) %collective-permute-start.7) | collective-permute-done | bytes 8224 | tf_op jit(solution)/shard_map/ppermute | solution.py:134
  22.0 1.5 %collective-permute-start.10 = (f32[8,256]{1,0:T(8,128)S(1)}, f32[8,256]{1,0:T(8,128)S(1)}, u32[]{:S(2)}, u32[]{:S(2)}) collective-permute-start(f32[8,256]{1,0:T(8,128)S(1)} %get-tuple-element.71.refs_2_), channel_id=1, source_target_pairs={{0,16},{1,17},{2,18},{3,19},{4,20},{5,21},{6,22},{7,23},{8,24},{9,... | collective-permute-start | bytes 24584 | tf_op jit(solution)/shard_map/ppermute | solution.py:134
  27.1 1.5 %collective-permute-start.13 = (f32[8,256]{1,0:T(8,128)S(1)}, f32[8,256]{1,0:T(8,128)S(1)}, u32[]{:S(2)}, u32[]{:S(2)}) collective-permute-start(f32[8,256]{1,0:T(8,128)S(1)} %get-tuple-element.73.refs_2_), channel_id=1, source_target_pairs={{0,16},{1,17},{2,18},{3,19},{4,20},{5,21},{6,22},{7,23},{8,24},{9,... | collective-permute-start | bytes 24584 | tf_op jit(solution)/shard_map/ppermute | solution.py:134
  32.2 1.5 %collective-permute-start.16 = (f32[8,256]{1,0:T(8,128)S(1)}, f32[8,256]{1,0:T(8,128)S(1)}, u32[]{:S(2)}, u32[]{:S(2)}) collective-permute-start(f32[8,256]{1,0:T(8,128)S(1)} %get-tuple-element.75.refs_2_), channel_id=1, source_target_pairs={{0,16},{1,17},{2,18},{3,19},{4,20},{5,21},{6,22},{7,23},{8,24},{9,... | collective-permute-start | bytes 24584 | tf_op jit(solution)/shard_map/ppermute | solution.py:134
  37.4 1.5 %collective-permute-start.19 = (f32[8,256]{1,0:T(8,128)S(1)}, f32[8,256]{1,0:T(8,128)S(1)}, u32[]{:S(2)}, u32[]{:S(2)}) collective-permute-start(f32[8,256]{1,0:T(8,128)S(1)} %get-tuple-element.77.refs_2_), channel_id=1, source_target_pairs={{0,16},{1,17},{2,18},{3,19},{4,20},{5,21},{6,22},{7,23},{8,24},{9,... | collective-permute-start | bytes 24584 | tf_op jit(solution)/shard_map/ppermute | solution.py:134
  38.8 1.2 %collective-permute-done.20.refs_4_ = f32[8,256]{1,0:T(8,128)S(1)} collective-permute-done((f32[8,256]{1,0:T(8,128)S(1)}, f32[8,256]{1,0:T(8,128)S(1)}, u32[]{:S(2)}, u32[]{:S(2)}) %collective-permute-start.20) | collective-permute-done | bytes 8224 | tf_op jit(solution)/shard_map/ppermute | solution.py:134
  42.5 1.5 %collective-permute-start.22 = (f32[8,256]{1,0:T(8,128)S(1)}, f32[8,256]{1,0:T(8,128)S(1)}, u32[]{:S(2)}, u32[]{:S(2)}) collective-permute-start(f32[8,256]{1,0:T(8,128)S(1)} %get-tuple-element.79.refs_2_), channel_id=1, source_target_pairs={{0,16},{1,17},{2,18},{3,19},{4,20},{5,21},{6,22},{7,23},{8,24},{9,... | collective-permute-start | bytes 24584 | tf_op jit(solution)/shard_map/ppermute | solution.py:134
  44.0 1.2 %collective-permute-done.23.refs_6_ = f32[8,256]{1,0:T(8,128)S(1)} collective-permute-done((f32[8,256]{1,0:T(8,128)S(1)}, f32[8,256]{1,0:T(8,128)S(1)}, u32[]{:S(2)}, u32[]{:S(2)}) %collective-permute-start.23) | collective-permute-done | bytes 8224 | tf_op jit(solution)/shard_map/ppermute | solution.py:134
  48.0 1.5 %collective-permute-start.25 = (f32[8,256]{1,0:T(8,128)S(1)}, f32[8,256]{1,0:T(8,128)S(1)}, u32[]{:S(2)}, u32[]{:S(2)}) collective-permute-start(f32[8,256]{1,0:T(8,128)S(1)} %get-tuple-element.82), channel_id=1, source_target_pairs={{0,16},{1,17},{2,18},{3,19},{4,20},{5,21},{6,22},{7,23},{8,24},{9,... | collective-permute-start | bytes 24584 | tf_op jit(solution)/shard_map/ppermute | solution.py:134
  49.4 1.2 %collective-permute-done.26.refs_5_ = f32[8,256]{1,0:T(8,128)S(1)} collective-permute-done((f32[8,256]{1,0:T(8,128)S(1)}, f32[8,256]{1,0:T(8,128)S(1)}, u32[]{:S(2)}, u32[]{:S(2)}) %collective-permute-start.26) | collective-permute-done | bytes 8224 | tf_op jit(solution)/shard_map/ppermute | solution.py:134
  53.1 1.5 %collective-permute-start.28 = (f32[8,256]{1,0:T(8,128)S(1)}, f32[8,256]{1,0:T(8,128)S(1)}, u32[]{:S(2)}, u32[]{:S(2)}) collective-permute-start(f32[8,256]{1,0:T(8,128)S(1)} %get-tuple-element.86), channel_id=1, source_target_pairs={{0,16},{1,17},{2,18},{3,19},{4,20},{5,21},{6,22},{7,23},{8,24},{9,... | collective-permute-start | bytes 24584 | tf_op jit(solution)/shard_map/ppermute | solution.py:134
  58.3 1.5 %collective-permute-start.31 = (f32[8,256]{1,0:T(8,128)S(1)}, f32[8,256]{1,0:T(8,128)S(1)}, u32[]{:S(2)}, u32[]{:S(2)}) collective-permute-start(f32[8,256]{1,0:T(8,128)S(1)} %get-tuple-element.90), channel_id=1, source_target_pairs={{0,16},{1,17},{2,18},{3,19},{4,20},{5,21},{6,22},{7,23},{8,24},{9,... | collective-permute-start | bytes 24584 | tf_op jit(solution)/shard_map/ppermute | solution.py:134
  63.5 1.5 %collective-permute-start.34 = (f32[8,256]{1,0:T(8,128)S(1)}, f32[8,256]{1,0:T(8,128)S(1)}, u32[]{:S(2)}, u32[]{:S(2)}) collective-permute-start(f32[8,256]{1,0:T(8,128)S(1)} %get-tuple-element.94), channel_id=1, source_target_pairs={{0,16},{1,17},{2,18},{3,19},{4,20},{5,21},{6,22},{7,23},{8,24},{9,... | collective-permute-start | bytes 24584 | tf_op jit(solution)/shard_map/ppermute | solution.py:134
  68.7 1.5 %collective-permute-start.37 = (f32[8,256]{1,0:T(8,128)S(1)}, f32[8,256]{1,0:T(8,128)S(1)}, u32[]{:S(2)}, u32[]{:S(2)}) collective-permute-start(f32[8,256]{1,0:T(8,128)S(1)} %get-tuple-element.98), channel_id=1, source_target_pairs={{0,16},{1,17},{2,18},{3,19},{4,20},{5,21},{6,22},{7,23},{8,24},{9,... | collective-permute-start | bytes 24584 | tf_op jit(solution)/shard_map/ppermute | solution.py:134
  73.8 1.5 %collective-permute-start.40 = (f32[8,256]{1,0:T(8,128)S(1)}, f32[8,256]{1,0:T(8,128)S(1)}, u32[]{:S(2)}, u32[]{:S(2)}) collective-permute-start(f32[8,256]{1,0:T(8,128)S(1)} %get-tuple-element.102), channel_id=1, source_target_pairs={{0,16},{1,17},{2,18},{3,19},{4,20},{5,21},{6,22},{7,23},{8,24},{9,... | collective-permute-start | bytes 24584 | tf_op jit(solution)/shard_map/ppermute | solution.py:134
  79.0 1.5 %collective-permute-start.43 = (f32[8,256]{1,0:T(8,128)S(1)}, f32[8,256]{1,0:T(8,128)S(1)}, u32[]{:S(2)}, u32[]{:S(2)}) collective-permute-start(f32[8,256]{1,0:T(8,128)S(1)} %get-tuple-element.107), channel_id=1, source_target_pairs={{0,16},{1,17},{2,18},{3,19},{4,20},{5,21},{6,22},{7,23},{8,24},{9,... | collective-permute-start | bytes 24584 | tf_op jit(solution)/shard_map/ppermute | solution.py:134
  83.1 3.0 %collective-permute-start.46 = (f32[2,8,256]{2,1,0:T(8,128)S(1)}, f32[2,8,256]{2,1,0:T(8,128)S(1)}, u32[]{:S(2)}, u32[]{:S(2)}) collective-permute-start(f32[2,8,256]{2,1,0:T(8,128)S(1)} %get-tuple-element.111), channel_id=1, source_target_pairs={{0,4},{1,5},{2,6},{3,7},{4,0},{5,1},{6,2},{7,3},{8,12},{9,13},{10,... | collective-permute-start | bytes 49160 | tf_op jit(solution)/shard_map/ppermute | solution.py:134
  (106 shorter events, 51.0 us)
Async XLA Ops:
  2.0 5.3 %collective-permute-start.1 = (f32[2,8,256]{2,1,0:T(8,128)S(1)}, f32[2,8,256]{2,1,0:T(8,128)S(1)}, u32[]{:S(2)}, u32[]{:S(2)}) collective-permute-start(f32[2,8,256]{2,1,0:T(8,128)S(1)} %get-tuple-element.61), channel_id=1, source_target_pairs={{0,2},{1,7},{2,0},{3,5},{4,6},{5,3},{6,4},{7,1},{8,10},{9,15},{10,... | collective-permute-start | bytes 49160 | tf_op jit(solution)/shard_map/ppermute | solution.py:134
  4.8 4.6 %collective-permute-start.2 = (f32[2,8,256]{2,1,0:T(8,128)S(1)}, f32[2,8,256]{2,1,0:T(8,128)S(1)}, u32[]{:S(2)}, u32[]{:S(2)}) collective-permute-start(f32[2,8,256]{2,1,0:T(8,128)S(1)} %get-tuple-element.65), channel_id=1, source_target_pairs={{0,4},{1,5},{2,6},{3,7},{4,0},{5,1},{6,2},{7,3},{8,12},{9,13},{10,... | collective-permute-start | bytes 49160 | tf_op jit(solution)/shard_map/ppermute | solution.py:134
  9.6 3.7 %collective-permute-start.5 = (f32[8,256]{1,0:T(8,128)S(1)}, f32[8,256]{1,0:T(8,128)S(1)}, u32[]{:S(2)}, u32[]{:S(2)}) collective-permute-start(f32[8,256]{1,0:T(8,128)S(1)} %get-tuple-element.66.refs_2_), channel_id=1, source_target_pairs={{0,8},{1,25},{2,10},{3,27},{4,12},{5,29},{6,14},{7,31},{8,0},{9,17... | collective-permute-start | bytes 24584 | tf_op jit(solution)/shard_map/ppermute | solution.py:134
  15.3 3.7 %collective-permute-start.8 = (f32[8,256]{1,0:T(8,128)S(1)}, f32[8,256]{1,0:T(8,128)S(1)}, u32[]{:S(2)}, u32[]{:S(2)}) collective-permute-start(f32[8,256]{1,0:T(8,128)S(1)} %get-tuple-element.69.refs_2_), channel_id=1, source_target_pairs={{0,8},{1,25},{2,10},{3,27},{4,12},{5,29},{6,14},{7,31},{8,0},{9,17... | collective-permute-start | bytes 24584 | tf_op jit(solution)/shard_map/ppermute | solution.py:134
  16.8 3.7 %collective-permute-start.7 = (f32[8,256]{1,0:T(8,128)S(1)}, f32[8,256]{1,0:T(8,128)S(1)}, u32[]{:S(2)}, u32[]{:S(2)}) collective-permute-start(f32[8,256]{1,0:T(8,128)S(1)} %get-tuple-element.69.refs_2_), channel_id=1, source_target_pairs={{0,16},{1,17},{2,18},{3,19},{4,20},{5,21},{6,22},{7,23},{8,24},{9,... | collective-permute-start | bytes 24584 | tf_op jit(solution)/shard_map/ppermute | solution.py:134
  20.9 3.7 %collective-permute-start.11 = (f32[8,256]{1,0:T(8,128)S(1)}, f32[8,256]{1,0:T(8,128)S(1)}, u32[]{:S(2)}, u32[]{:S(2)}) collective-permute-start(f32[8,256]{1,0:T(8,128)S(1)} %get-tuple-element.71.refs_2_), channel_id=1, source_target_pairs={{0,8},{1,25},{2,10},{3,27},{4,12},{5,29},{6,14},{7,31},{8,0},{9,17... | collective-permute-start | bytes 24584 | tf_op jit(solution)/shard_map/ppermute | solution.py:134
  26.0 3.7 %collective-permute-start.14 = (f32[8,256]{1,0:T(8,128)S(1)}, f32[8,256]{1,0:T(8,128)S(1)}, u32[]{:S(2)}, u32[]{:S(2)}) collective-permute-start(f32[8,256]{1,0:T(8,128)S(1)} %get-tuple-element.73.refs_2_), channel_id=1, source_target_pairs={{0,8},{1,25},{2,10},{3,27},{4,12},{5,29},{6,14},{7,31},{8,0},{9,17... | collective-permute-start | bytes 24584 | tf_op jit(solution)/shard_map/ppermute | solution.py:134
  27.1 3.7 %collective-permute-start.13 = (f32[8,256]{1,0:T(8,128)S(1)}, f32[8,256]{1,0:T(8,128)S(1)}, u32[]{:S(2)}, u32[]{:S(2)}) collective-permute-start(f32[8,256]{1,0:T(8,128)S(1)} %get-tuple-element.73.refs_2_), channel_id=1, source_target_pairs={{0,16},{1,17},{2,18},{3,19},{4,20},{5,21},{6,22},{7,23},{8,24},{9,... | collective-permute-start | bytes 24584 | tf_op jit(solution)/shard_map/ppermute | solution.py:134
  31.2 3.7 %collective-permute-start.17 = (f32[8,256]{1,0:T(8,128)S(1)}, f32[8,256]{1,0:T(8,128)S(1)}, u32[]{:S(2)}, u32[]{:S(2)}) collective-permute-start(f32[8,256]{1,0:T(8,128)S(1)} %get-tuple-element.75.refs_2_), channel_id=1, source_target_pairs={{0,8},{1,25},{2,10},{3,27},{4,12},{5,29},{6,14},{7,31},{8,0},{9,17... | collective-permute-start | bytes 24584 | tf_op jit(solution)/shard_map/ppermute | solution.py:134
  32.2 3.7 %collective-permute-start.16 = (f32[8,256]{1,0:T(8,128)S(1)}, f32[8,256]{1,0:T(8,128)S(1)}, u32[]{:S(2)}, u32[]{:S(2)}) collective-permute-start(f32[8,256]{1,0:T(8,128)S(1)} %get-tuple-element.75.refs_2_), channel_id=1, source_target_pairs={{0,16},{1,17},{2,18},{3,19},{4,20},{5,21},{6,22},{7,23},{8,24},{9,... | collective-permute-start | bytes 24584 | tf_op jit(solution)/shard_map/ppermute | solution.py:134
  36.4 3.7 %collective-permute-start.20 = (f32[8,256]{1,0:T(8,128)S(1)}, f32[8,256]{1,0:T(8,128)S(1)}, u32[]{:S(2)}, u32[]{:S(2)}) collective-permute-start(f32[8,256]{1,0:T(8,128)S(1)} %get-tuple-element.77.refs_2_), channel_id=1, source_target_pairs={{0,8},{1,25},{2,10},{3,27},{4,12},{5,29},{6,14},{7,31},{8,0},{9,17... | collective-permute-start | bytes 24584 | tf_op jit(solution)/shard_map/ppermute | solution.py:134
  41.5 3.7 %collective-permute-start.23 = (f32[8,256]{1,0:T(8,128)S(1)}, f32[8,256]{1,0:T(8,128)S(1)}, u32[]{:S(2)}, u32[]{:S(2)}) collective-permute-start(f32[8,256]{1,0:T(8,128)S(1)} %get-tuple-element.79.refs_2_), channel_id=1, source_target_pairs={{0,8},{1,25},{2,10},{3,27},{4,12},{5,29},{6,14},{7,31},{8,0},{9,17... | collective-permute-start | bytes 24584 | tf_op jit(solution)/shard_map/ppermute | solution.py:134
  42.5 3.7 %collective-permute-start.22 = (f32[8,256]{1,0:T(8,128)S(1)}, f32[8,256]{1,0:T(8,128)S(1)}, u32[]{:S(2)}, u32[]{:S(2)}) collective-permute-start(f32[8,256]{1,0:T(8,128)S(1)} %get-tuple-element.79.refs_2_), channel_id=1, source_target_pairs={{0,16},{1,17},{2,18},{3,19},{4,20},{5,21},{6,22},{7,23},{8,24},{9,... | collective-permute-start | bytes 24584 | tf_op jit(solution)/shard_map/ppermute | solution.py:134
  46.9 3.7 %collective-permute-start.26 = (f32[8,256]{1,0:T(8,128)S(1)}, f32[8,256]{1,0:T(8,128)S(1)}, u32[]{:S(2)}, u32[]{:S(2)}) collective-permute-start(f32[8,256]{1,0:T(8,128)S(1)} %get-tuple-element.83), channel_id=1, source_target_pairs={{0,8},{1,25},{2,10},{3,27},{4,12},{5,29},{6,14},{7,31},{8,0},{9,17... | collective-permute-start | bytes 24584 | tf_op jit(solution)/shard_map/ppermute | solution.py:134
  48.0 3.7 %collective-permute-start.25 = (f32[8,256]{1,0:T(8,128)S(1)}, f32[8,256]{1,0:T(8,128)S(1)}, u32[]{:S(2)}, u32[]{:S(2)}) collective-permute-start(f32[8,256]{1,0:T(8,128)S(1)} %get-tuple-element.82), channel_id=1, source_target_pairs={{0,16},{1,17},{2,18},{3,19},{4,20},{5,21},{6,22},{7,23},{8,24},{9,... | collective-permute-start | bytes 24584 | tf_op jit(solution)/shard_map/ppermute | solution.py:134
  52.1 3.7 %collective-permute-start.29 = (f32[8,256]{1,0:T(8,128)S(1)}, f32[8,256]{1,0:T(8,128)S(1)}, u32[]{:S(2)}, u32[]{:S(2)}) collective-permute-start(f32[8,256]{1,0:T(8,128)S(1)} %get-tuple-element.87), channel_id=1, source_target_pairs={{0,8},{1,25},{2,10},{3,27},{4,12},{5,29},{6,14},{7,31},{8,0},{9,17... | collective-permute-start | bytes 24584 | tf_op jit(solution)/shard_map/ppermute | solution.py:134
  53.1 3.7 %collective-permute-start.28 = (f32[8,256]{1,0:T(8,128)S(1)}, f32[8,256]{1,0:T(8,128)S(1)}, u32[]{:S(2)}, u32[]{:S(2)}) collective-permute-start(f32[8,256]{1,0:T(8,128)S(1)} %get-tuple-element.86), channel_id=1, source_target_pairs={{0,16},{1,17},{2,18},{3,19},{4,20},{5,21},{6,22},{7,23},{8,24},{9,... | collective-permute-start | bytes 24584 | tf_op jit(solution)/shard_map/ppermute | solution.py:134
  57.3 3.7 %collective-permute-start.32 = (f32[8,256]{1,0:T(8,128)S(1)}, f32[8,256]{1,0:T(8,128)S(1)}, u32[]{:S(2)}, u32[]{:S(2)}) collective-permute-start(f32[8,256]{1,0:T(8,128)S(1)} %get-tuple-element.91), channel_id=1, source_target_pairs={{0,8},{1,25},{2,10},{3,27},{4,12},{5,29},{6,14},{7,31},{8,0},{9,17... | collective-permute-start | bytes 24584 | tf_op jit(solution)/shard_map/ppermute | solution.py:134
  62.4 3.7 %collective-permute-start.35 = (f32[8,256]{1,0:T(8,128)S(1)}, f32[8,256]{1,0:T(8,128)S(1)}, u32[]{:S(2)}, u32[]{:S(2)}) collective-permute-start(f32[8,256]{1,0:T(8,128)S(1)} %get-tuple-element.95), channel_id=1, source_target_pairs={{0,8},{1,25},{2,10},{3,27},{4,12},{5,29},{6,14},{7,31},{8,0},{9,17... | collective-permute-start | bytes 24584 | tf_op jit(solution)/shard_map/ppermute | solution.py:134
  67.6 3.7 %collective-permute-start.38 = (f32[8,256]{1,0:T(8,128)S(1)}, f32[8,256]{1,0:T(8,128)S(1)}, u32[]{:S(2)}, u32[]{:S(2)}) collective-permute-start(f32[8,256]{1,0:T(8,128)S(1)} %get-tuple-element.99), channel_id=1, source_target_pairs={{0,8},{1,25},{2,10},{3,27},{4,12},{5,29},{6,14},{7,31},{8,0},{9,17... | collective-permute-start | bytes 24584 | tf_op jit(solution)/shard_map/ppermute | solution.py:134
  72.8 3.7 %collective-permute-start.41 = (f32[8,256]{1,0:T(8,128)S(1)}, f32[8,256]{1,0:T(8,128)S(1)}, u32[]{:S(2)}, u32[]{:S(2)}) collective-permute-start(f32[8,256]{1,0:T(8,128)S(1)} %get-tuple-element.103), channel_id=1, source_target_pairs={{0,8},{1,25},{2,10},{3,27},{4,12},{5,29},{6,14},{7,31},{8,0},{9,17... | collective-permute-start | bytes 24584 | tf_op jit(solution)/shard_map/ppermute | solution.py:134
  78.0 3.7 %collective-permute-start.44 = (f32[8,256]{1,0:T(8,128)S(1)}, f32[8,256]{1,0:T(8,128)S(1)}, u32[]{:S(2)}, u32[]{:S(2)}) collective-permute-start(f32[8,256]{1,0:T(8,128)S(1)} %get-tuple-element.108), channel_id=1, source_target_pairs={{0,8},{1,25},{2,10},{3,27},{4,12},{5,29},{6,14},{7,31},{8,0},{9,17... | collective-permute-start | bytes 24584 | tf_op jit(solution)/shard_map/ppermute | solution.py:134
  83.1 3.8 %collective-permute-start.47 = (f32[2,8,256]{2,1,0:T(8,128)S(1)}, f32[2,8,256]{2,1,0:T(8,128)S(1)}, u32[]{:S(2)}, u32[]{:S(2)}) collective-permute-start(f32[2,8,256]{2,1,0:T(8,128)S(1)} %get-tuple-element.112), channel_id=1, source_target_pairs={{0,2},{1,7},{2,0},{3,5},{4,6},{5,3},{6,4},{7,1},{8,10},{9,15},{10,... | collective-permute-start | bytes 49160 | tf_op jit(solution)/shard_map/ppermute | solution.py:134
  83.1 4.9 %collective-permute-start.46 = (f32[2,8,256]{2,1,0:T(8,128)S(1)}, f32[2,8,256]{2,1,0:T(8,128)S(1)}, u32[]{:S(2)}, u32[]{:S(2)}) collective-permute-start(f32[2,8,256]{2,1,0:T(8,128)S(1)} %get-tuple-element.111), channel_id=1, source_target_pairs={{0,4},{1,5},{2,6},{3,7},{4,0},{5,1},{6,2},{7,3},{8,12},{9,13},{10,... | collective-permute-start | bytes 49160 | tf_op jit(solution)/shard_map/ppermute | solution.py:134
  (27 other events, 90.6 us)

commit v8 on v7

--- a/solution.py
+++ b/solution.py
@@ -61,8 +61,8 @@
     return total
 
 
-def routes(count):
-    order = [mask for mask in (1, 3, 2) if mask < count] + list(range(4, count))
+def routes(count, first):
+    order = [mask for mask in first if mask < count] + list(range(4, count))
     return [tuple(order[i : i + 2]) for i in range(0, len(order) - 1, 2)], order[-1]
 
 
@@ -115,7 +115,7 @@
     own_rows = VMEM((levels, each, size), F32)
     all_rows = VMEM((levels * owners, each, size), F32)
     packed_rows = VMEM((columns, each, size), F32)
-    row_routes, layer_routes = routes(owners), routes(layers)
+    row_routes, layer_routes = routes(owners, (1, 3, 2)), routes(layers, (2, 3, 1))
     dma = pltpu.SemaphoreType.DMA
 
     def swap(array):

time: 89.5 us -> 89.4 us (level)
  waiting for transfers between devices: 32.3 us -> 31.3 us
    ppermute x32, starting transfers between devices: 44.5 us -> 47.5 us  [send(): return lax.ppermute(array, ('row', 'col'), steps)]
    ppermute x17, waiting for transfers between devices: 2.84 us -> 0.05 us  [swap(): return lax.ppermute(array, 'col', [(c, c ^ 1) for c in range(columns)])]
    ppermute x17, starting transfers between devices: 3.26 us -> 0.99 us  [swap(): return lax.ppermute(array, 'col', [(c, c ^ 1) for c in range(columns)])]
    ppermute x32, waiting for transfers between devices: 29.4 us -> 31.3 us  [send(): return lax.ppermute(array, ('row', 'col'), steps)]
  transfers between devices with their start and end apart: 49 -> 49, of which waited for: 45 -> 32; matrix products, arithmetic and copies ran while one was open for 0% -> 0% of each run, Pallas kernels for 4% -> 4%
where the time goes in v8:
time: 89.4 us; the launch traced here: 89.2 us
  starting transfers between devices  48.5 us (54%)
  waiting for transfers between devices  31.3 us (35%)
  Pallas kernels  9.18 us (10%)
    ppermute x32, starting transfers between devices, send(): return lax.ppermute(array, ('row', 'col'), steps)  47.5 us
    ppermute x32, waiting for transfers between devices, send(): return lax.ppermute(array, ('row', 'col'), steps)  31.3 us
    pallas_call x28, Pallas kernels, call(): pl.pallas_call(kernel, in_specs=[spec(key) for key in in_names], out_spec...  9.18 us
  transfers between devices with their start and end apart: 49, of which 32 were waited for; matrix products, arithmetic and copies ran while one was open for 0% of the time, Pallas kernels for 4%

profile of v8, /device:TPU:0, one launch (start us, length us, event | category | flops | bytes accessed | tf_op | source)
XLA Modules:
  0.0 89.2 jit_solution(10092887611335679906)
XLA Ops:
  0.5 1.4 %pack.1 = (f32[32,256]{1,0:T(8,128)S(1)}, bf16[256,256]{1,0:T(8,128)(2,1)S(1)}, bf16[256,256]{1,0:T(8,128)(2,1)S(1)}, bf16[3,256,256]{2,1,0:T(8,128)(2,1)S(1)}) custom-call(f32[8,1,32,32]{3,2,1,0:T(8,128)} %refs_0_.7, bf16[8,1,256,256]{3,2,1,0:T(8,128)(2,1)} %refs_1_.25, bf16[7,1,3,256,256]{4,3,2,1,0:T(8,128)(2,1)} %refs_2_.13), custom_call_target="tpu_custom_call" | custom-call | tf_op jit(solution)/shard_map/pack/pallas_call | solution.py:93
  2.0 3.7 %collective-permute-start.1 = (f32[2,8,256]{2,1,0:T(8,128)S(1)}, f32[2,8,256]{2,1,0:T(8,128)S(1)}, u32[]{:S(2)}, u32[]{:S(2)}) collective-permute-start(f32[2,8,256]{2,1,0:T(8,128)S(1)} %get-tuple-element.61), channel_id=1, source_target_pairs={{0,4},{1,7},{2,6},{3,5},{4,0},{5,3},{6,2},{7,1},{8,12},{9,15},{10,... | collective-permute-start | bytes 49160 | tf_op jit(solution)/shard_map/ppermute | solution.py:134
  5.8 1.6 %collective-permute-start.2 = (f32[2,8,256]{2,1,0:T(8,128)S(1)}, f32[2,8,256]{2,1,0:T(8,128)S(1)}, u32[]{:S(2)}, u32[]{:S(2)}) collective-permute-start(f32[2,8,256]{2,1,0:T(8,128)S(1)} %get-tuple-element.65), channel_id=1, source_target_pairs={{0,2},{1,3},{2,0},{3,1},{4,6},{5,7},{6,4},{7,5},{8,10},{9,11},{10,... | collective-permute-start | bytes 49160 | tf_op jit(solution)/shard_map/ppermute | solution.py:134
  9.7 1.5 %collective-permute-start.5 = (f32[8,256]{1,0:T(8,128)S(1)}, f32[8,256]{1,0:T(8,128)S(1)}, u32[]{:S(2)}, u32[]{:S(2)}) collective-permute-start(f32[8,256]{1,0:T(8,128)S(1)} %get-tuple-element.66.refs_2_), channel_id=1, source_target_pairs={{0,8},{1,25},{2,10},{3,27},{4,12},{5,29},{6,14},{7,31},{8,0},{9,17... | collective-permute-start | bytes 24584 | tf_op jit(solution)/shard_map/ppermute | solution.py:134
  11.2 1.5 %collective-permute-start.4 = (f32[8,256]{1,0:T(8,128)S(1)}, f32[8,256]{1,0:T(8,128)S(1)}, u32[]{:S(2)}, u32[]{:S(2)}) collective-permute-start(f32[8,256]{1,0:T(8,128)S(1)} %get-tuple-element.66.refs_2_), channel_id=1, source_target_pairs={{0,16},{1,17},{2,18},{3,19},{4,20},{5,21},{6,22},{7,23},{8,24},{9,... | collective-permute-start | bytes 24584 | tf_op jit(solution)/shard_map/ppermute | solution.py:134
  16.4 1.5 %collective-permute-start.7 = (f32[8,256]{1,0:T(8,128)S(1)}, f32[8,256]{1,0:T(8,128)S(1)}, u32[]{:S(2)}, u32[]{:S(2)}) collective-permute-start(f32[8,256]{1,0:T(8,128)S(1)} %get-tuple-element.69.refs_2_), channel_id=1, source_target_pairs={{0,16},{1,17},{2,18},{3,19},{4,20},{5,21},{6,22},{7,23},{8,24},{9,... | collective-permute-start | bytes 24584 | tf_op jit(solution)/shard_map/ppermute | solution.py:134
  21.5 1.5 %collective-permute-start.10 = (f32[8,256]{1,0:T(8,128)S(1)}, f32[8,256]{1,0:T(8,128)S(1)}, u32[]{:S(2)}, u32[]{:S(2)}) collective-permute-start(f32[8,256]{1,0:T(8,128)S(1)} %get-tuple-element.71.refs_2_), channel_id=1, source_target_pairs={{0,16},{1,17},{2,18},{3,19},{4,20},{5,21},{6,22},{7,23},{8,24},{9,... | collective-permute-start | bytes 24584 | tf_op jit(solution)/shard_map/ppermute | solution.py:134
  26.6 1.5 %collective-permute-start.13 = (f32[8,256]{1,0:T(8,128)S(1)}, f32[8,256]{1,0:T(8,128)S(1)}, u32[]{:S(2)}, u32[]{:S(2)}) collective-permute-start(f32[8,256]{1,0:T(8,128)S(1)} %get-tuple-element.73.refs_2_), channel_id=1, source_target_pairs={{0,16},{1,17},{2,18},{3,19},{4,20},{5,21},{6,22},{7,23},{8,24},{9,... | collective-permute-start | bytes 24584 | tf_op jit(solution)/shard_map/ppermute | solution.py:134
  31.8 1.5 %collective-permute-start.16 = (f32[8,256]{1,0:T(8,128)S(1)}, f32[8,256]{1,0:T(8,128)S(1)}, u32[]{:S(2)}, u32[]{:S(2)}) collective-permute-start(f32[8,256]{1,0:T(8,128)S(1)} %get-tuple-element.75.refs_2_), channel_id=1, source_target_pairs={{0,16},{1,17},{2,18},{3,19},{4,20},{5,21},{6,22},{7,23},{8,24},{9,... | collective-permute-start | bytes 24584 | tf_op jit(solution)/shard_map/ppermute | solution.py:134
  36.9 1.5 %collective-permute-start.19 = (f32[8,256]{1,0:T(8,128)S(1)}, f32[8,256]{1,0:T(8,128)S(1)}, u32[]{:S(2)}, u32[]{:S(2)}) collective-permute-start(f32[8,256]{1,0:T(8,128)S(1)} %get-tuple-element.77.refs_2_), channel_id=1, source_target_pairs={{0,16},{1,17},{2,18},{3,19},{4,20},{5,21},{6,22},{7,23},{8,24},{9,... | collective-permute-start | bytes 24584 | tf_op jit(solution)/shard_map/ppermute | solution.py:134
  42.0 1.5 %collective-permute-start.22 = (f32[8,256]{1,0:T(8,128)S(1)}, f32[8,256]{1,0:T(8,128)S(1)}, u32[]{:S(2)}, u32[]{:S(2)}) collective-permute-start(f32[8,256]{1,0:T(8,128)S(1)} %get-tuple-element.79.refs_2_), channel_id=1, source_target_pairs={{0,16},{1,17},{2,18},{3,19},{4,20},{5,21},{6,22},{7,23},{8,24},{9,... | collective-permute-start | bytes 24584 | tf_op jit(solution)/shard_map/ppermute | solution.py:134
  47.5 1.5 %collective-permute-start.25 = (f32[8,256]{1,0:T(8,128)S(1)}, f32[8,256]{1,0:T(8,128)S(1)}, u32[]{:S(2)}, u32[]{:S(2)}) collective-permute-start(f32[8,256]{1,0:T(8,128)S(1)} %get-tuple-element.82), channel_id=1, source_target_pairs={{0,16},{1,17},{2,18},{3,19},{4,20},{5,21},{6,22},{7,23},{8,24},{9,... | collective-permute-start | bytes 24584 | tf_op jit(solution)/shard_map/ppermute | solution.py:134
  51.4 1.2 %collective-permute-start.29 = (f32[8,256]{1,0:T(8,128)S(1)}, f32[8,256]{1,0:T(8,128)S(1)}, u32[]{:S(2)}, u32[]{:S(2)}) collective-permute-start(f32[8,256]{1,0:T(8,128)S(1)} %get-tuple-element.87), channel_id=1, source_target_pairs={{0,8},{1,25},{2,10},{3,27},{4,12},{5,29},{6,14},{7,31},{8,0},{9,17... | collective-permute-start | bytes 24584 | tf_op jit(solution)/shard_map/ppermute | solution.py:134
  52.7 1.5 %collective-permute-start.28 = (f32[8,256]{1,0:T(8,128)S(1)}, f32[8,256]{1,0:T(8,128)S(1)}, u32[]{:S(2)}, u32[]{:S(2)}) collective-permute-start(f32[8,256]{1,0:T(8,128)S(1)} %get-tuple-element.86), channel_id=1, source_target_pairs={{0,16},{1,17},{2,18},{3,19},{4,20},{5,21},{6,22},{7,23},{8,24},{9,... | collective-permute-start | bytes 24584 | tf_op jit(solution)/shard_map/ppermute | solution.py:134
  56.6 1.2 %collective-permute-start.32 = (f32[8,256]{1,0:T(8,128)S(1)}, f32[8,256]{1,0:T(8,128)S(1)}, u32[]{:S(2)}, u32[]{:S(2)}) collective-permute-start(f32[8,256]{1,0:T(8,128)S(1)} %get-tuple-element.91), channel_id=1, source_target_pairs={{0,8},{1,25},{2,10},{3,27},{4,12},{5,29},{6,14},{7,31},{8,0},{9,17... | collective-permute-start | bytes 24584 | tf_op jit(solution)/shard_map/ppermute | solution.py:134
  57.8 1.5 %collective-permute-start.31 = (f32[8,256]{1,0:T(8,128)S(1)}, f32[8,256]{1,0:T(8,128)S(1)}, u32[]{:S(2)}, u32[]{:S(2)}) collective-permute-start(f32[8,256]{1,0:T(8,128)S(1)} %get-tuple-element.90), channel_id=1, source_target_pairs={{0,16},{1,17},{2,18},{3,19},{4,20},{5,21},{6,22},{7,23},{8,24},{9,... | collective-permute-start | bytes 24584 | tf_op jit(solution)/shard_map/ppermute | solution.py:134
  61.8 1.2 %collective-permute-start.35 = (f32[8,256]{1,0:T(8,128)S(1)}, f32[8,256]{1,0:T(8,128)S(1)}, u32[]{:S(2)}, u32[]{:S(2)}) collective-permute-start(f32[8,256]{1,0:T(8,128)S(1)} %get-tuple-element.95), channel_id=1, source_target_pairs={{0,8},{1,25},{2,10},{3,27},{4,12},{5,29},{6,14},{7,31},{8,0},{9,17... | collective-permute-start | bytes 24584 | tf_op jit(solution)/shard_map/ppermute | solution.py:134
  63.0 1.5 %collective-permute-start.34 = (f32[8,256]{1,0:T(8,128)S(1)}, f32[8,256]{1,0:T(8,128)S(1)}, u32[]{:S(2)}, u32[]{:S(2)}) collective-permute-start(f32[8,256]{1,0:T(8,128)S(1)} %get-tuple-element.94), channel_id=1, source_target_pairs={{0,16},{1,17},{2,18},{3,19},{4,20},{5,21},{6,22},{7,23},{8,24},{9,... | collective-permute-start | bytes 24584 | tf_op jit(solution)/shard_map/ppermute | solution.py:134
  68.2 1.5 %collective-permute-start.37 = (f32[8,256]{1,0:T(8,128)S(1)}, f32[8,256]{1,0:T(8,128)S(1)}, u32[]{:S(2)}, u32[]{:S(2)}) collective-permute-start(f32[8,256]{1,0:T(8,128)S(1)} %get-tuple-element.98), channel_id=1, source_target_pairs={{0,16},{1,17},{2,18},{3,19},{4,20},{5,21},{6,22},{7,23},{8,24},{9,... | collective-permute-start | bytes 24584 | tf_op jit(solution)/shard_map/ppermute | solution.py:134
  73.4 1.5 %collective-permute-start.40 = (f32[8,256]{1,0:T(8,128)S(1)}, f32[8,256]{1,0:T(8,128)S(1)}, u32[]{:S(2)}, u32[]{:S(2)}) collective-permute-start(f32[8,256]{1,0:T(8,128)S(1)} %get-tuple-element.102), channel_id=1, source_target_pairs={{0,16},{1,17},{2,18},{3,19},{4,20},{5,21},{6,22},{7,23},{8,24},{9,... | collective-permute-start | bytes 24584 | tf_op jit(solution)/shard_map/ppermute | solution.py:134
  78.6 1.5 %collective-permute-start.43 = (f32[8,256]{1,0:T(8,128)S(1)}, f32[8,256]{1,0:T(8,128)S(1)}, u32[]{:S(2)}, u32[]{:S(2)}) collective-permute-start(f32[8,256]{1,0:T(8,128)S(1)} %get-tuple-element.107), channel_id=1, source_target_pairs={{0,16},{1,17},{2,18},{3,19},{4,20},{5,21},{6,22},{7,23},{8,24},{9,... | collective-permute-start | bytes 24584 | tf_op jit(solution)/shard_map/ppermute | solution.py:134
  82.4 2.1 %collective-permute-start.47 = (f32[2,8,256]{2,1,0:T(8,128)S(1)}, f32[2,8,256]{2,1,0:T(8,128)S(1)}, u32[]{:S(2)}, u32[]{:S(2)}) collective-permute-start(f32[2,8,256]{2,1,0:T(8,128)S(1)} %get-tuple-element.112), channel_id=1, source_target_pairs={{0,4},{1,7},{2,6},{3,5},{4,0},{5,3},{6,2},{7,1},{8,12},{9,15},{10,... | collective-permute-start | bytes 49160 | tf_op jit(solution)/shard_map/ppermute | solution.py:134
  84.5 1.6 %collective-permute-start.46 = (f32[2,8,256]{2,1,0:T(8,128)S(1)}, f32[2,8,256]{2,1,0:T(8,128)S(1)}, u32[]{:S(2)}, u32[]{:S(2)}) collective-permute-start(f32[2,8,256]{2,1,0:T(8,128)S(1)} %get-tuple-element.111), channel_id=1, source_target_pairs={{0,2},{1,3},{2,0},{3,1},{4,6},{5,7},{6,4},{7,5},{8,10},{9,11},{10,... | collective-permute-start | bytes 49160 | tf_op jit(solution)/shard_map/ppermute | solution.py:134
  87.1 1.3 %collective-permute-done.46.refs_1_ = f32[2,8,256]{2,1,0:T(8,128)S(1)} collective-permute-done((f32[2,8,256]{2,1,0:T(8,128)S(1)}, f32[2,8,256]{2,1,0:T(8,128)S(1)}, u32[]{:S(2)}, u32[]{:S(2)}) %collective-permute-start.46) | collective-permute-done | bytes 16416 | tf_op jit(solution)/shard_map/ppermute | solution.py:134
  (106 shorter events, 50.7 us)
Async XLA Ops:
  2.0 5.6 %collective-permute-start.1 = (f32[2,8,256]{2,1,0:T(8,128)S(1)}, f32[2,8,256]{2,1,0:T(8,128)S(1)}, u32[]{:S(2)}, u32[]{:S(2)}) collective-permute-start(f32[2,8,256]{2,1,0:T(8,128)S(1)} %get-tuple-element.61), channel_id=1, source_target_pairs={{0,4},{1,7},{2,6},{3,5},{4,0},{5,3},{6,2},{7,1},{8,12},{9,15},{10,... | collective-permute-start | bytes 49160 | tf_op jit(solution)/shard_map/ppermute | solution.py:134
  5.8 3.7 %collective-permute-start.2 = (f32[2,8,256]{2,1,0:T(8,128)S(1)}, f32[2,8,256]{2,1,0:T(8,128)S(1)}, u32[]{:S(2)}, u32[]{:S(2)}) collective-permute-start(f32[2,8,256]{2,1,0:T(8,128)S(1)} %get-tuple-element.65), channel_id=1, source_target_pairs={{0,2},{1,3},{2,0},{3,1},{4,6},{5,7},{6,4},{7,5},{8,10},{9,11},{10,... | collective-permute-start | bytes 49160 | tf_op jit(solution)/shard_map/ppermute | solution.py:134
  9.7 3.7 %collective-permute-start.5 = (f32[8,256]{1,0:T(8,128)S(1)}, f32[8,256]{1,0:T(8,128)S(1)}, u32[]{:S(2)}, u32[]{:S(2)}) collective-permute-start(f32[8,256]{1,0:T(8,128)S(1)} %get-tuple-element.66.refs_2_), channel_id=1, source_target_pairs={{0,8},{1,25},{2,10},{3,27},{4,12},{5,29},{6,14},{7,31},{8,0},{9,17... | collective-permute-start | bytes 24584 | tf_op jit(solution)/shard_map/ppermute | solution.py:134
  15.2 3.7 %collective-permute-start.8 = (f32[8,256]{1,0:T(8,128)S(1)}, f32[8,256]{1,0:T(8,128)S(1)}, u32[]{:S(2)}, u32[]{:S(2)}) collective-permute-start(f32[8,256]{1,0:T(8,128)S(1)} %get-tuple-element.69.refs_2_), channel_id=1, source_target_pairs={{0,8},{1,25},{2,10},{3,27},{4,12},{5,29},{6,14},{7,31},{8,0},{9,17... | collective-permute-start | bytes 24584 | tf_op jit(solution)/shard_map/ppermute | solution.py:134
  16.4 3.7 %collective-permute-start.7 = (f32[8,256]{1,0:T(8,128)S(1)}, f32[8,256]{1,0:T(8,128)S(1)}, u32[]{:S(2)}, u32[]{:S(2)}) collective-permute-start(f32[8,256]{1,0:T(8,128)S(1)} %get-tuple-element.69.refs_2_), channel_id=1, source_target_pairs={{0,16},{1,17},{2,18},{3,19},{4,20},{5,21},{6,22},{7,23},{8,24},{9,... | collective-permute-start | bytes 24584 | tf_op jit(solution)/shard_map/ppermute | solution.py:134
  20.3 3.7 %collective-permute-start.11 = (f32[8,256]{1,0:T(8,128)S(1)}, f32[8,256]{1,0:T(8,128)S(1)}, u32[]{:S(2)}, u32[]{:S(2)}) collective-permute-start(f32[8,256]{1,0:T(8,128)S(1)} %get-tuple-element.71.refs_2_), channel_id=1, source_target_pairs={{0,8},{1,25},{2,10},{3,27},{4,12},{5,29},{6,14},{7,31},{8,0},{9,17... | collective-permute-start | bytes 24584 | tf_op jit(solution)/shard_map/ppermute | solution.py:134
  21.5 3.7 %collective-permute-start.10 = (f32[8,256]{1,0:T(8,128)S(1)}, f32[8,256]{1,0:T(8,128)S(1)}, u32[]{:S(2)}, u32[]{:S(2)}) collective-permute-start(f32[8,256]{1,0:T(8,128)S(1)} %get-tuple-element.71.refs_2_), channel_id=1, source_target_pairs={{0,16},{1,17},{2,18},{3,19},{4,20},{5,21},{6,22},{7,23},{8,24},{9,... | collective-permute-start | bytes 24584 | tf_op jit(solution)/shard_map/ppermute | solution.py:134
  25.5 3.7 %collective-permute-start.14 = (f32[8,256]{1,0:T(8,128)S(1)}, f32[8,256]{1,0:T(8,128)S(1)}, u32[]{:S(2)}, u32[]{:S(2)}) collective-permute-start(f32[8,256]{1,0:T(8,128)S(1)} %get-tuple-element.73.refs_2_), channel_id=1, source_target_pairs={{0,8},{1,25},{2,10},{3,27},{4,12},{5,29},{6,14},{7,31},{8,0},{9,17... | collective-permute-start | bytes 24584 | tf_op jit(solution)/shard_map/ppermute | solution.py:134
  26.6 3.7 %collective-permute-start.13 = (f32[8,256]{1,0:T(8,128)S(1)}, f32[8,256]{1,0:T(8,128)S(1)}, u32[]{:S(2)}, u32[]{:S(2)}) collective-permute-start(f32[8,256]{1,0:T(8,128)S(1)} %get-tuple-element.73.refs_2_), channel_id=1, source_target_pairs={{0,16},{1,17},{2,18},{3,19},{4,20},{5,21},{6,22},{7,23},{8,24},{9,... | collective-permute-start | bytes 24584 | tf_op jit(solution)/shard_map/ppermute | solution.py:134
  30.6 3.7 %collective-permute-start.17 = (f32[8,256]{1,0:T(8,128)S(1)}, f32[8,256]{1,0:T(8,128)S(1)}, u32[]{:S(2)}, u32[]{:S(2)}) collective-permute-start(f32[8,256]{1,0:T(8,128)S(1)} %get-tuple-element.75.refs_2_), channel_id=1, source_target_pairs={{0,8},{1,25},{2,10},{3,27},{4,12},{5,29},{6,14},{7,31},{8,0},{9,17... | collective-permute-start | bytes 24584 | tf_op jit(solution)/shard_map/ppermute | solution.py:134
  31.8 3.7 %collective-permute-start.16 = (f32[8,256]{1,0:T(8,128)S(1)}, f32[8,256]{1,0:T(8,128)S(1)}, u32[]{:S(2)}, u32[]{:S(2)}) collective-permute-start(f32[8,256]{1,0:T(8,128)S(1)} %get-tuple-element.75.refs_2_), channel_id=1, source_target_pairs={{0,16},{1,17},{2,18},{3,19},{4,20},{5,21},{6,22},{7,23},{8,24},{9,... | collective-permute-start | bytes 24584 | tf_op jit(solution)/shard_map/ppermute | solution.py:134
  35.7 3.7 %collective-permute-start.20 = (f32[8,256]{1,0:T(8,128)S(1)}, f32[8,256]{1,0:T(8,128)S(1)}, u32[]{:S(2)}, u32[]{:S(2)}) collective-permute-start(f32[8,256]{1,0:T(8,128)S(1)} %get-tuple-element.77.refs_2_), channel_id=1, source_target_pairs={{0,8},{1,25},{2,10},{3,27},{4,12},{5,29},{6,14},{7,31},{8,0},{9,17... | collective-permute-start | bytes 24584 | tf_op jit(solution)/shard_map/ppermute | solution.py:134
  40.9 3.7 %collective-permute-start.23 = (f32[8,256]{1,0:T(8,128)S(1)}, f32[8,256]{1,0:T(8,128)S(1)}, u32[]{:S(2)}, u32[]{:S(2)}) collective-permute-start(f32[8,256]{1,0:T(8,128)S(1)} %get-tuple-element.79.refs_2_), channel_id=1, source_target_pairs={{0,8},{1,25},{2,10},{3,27},{4,12},{5,29},{6,14},{7,31},{8,0},{9,17... | collective-permute-start | bytes 24584 | tf_op jit(solution)/shard_map/ppermute | solution.py:134
  42.0 3.7 %collective-permute-start.22 = (f32[8,256]{1,0:T(8,128)S(1)}, f32[8,256]{1,0:T(8,128)S(1)}, u32[]{:S(2)}, u32[]{:S(2)}) collective-permute-start(f32[8,256]{1,0:T(8,128)S(1)} %get-tuple-element.79.refs_2_), channel_id=1, source_target_pairs={{0,16},{1,17},{2,18},{3,19},{4,20},{5,21},{6,22},{7,23},{8,24},{9,... | collective-permute-start | bytes 24584 | tf_op jit(solution)/shard_map/ppermute | solution.py:134
  46.3 3.7 %collective-permute-start.26 = (f32[8,256]{1,0:T(8,128)S(1)}, f32[8,256]{1,0:T(8,128)S(1)}, u32[]{:S(2)}, u32[]{:S(2)}) collective-permute-start(f32[8,256]{1,0:T(8,128)S(1)} %get-tuple-element.83), channel_id=1, source_target_pairs={{0,8},{1,25},{2,10},{3,27},{4,12},{5,29},{6,14},{7,31},{8,0},{9,17... | collective-permute-start | bytes 24584 | tf_op jit(solution)/shard_map/ppermute | solution.py:134
  47.5 3.7 %collective-permute-start.25 = (f32[8,256]{1,0:T(8,128)S(1)}, f32[8,256]{1,0:T(8,128)S(1)}, u32[]{:S(2)}, u32[]{:S(2)}) collective-permute-start(f32[8,256]{1,0:T(8,128)S(1)} %get-tuple-element.82), channel_id=1, source_target_pairs={{0,16},{1,17},{2,18},{3,19},{4,20},{5,21},{6,22},{7,23},{8,24},{9,... | collective-permute-start | bytes 24584 | tf_op jit(solution)/shard_map/ppermute | solution.py:134
  51.4 3.7 %collective-permute-start.29 = (f32[8,256]{1,0:T(8,128)S(1)}, f32[8,256]{1,0:T(8,128)S(1)}, u32[]{:S(2)}, u32[]{:S(2)}) collective-permute-start(f32[8,256]{1,0:T(8,128)S(1)} %get-tuple-element.87), channel_id=1, source_target_pairs={{0,8},{1,25},{2,10},{3,27},{4,12},{5,29},{6,14},{7,31},{8,0},{9,17... | collective-permute-start | bytes 24584 | tf_op jit(solution)/shard_map/ppermute | solution.py:134
  56.6 3.7 %collective-permute-start.32 = (f32[8,256]{1,0:T(8,128)S(1)}, f32[8,256]{1,0:T(8,128)S(1)}, u32[]{:S(2)}, u32[]{:S(2)}) collective-permute-start(f32[8,256]{1,0:T(8,128)S(1)} %get-tuple-element.91), channel_id=1, source_target_pairs={{0,8},{1,25},{2,10},{3,27},{4,12},{5,29},{6,14},{7,31},{8,0},{9,17... | collective-permute-start | bytes 24584 | tf_op jit(solution)/shard_map/ppermute | solution.py:134
  61.8 3.7 %collective-permute-start.35 = (f32[8,256]{1,0:T(8,128)S(1)}, f32[8,256]{1,0:T(8,128)S(1)}, u32[]{:S(2)}, u32[]{:S(2)}) collective-permute-start(f32[8,256]{1,0:T(8,128)S(1)} %get-tuple-element.95), channel_id=1, source_target_pairs={{0,8},{1,25},{2,10},{3,27},{4,12},{5,29},{6,14},{7,31},{8,0},{9,17... | collective-permute-start | bytes 24584 | tf_op jit(solution)/shard_map/ppermute | solution.py:134
  67.0 3.7 %collective-permute-start.38 = (f32[8,256]{1,0:T(8,128)S(1)}, f32[8,256]{1,0:T(8,128)S(1)}, u32[]{:S(2)}, u32[]{:S(2)}) collective-permute-start(f32[8,256]{1,0:T(8,128)S(1)} %get-tuple-element.99), channel_id=1, source_target_pairs={{0,8},{1,25},{2,10},{3,27},{4,12},{5,29},{6,14},{7,31},{8,0},{9,17... | collective-permute-start | bytes 24584 | tf_op jit(solution)/shard_map/ppermute | solution.py:134
  72.1 3.7 %collective-permute-start.41 = (f32[8,256]{1,0:T(8,128)S(1)}, f32[8,256]{1,0:T(8,128)S(1)}, u32[]{:S(2)}, u32[]{:S(2)}) collective-permute-start(f32[8,256]{1,0:T(8,128)S(1)} %get-tuple-element.103), channel_id=1, source_target_pairs={{0,8},{1,25},{2,10},{3,27},{4,12},{5,29},{6,14},{7,31},{8,0},{9,17... | collective-permute-start | bytes 24584 | tf_op jit(solution)/shard_map/ppermute | solution.py:134
  77.3 3.7 %collective-permute-start.44 = (f32[8,256]{1,0:T(8,128)S(1)}, f32[8,256]{1,0:T(8,128)S(1)}, u32[]{:S(2)}, u32[]{:S(2)}) collective-permute-start(f32[8,256]{1,0:T(8,128)S(1)} %get-tuple-element.108), channel_id=1, source_target_pairs={{0,8},{1,25},{2,10},{3,27},{4,12},{5,29},{6,14},{7,31},{8,0},{9,17... | collective-permute-start | bytes 24584 | tf_op jit(solution)/shard_map/ppermute | solution.py:134
  82.4 4.7 %collective-permute-start.47 = (f32[2,8,256]{2,1,0:T(8,128)S(1)}, f32[2,8,256]{2,1,0:T(8,128)S(1)}, u32[]{:S(2)}, u32[]{:S(2)}) collective-permute-start(f32[2,8,256]{2,1,0:T(8,128)S(1)} %get-tuple-element.112), channel_id=1, source_target_pairs={{0,4},{1,7},{2,6},{3,5},{4,0},{5,3},{6,2},{7,1},{8,12},{9,15},{10,... | collective-permute-start | bytes 49160 | tf_op jit(solution)/shard_map/ppermute | solution.py:134
  84.5 3.9 %collective-permute-start.46 = (f32[2,8,256]{2,1,0:T(8,128)S(1)}, f32[2,8,256]{2,1,0:T(8,128)S(1)}, u32[]{:S(2)}, u32[]{:S(2)}) collective-permute-start(f32[2,8,256]{2,1,0:T(8,128)S(1)} %get-tuple-element.111), channel_id=1, source_target_pairs={{0,2},{1,3},{2,0},{3,1},{4,6},{5,7},{6,4},{7,5},{8,10},{9,11},{10,... | collective-permute-start | bytes 49160 | tf_op jit(solution)/shard_map/ppermute | solution.py:134
  (27 other events, 88.7 us)

commit v9 on v8

--- a/solution.py
+++ b/solution.py
@@ -115,7 +115,7 @@
     own_rows = VMEM((levels, each, size), F32)
     all_rows = VMEM((levels * owners, each, size), F32)
     packed_rows = VMEM((columns, each, size), F32)
-    row_routes, layer_routes = routes(owners, (1, 3, 2)), routes(layers, (2, 3, 1))
+    row_routes, layer_routes = routes(owners, (2, 3, 1)), routes(layers, (2, 3, 1))
     dma = pltpu.SemaphoreType.DMA
 
     def swap(array):

time: 89.4 us -> 89.4 us (level)
  no operation moved by 1% of the time
where the time goes in v9:
time: 89.4 us; the launch traced here: 89.2 us
  starting transfers between devices  48.1 us (54%)
  waiting for transfers between devices  31.8 us (36%)
  Pallas kernels  9.18 us (10%)
    ppermute x32, starting transfers between devices, send(): return lax.ppermute(array, ('row', 'col'), steps)  47.1 us
    ppermute x32, waiting for transfers between devices, send(): return lax.ppermute(array, ('row', 'col'), steps)  31.7 us
    pallas_call x28, Pallas kernels, call(): pl.pallas_call(kernel, in_specs=[spec(key) for key in in_names], out_spec...  9.18 us
  transfers between devices with their start and end apart: 49, of which 32 were waited for; matrix products, arithmetic and copies ran while one was open for 0% of the time, Pallas kernels for 4%

profile of v9, /device:TPU:0, one launch (start us, length us, event | category | flops | bytes accessed | tf_op | source)
XLA Modules:
  0.0 89.2 jit_solution(2448636988956749905)
XLA Ops:
  0.5 1.4 %pack.1 = (f32[32,256]{1,0:T(8,128)S(1)}, bf16[256,256]{1,0:T(8,128)(2,1)S(1)}, bf16[256,256]{1,0:T(8,128)(2,1)S(1)}, bf16[3,256,256]{2,1,0:T(8,128)(2,1)S(1)}) custom-call(f32[8,1,32,32]{3,2,1,0:T(8,128)} %refs_0_.7, bf16[8,1,256,256]{3,2,1,0:T(8,128)(2,1)} %refs_1_.25, bf16[7,1,3,256,256]{4,3,2,1,0:T(8,128)(2,1)} %refs_2_.13), custom_call_target="tpu_custom_call" | custom-call | tf_op jit(solution)/shard_map/pack/pallas_call | solution.py:93
  2.0 3.7 %collective-permute-start.1 = (f32[2,8,256]{2,1,0:T(8,128)S(1)}, f32[2,8,256]{2,1,0:T(8,128)S(1)}, u32[]{:S(2)}, u32[]{:S(2)}) collective-permute-start(f32[2,8,256]{2,1,0:T(8,128)S(1)} %get-tuple-element.61), channel_id=1, source_target_pairs={{0,4},{1,7},{2,6},{3,5},{4,0},{5,3},{6,2},{7,1},{8,12},{9,15},{10,... | collective-permute-start | bytes 49160 | tf_op jit(solution)/shard_map/ppermute | solution.py:134
  5.8 1.6 %collective-permute-start.2 = (f32[2,8,256]{2,1,0:T(8,128)S(1)}, f32[2,8,256]{2,1,0:T(8,128)S(1)}, u32[]{:S(2)}, u32[]{:S(2)}) collective-permute-start(f32[2,8,256]{2,1,0:T(8,128)S(1)} %get-tuple-element.65), channel_id=1, source_target_pairs={{0,2},{1,3},{2,0},{3,1},{4,6},{5,7},{6,4},{7,5},{8,10},{9,11},{10,... | collective-permute-start | bytes 49160 | tf_op jit(solution)/shard_map/ppermute | solution.py:134
  9.7 1.5 %collective-permute-start.5 = (f32[8,256]{1,0:T(8,128)S(1)}, f32[8,256]{1,0:T(8,128)S(1)}, u32[]{:S(2)}, u32[]{:S(2)}) collective-permute-start(f32[8,256]{1,0:T(8,128)S(1)} %get-tuple-element.66.refs_2_), channel_id=1, source_target_pairs={{0,16},{1,25},{2,18},{3,27},{4,20},{5,29},{6,22},{7,31},{8,24},{9,... | collective-permute-start | bytes 24584 | tf_op jit(solution)/shard_map/ppermute | solution.py:134
  11.3 1.5 %collective-permute-start.4 = (f32[8,256]{1,0:T(8,128)S(1)}, f32[8,256]{1,0:T(8,128)S(1)}, u32[]{:S(2)}, u32[]{:S(2)}) collective-permute-start(f32[8,256]{1,0:T(8,128)S(1)} %get-tuple-element.66.refs_2_), channel_id=1, source_target_pairs={{0,8},{1,9},{2,10},{3,11},{4,12},{5,13},{6,14},{7,15},{8,0},{9,1},... | collective-permute-start | bytes 24584 | tf_op jit(solution)/shard_map/ppermute | solution.py:134
  16.4 1.5 %collective-permute-start.7 = (f32[8,256]{1,0:T(8,128)S(1)}, f32[8,256]{1,0:T(8,128)S(1)}, u32[]{:S(2)}, u32[]{:S(2)}) collective-permute-start(f32[8,256]{1,0:T(8,128)S(1)} %get-tuple-element.69.refs_2_), channel_id=1, source_target_pairs={{0,8},{1,9},{2,10},{3,11},{4,12},{5,13},{6,14},{7,15},{8,0},{9,1},... | collective-permute-start | bytes 24584 | tf_op jit(solution)/shard_map/ppermute | solution.py:134
  21.5 1.5 %collective-permute-start.10 = (f32[8,256]{1,0:T(8,128)S(1)}, f32[8,256]{1,0:T(8,128)S(1)}, u32[]{:S(2)}, u32[]{:S(2)}) collective-permute-start(f32[8,256]{1,0:T(8,128)S(1)} %get-tuple-element.71.refs_2_), channel_id=1, source_target_pairs={{0,8},{1,9},{2,10},{3,11},{4,12},{5,13},{6,14},{7,15},{8,0},{9,1},... | collective-permute-start | bytes 24584 | tf_op jit(solution)/shard_map/ppermute | solution.py:134
  26.7 1.5 %collective-permute-start.13 = (f32[8,256]{1,0:T(8,128)S(1)}, f32[8,256]{1,0:T(8,128)S(1)}, u32[]{:S(2)}, u32[]{:S(2)}) collective-permute-start(f32[8,256]{1,0:T(8,128)S(1)} %get-tuple-element.73.refs_2_), channel_id=1, source_target_pairs={{0,8},{1,9},{2,10},{3,11},{4,12},{5,13},{6,14},{7,15},{8,0},{9,1},... | collective-permute-start | bytes 24584 | tf_op jit(solution)/shard_map/ppermute | solution.py:134
  31.8 1.5 %collective-permute-start.16 = (f32[8,256]{1,0:T(8,128)S(1)}, f32[8,256]{1,0:T(8,128)S(1)}, u32[]{:S(2)}, u32[]{:S(2)}) collective-permute-start(f32[8,256]{1,0:T(8,128)S(1)} %get-tuple-element.75.refs_2_), channel_id=1, source_target_pairs={{0,8},{1,9},{2,10},{3,11},{4,12},{5,13},{6,14},{7,15},{8,0},{9,1},... | collective-permute-start | bytes 24584 | tf_op jit(solution)/shard_map/ppermute | solution.py:134
  36.9 1.5 %collective-permute-start.19 = (f32[8,256]{1,0:T(8,128)S(1)}, f32[8,256]{1,0:T(8,128)S(1)}, u32[]{:S(2)}, u32[]{:S(2)}) collective-permute-start(f32[8,256]{1,0:T(8,128)S(1)} %get-tuple-element.77.refs_2_), channel_id=1, source_target_pairs={{0,8},{1,9},{2,10},{3,11},{4,12},{5,13},{6,14},{7,15},{8,0},{9,1},... | collective-permute-start | bytes 24584 | tf_op jit(solution)/shard_map/ppermute | solution.py:134
  42.1 1.5 %collective-permute-start.22 = (f32[8,256]{1,0:T(8,128)S(1)}, f32[8,256]{1,0:T(8,128)S(1)}, u32[]{:S(2)}, u32[]{:S(2)}) collective-permute-start(f32[8,256]{1,0:T(8,128)S(1)} %get-tuple-element.79.refs_2_), channel_id=1, source_target_pairs={{0,8},{1,9},{2,10},{3,11},{4,12},{5,13},{6,14},{7,15},{8,0},{9,1},... | collective-permute-start | bytes 24584 | tf_op jit(solution)/shard_map/ppermute | solution.py:134
  47.5 1.5 %collective-permute-start.25 = (f32[8,256]{1,0:T(8,128)S(1)}, f32[8,256]{1,0:T(8,128)S(1)}, u32[]{:S(2)}, u32[]{:S(2)}) collective-permute-start(f32[8,256]{1,0:T(8,128)S(1)} %get-tuple-element.82), channel_id=1, source_target_pairs={{0,8},{1,9},{2,10},{3,11},{4,12},{5,13},{6,14},{7,15},{8,0},{9,1},... | collective-permute-start | bytes 24584 | tf_op jit(solution)/shard_map/ppermute | solution.py:134
  51.5 1.2 %collective-permute-start.29 = (f32[8,256]{1,0:T(8,128)S(1)}, f32[8,256]{1,0:T(8,128)S(1)}, u32[]{:S(2)}, u32[]{:S(2)}) collective-permute-start(f32[8,256]{1,0:T(8,128)S(1)} %get-tuple-element.87), channel_id=1, source_target_pairs={{0,16},{1,25},{2,18},{3,27},{4,20},{5,29},{6,22},{7,31},{8,24},{9,... | collective-permute-start | bytes 24584 | tf_op jit(solution)/shard_map/ppermute | solution.py:134
  52.7 1.5 %collective-permute-start.28 = (f32[8,256]{1,0:T(8,128)S(1)}, f32[8,256]{1,0:T(8,128)S(1)}, u32[]{:S(2)}, u32[]{:S(2)}) collective-permute-start(f32[8,256]{1,0:T(8,128)S(1)} %get-tuple-element.86), channel_id=1, source_target_pairs={{0,8},{1,9},{2,10},{3,11},{4,12},{5,13},{6,14},{7,15},{8,0},{9,1},... | collective-permute-start | bytes 24584 | tf_op jit(solution)/shard_map/ppermute | solution.py:134
  57.9 1.5 %collective-permute-start.31 = (f32[8,256]{1,0:T(8,128)S(1)}, f32[8,256]{1,0:T(8,128)S(1)}, u32[]{:S(2)}, u32[]{:S(2)}) collective-permute-start(f32[8,256]{1,0:T(8,128)S(1)} %get-tuple-element.90), channel_id=1, source_target_pairs={{0,8},{1,9},{2,10},{3,11},{4,12},{5,13},{6,14},{7,15},{8,0},{9,1},... | collective-permute-start | bytes 24584 | tf_op jit(solution)/shard_map/ppermute | solution.py:134
  63.1 1.5 %collective-permute-start.34 = (f32[8,256]{1,0:T(8,128)S(1)}, f32[8,256]{1,0:T(8,128)S(1)}, u32[]{:S(2)}, u32[]{:S(2)}) collective-permute-start(f32[8,256]{1,0:T(8,128)S(1)} %get-tuple-element.94), channel_id=1, source_target_pairs={{0,8},{1,9},{2,10},{3,11},{4,12},{5,13},{6,14},{7,15},{8,0},{9,1},... | collective-permute-start | bytes 24584 | tf_op jit(solution)/shard_map/ppermute | solution.py:134
  68.2 1.5 %collective-permute-start.37 = (f32[8,256]{1,0:T(8,128)S(1)}, f32[8,256]{1,0:T(8,128)S(1)}, u32[]{:S(2)}, u32[]{:S(2)}) collective-permute-start(f32[8,256]{1,0:T(8,128)S(1)} %get-tuple-element.98), channel_id=1, source_target_pairs={{0,8},{1,9},{2,10},{3,11},{4,12},{5,13},{6,14},{7,15},{8,0},{9,1},... | collective-permute-start | bytes 24584 | tf_op jit(solution)/shard_map/ppermute | solution.py:134
  72.2 1.2 %collective-permute-start.41 = (f32[8,256]{1,0:T(8,128)S(1)}, f32[8,256]{1,0:T(8,128)S(1)}, u32[]{:S(2)}, u32[]{:S(2)}) collective-permute-start(f32[8,256]{1,0:T(8,128)S(1)} %get-tuple-element.103), channel_id=1, source_target_pairs={{0,16},{1,25},{2,18},{3,27},{4,20},{5,29},{6,22},{7,31},{8,24},{9,... | collective-permute-start | bytes 24584 | tf_op jit(solution)/shard_map/ppermute | solution.py:134
  73.4 1.5 %collective-permute-start.40 = (f32[8,256]{1,0:T(8,128)S(1)}, f32[8,256]{1,0:T(8,128)S(1)}, u32[]{:S(2)}, u32[]{:S(2)}) collective-permute-start(f32[8,256]{1,0:T(8,128)S(1)} %get-tuple-element.102), channel_id=1, source_target_pairs={{0,8},{1,9},{2,10},{3,11},{4,12},{5,13},{6,14},{7,15},{8,0},{9,1},... | collective-permute-start | bytes 24584 | tf_op jit(solution)/shard_map/ppermute | solution.py:134
  77.4 1.2 %collective-permute-start.44 = (f32[8,256]{1,0:T(8,128)S(1)}, f32[8,256]{1,0:T(8,128)S(1)}, u32[]{:S(2)}, u32[]{:S(2)}) collective-permute-start(f32[8,256]{1,0:T(8,128)S(1)} %get-tuple-element.108), channel_id=1, source_target_pairs={{0,16},{1,25},{2,18},{3,27},{4,20},{5,29},{6,22},{7,31},{8,24},{9,... | collective-permute-start | bytes 24584 | tf_op jit(solution)/shard_map/ppermute | solution.py:134
  78.6 1.5 %collective-permute-start.43 = (f32[8,256]{1,0:T(8,128)S(1)}, f32[8,256]{1,0:T(8,128)S(1)}, u32[]{:S(2)}, u32[]{:S(2)}) collective-permute-start(f32[8,256]{1,0:T(8,128)S(1)} %get-tuple-element.107), channel_id=1, source_target_pairs={{0,8},{1,9},{2,10},{3,11},{4,12},{5,13},{6,14},{7,15},{8,0},{9,1},... | collective-permute-start | bytes 24584 | tf_op jit(solution)/shard_map/ppermute | solution.py:134
  82.5 2.1 %collective-permute-start.47 = (f32[2,8,256]{2,1,0:T(8,128)S(1)}, f32[2,8,256]{2,1,0:T(8,128)S(1)}, u32[]{:S(2)}, u32[]{:S(2)}) collective-permute-start(f32[2,8,256]{2,1,0:T(8,128)S(1)} %get-tuple-element.112), channel_id=1, source_target_pairs={{0,4},{1,7},{2,6},{3,5},{4,0},{5,3},{6,2},{7,1},{8,12},{9,15},{10,... | collective-permute-start | bytes 49160 | tf_op jit(solution)/shard_map/ppermute | solution.py:134
  84.6 1.6 %collective-permute-start.46 = (f32[2,8,256]{2,1,0:T(8,128)S(1)}, f32[2,8,256]{2,1,0:T(8,128)S(1)}, u32[]{:S(2)}, u32[]{:S(2)}) collective-permute-start(f32[2,8,256]{2,1,0:T(8,128)S(1)} %get-tuple-element.111), channel_id=1, source_target_pairs={{0,2},{1,3},{2,0},{3,1},{4,6},{5,7},{6,4},{7,5},{8,10},{9,11},{10,... | collective-permute-start | bytes 49160 | tf_op jit(solution)/shard_map/ppermute | solution.py:134
  87.1 1.3 %collective-permute-done.46.refs_1_ = f32[2,8,256]{2,1,0:T(8,128)S(1)} collective-permute-done((f32[2,8,256]{2,1,0:T(8,128)S(1)}, f32[2,8,256]{2,1,0:T(8,128)S(1)}, u32[]{:S(2)}, u32[]{:S(2)}) %collective-permute-start.46) | collective-permute-done | bytes 16416 | tf_op jit(solution)/shard_map/ppermute | solution.py:134
  (106 shorter events, 51.1 us)
Async XLA Ops:
  2.0 5.6 %collective-permute-start.1 = (f32[2,8,256]{2,1,0:T(8,128)S(1)}, f32[2,8,256]{2,1,0:T(8,128)S(1)}, u32[]{:S(2)}, u32[]{:S(2)}) collective-permute-start(f32[2,8,256]{2,1,0:T(8,128)S(1)} %get-tuple-element.61), channel_id=1, source_target_pairs={{0,4},{1,7},{2,6},{3,5},{4,0},{5,3},{6,2},{7,1},{8,12},{9,15},{10,... | collective-permute-start | bytes 49160 | tf_op jit(solution)/shard_map/ppermute | solution.py:134
  5.8 3.7 %collective-permute-start.2 = (f32[2,8,256]{2,1,0:T(8,128)S(1)}, f32[2,8,256]{2,1,0:T(8,128)S(1)}, u32[]{:S(2)}, u32[]{:S(2)}) collective-permute-start(f32[2,8,256]{2,1,0:T(8,128)S(1)} %get-tuple-element.65), channel_id=1, source_target_pairs={{0,2},{1,3},{2,0},{3,1},{4,6},{5,7},{6,4},{7,5},{8,10},{9,11},{10,... | collective-permute-start | bytes 49160 | tf_op jit(solution)/shard_map/ppermute | solution.py:134
  9.7 3.7 %collective-permute-start.5 = (f32[8,256]{1,0:T(8,128)S(1)}, f32[8,256]{1,0:T(8,128)S(1)}, u32[]{:S(2)}, u32[]{:S(2)}) collective-permute-start(f32[8,256]{1,0:T(8,128)S(1)} %get-tuple-element.66.refs_2_), channel_id=1, source_target_pairs={{0,16},{1,25},{2,18},{3,27},{4,20},{5,29},{6,22},{7,31},{8,24},{9,... | collective-permute-start | bytes 24584 | tf_op jit(solution)/shard_map/ppermute | solution.py:134
  11.3 3.7 %collective-permute-start.4 = (f32[8,256]{1,0:T(8,128)S(1)}, f32[8,256]{1,0:T(8,128)S(1)}, u32[]{:S(2)}, u32[]{:S(2)}) collective-permute-start(f32[8,256]{1,0:T(8,128)S(1)} %get-tuple-element.66.refs_2_), channel_id=1, source_target_pairs={{0,8},{1,9},{2,10},{3,11},{4,12},{5,13},{6,14},{7,15},{8,0},{9,1},... | collective-permute-start | bytes 24584 | tf_op jit(solution)/shard_map/ppermute | solution.py:134
  15.2 3.7 %collective-permute-start.8 = (f32[8,256]{1,0:T(8,128)S(1)}, f32[8,256]{1,0:T(8,128)S(1)}, u32[]{:S(2)}, u32[]{:S(2)}) collective-permute-start(f32[8,256]{1,0:T(8,128)S(1)} %get-tuple-element.69.refs_2_), channel_id=1, source_target_pairs={{0,16},{1,25},{2,18},{3,27},{4,20},{5,29},{6,22},{7,31},{8,24},{9,... | collective-permute-start | bytes 24584 | tf_op jit(solution)/shard_map/ppermute | solution.py:134
  20.4 3.7 %collective-permute-start.11 = (f32[8,256]{1,0:T(8,128)S(1)}, f32[8,256]{1,0:T(8,128)S(1)}, u32[]{:S(2)}, u32[]{:S(2)}) collective-permute-start(f32[8,256]{1,0:T(8,128)S(1)} %get-tuple-element.71.refs_2_), channel_id=1, source_target_pairs={{0,16},{1,25},{2,18},{3,27},{4,20},{5,29},{6,22},{7,31},{8,24},{9,... | collective-permute-start | bytes 24584 | tf_op jit(solution)/shard_map/ppermute | solution.py:134
  25.5 3.7 %collective-permute-start.14 = (f32[8,256]{1,0:T(8,128)S(1)}, f32[8,256]{1,0:T(8,128)S(1)}, u32[]{:S(2)}, u32[]{:S(2)}) collective-permute-start(f32[8,256]{1,0:T(8,128)S(1)} %get-tuple-element.73.refs_2_), channel_id=1, source_target_pairs={{0,16},{1,25},{2,18},{3,27},{4,20},{5,29},{6,22},{7,31},{8,24},{9,... | collective-permute-start | bytes 24584 | tf_op jit(solution)/shard_map/ppermute | solution.py:134
  26.7 3.7 %collective-permute-start.13 = (f32[8,256]{1,0:T(8,128)S(1)}, f32[8,256]{1,0:T(8,128)S(1)}, u32[]{:S(2)}, u32[]{:S(2)}) collective-permute-start(f32[8,256]{1,0:T(8,128)S(1)} %get-tuple-element.73.refs_2_), channel_id=1, source_target_pairs={{0,8},{1,9},{2,10},{3,11},{4,12},{5,13},{6,14},{7,15},{8,0},{9,1},... | collective-permute-start | bytes 24584 | tf_op jit(solution)/shard_map/ppermute | solution.py:134
  30.6 3.7 %collective-permute-start.17 = (f32[8,256]{1,0:T(8,128)S(1)}, f32[8,256]{1,0:T(8,128)S(1)}, u32[]{:S(2)}, u32[]{:S(2)}) collective-permute-start(f32[8,256]{1,0:T(8,128)S(1)} %get-tuple-element.75.refs_2_), channel_id=1, source_target_pairs={{0,16},{1,25},{2,18},{3,27},{4,20},{5,29},{6,22},{7,31},{8,24},{9,... | collective-permute-start | bytes 24584 | tf_op jit(solution)/shard_map/ppermute | solution.py:134
  31.8 3.7 %collective-permute-start.16 = (f32[8,256]{1,0:T(8,128)S(1)}, f32[8,256]{1,0:T(8,128)S(1)}, u32[]{:S(2)}, u32[]{:S(2)}) collective-permute-start(f32[8,256]{1,0:T(8,128)S(1)} %get-tuple-element.75.refs_2_), channel_id=1, source_target_pairs={{0,8},{1,9},{2,10},{3,11},{4,12},{5,13},{6,14},{7,15},{8,0},{9,1},... | collective-permute-start | bytes 24584 | tf_op jit(solution)/shard_map/ppermute | solution.py:134
  35.8 3.7 %collective-permute-start.20 = (f32[8,256]{1,0:T(8,128)S(1)}, f32[8,256]{1,0:T(8,128)S(1)}, u32[]{:S(2)}, u32[]{:S(2)}) collective-permute-start(f32[8,256]{1,0:T(8,128)S(1)} %get-tuple-element.77.refs_2_), channel_id=1, source_target_pairs={{0,16},{1,25},{2,18},{3,27},{4,20},{5,29},{6,22},{7,31},{8,24},{9,... | collective-permute-start | bytes 24584 | tf_op jit(solution)/shard_map/ppermute | solution.py:134
  36.9 3.7 %collective-permute-start.19 = (f32[8,256]{1,0:T(8,128)S(1)}, f32[8,256]{1,0:T(8,128)S(1)}, u32[]{:S(2)}, u32[]{:S(2)}) collective-permute-start(f32[8,256]{1,0:T(8,128)S(1)} %get-tuple-element.77.refs_2_), channel_id=1, source_target_pairs={{0,8},{1,9},{2,10},{3,11},{4,12},{5,13},{6,14},{7,15},{8,0},{9,1},... | collective-permute-start | bytes 24584 | tf_op jit(solution)/shard_map/ppermute | solution.py:134
  40.9 3.7 %collective-permute-start.23 = (f32[8,256]{1,0:T(8,128)S(1)}, f32[8,256]{1,0:T(8,128)S(1)}, u32[]{:S(2)}, u32[]{:S(2)}) collective-permute-start(f32[8,256]{1,0:T(8,128)S(1)} %get-tuple-element.79.refs_2_), channel_id=1, source_target_pairs={{0,16},{1,25},{2,18},{3,27},{4,20},{5,29},{6,22},{7,31},{8,24},{9,... | collective-permute-start | bytes 24584 | tf_op jit(solution)/shard_map/ppermute | solution.py:134
  42.1 3.7 %collective-permute-start.22 = (f32[8,256]{1,0:T(8,128)S(1)}, f32[8,256]{1,0:T(8,128)S(1)}, u32[]{:S(2)}, u32[]{:S(2)}) collective-permute-start(f32[8,256]{1,0:T(8,128)S(1)} %get-tuple-element.79.refs_2_), channel_id=1, source_target_pairs={{0,8},{1,9},{2,10},{3,11},{4,12},{5,13},{6,14},{7,15},{8,0},{9,1},... | collective-permute-start | bytes 24584 | tf_op jit(solution)/shard_map/ppermute | solution.py:134
  46.3 3.7 %collective-permute-start.26 = (f32[8,256]{1,0:T(8,128)S(1)}, f32[8,256]{1,0:T(8,128)S(1)}, u32[]{:S(2)}, u32[]{:S(2)}) collective-permute-start(f32[8,256]{1,0:T(8,128)S(1)} %get-tuple-element.83), channel_id=1, source_target_pairs={{0,16},{1,25},{2,18},{3,27},{4,20},{5,29},{6,22},{7,31},{8,24},{9,... | collective-permute-start | bytes 24584 | tf_op jit(solution)/shard_map/ppermute | solution.py:134
  47.5 3.7 %collective-permute-start.25 = (f32[8,256]{1,0:T(8,128)S(1)}, f32[8,256]{1,0:T(8,128)S(1)}, u32[]{:S(2)}, u32[]{:S(2)}) collective-permute-start(f32[8,256]{1,0:T(8,128)S(1)} %get-tuple-element.82), channel_id=1, source_target_pairs={{0,8},{1,9},{2,10},{3,11},{4,12},{5,13},{6,14},{7,15},{8,0},{9,1},... | collective-permute-start | bytes 24584 | tf_op jit(solution)/shard_map/ppermute | solution.py:134
  51.5 3.7 %collective-permute-start.29 = (f32[8,256]{1,0:T(8,128)S(1)}, f32[8,256]{1,0:T(8,128)S(1)}, u32[]{:S(2)}, u32[]{:S(2)}) collective-permute-start(f32[8,256]{1,0:T(8,128)S(1)} %get-tuple-element.87), channel_id=1, source_target_pairs={{0,16},{1,25},{2,18},{3,27},{4,20},{5,29},{6,22},{7,31},{8,24},{9,... | collective-permute-start | bytes 24584 | tf_op jit(solution)/shard_map/ppermute | solution.py:134
  56.6 3.7 %collective-permute-start.32 = (f32[8,256]{1,0:T(8,128)S(1)}, f32[8,256]{1,0:T(8,128)S(1)}, u32[]{:S(2)}, u32[]{:S(2)}) collective-permute-start(f32[8,256]{1,0:T(8,128)S(1)} %get-tuple-element.91), channel_id=1, source_target_pairs={{0,16},{1,25},{2,18},{3,27},{4,20},{5,29},{6,22},{7,31},{8,24},{9,... | collective-permute-start | bytes 24584 | tf_op jit(solution)/shard_map/ppermute | solution.py:134
  61.8 3.7 %collective-permute-start.35 = (f32[8,256]{1,0:T(8,128)S(1)}, f32[8,256]{1,0:T(8,128)S(1)}, u32[]{:S(2)}, u32[]{:S(2)}) collective-permute-start(f32[8,256]{1,0:T(8,128)S(1)} %get-tuple-element.95), channel_id=1, source_target_pairs={{0,16},{1,25},{2,18},{3,27},{4,20},{5,29},{6,22},{7,31},{8,24},{9,... | collective-permute-start | bytes 24584 | tf_op jit(solution)/shard_map/ppermute | solution.py:134
  67.0 3.7 %collective-permute-start.38 = (f32[8,256]{1,0:T(8,128)S(1)}, f32[8,256]{1,0:T(8,128)S(1)}, u32[]{:S(2)}, u32[]{:S(2)}) collective-permute-start(f32[8,256]{1,0:T(8,128)S(1)} %get-tuple-element.99), channel_id=1, source_target_pairs={{0,16},{1,25},{2,18},{3,27},{4,20},{5,29},{6,22},{7,31},{8,24},{9,... | collective-permute-start | bytes 24584 | tf_op jit(solution)/shard_map/ppermute | solution.py:134
  72.2 3.7 %collective-permute-start.41 = (f32[8,256]{1,0:T(8,128)S(1)}, f32[8,256]{1,0:T(8,128)S(1)}, u32[]{:S(2)}, u32[]{:S(2)}) collective-permute-start(f32[8,256]{1,0:T(8,128)S(1)} %get-tuple-element.103), channel_id=1, source_target_pairs={{0,16},{1,25},{2,18},{3,27},{4,20},{5,29},{6,22},{7,31},{8,24},{9,... | collective-permute-start | bytes 24584 | tf_op jit(solution)/shard_map/ppermute | solution.py:134
  77.4 3.7 %collective-permute-start.44 = (f32[8,256]{1,0:T(8,128)S(1)}, f32[8,256]{1,0:T(8,128)S(1)}, u32[]{:S(2)}, u32[]{:S(2)}) collective-permute-start(f32[8,256]{1,0:T(8,128)S(1)} %get-tuple-element.108), channel_id=1, source_target_pairs={{0,16},{1,25},{2,18},{3,27},{4,20},{5,29},{6,22},{7,31},{8,24},{9,... | collective-permute-start | bytes 24584 | tf_op jit(solution)/shard_map/ppermute | solution.py:134
  82.5 4.7 %collective-permute-start.47 = (f32[2,8,256]{2,1,0:T(8,128)S(1)}, f32[2,8,256]{2,1,0:T(8,128)S(1)}, u32[]{:S(2)}, u32[]{:S(2)}) collective-permute-start(f32[2,8,256]{2,1,0:T(8,128)S(1)} %get-tuple-element.112), channel_id=1, source_target_pairs={{0,4},{1,7},{2,6},{3,5},{4,0},{5,3},{6,2},{7,1},{8,12},{9,15},{10,... | collective-permute-start | bytes 49160 | tf_op jit(solution)/shard_map/ppermute | solution.py:134
  84.6 3.9 %collective-permute-start.46 = (f32[2,8,256]{2,1,0:T(8,128)S(1)}, f32[2,8,256]{2,1,0:T(8,128)S(1)}, u32[]{:S(2)}, u32[]{:S(2)}) collective-permute-start(f32[2,8,256]{2,1,0:T(8,128)S(1)} %get-tuple-element.111), channel_id=1, source_target_pairs={{0,2},{1,3},{2,0},{3,1},{4,6},{5,7},{6,4},{7,5},{8,10},{9,11},{10,... | collective-permute-start | bytes 49160 | tf_op jit(solution)/shard_map/ppermute | solution.py:134
  (27 other events, 88.8 us)
